TPU v7x, 32 devices: a whole 2x2x4 slice. The times are simulated.
32 devices in a mesh: tm: 8 (over z, y), rows: 4 (over x, core).
Axes of the slice: x: 2, y: 2, z: 4, core: 2. Of those that a mesh axis runs over, the one named last changes fastest.
Arguments:
- state: float32 [16, 128, 512], P('tm', 'rows'), may hold values from -6 to 6
- source: float32 [16, 128, 512], P('tm', 'rows'), may hold values from -6 to 6
- start: float32 [128, 512], P('rows'), may hold values from -6 to 6
- velocity: float32 [2, 128, 512], P(None, 'rows'), may hold values from -6 to 6
Outputs:
- updated: float32 [16, 128, 512], P('tm', 'rows')
All inputs are finite; a program needn't handle non-finite values.
Results may differ from a plain program's by a relative error of at most 0.0003.
Values sent between devices are 32-bit elements; how exact they have to be, the bound alone decides.
No kernel may reach another device: no remote copies, remote signals or barrier semaphores. Data moves between devices by JAX's collectives and lax.ppermute only.
A program may use at most 64 MiB of HBM per device.

v0:
```python
import math

import jax
import jax.numpy as jnp
from jax import lax
from jax.sharding import PartitionSpec as P

diffusion = 0.25
wrap_weight = 0.05


def from_behind(array, axis, by):
    count = lax.axis_size(axis)
    pairs = [(i, i + by) for i in range(count) if 0 <= i + by < count]
    return lax.ppermute(array, axis, pairs)


def extended(cells, sides, width):
    for axis, dim in sides:
        count = lax.axis_size(axis)
        ends = count - 1
        head = lax.slice_in_dim(cells, 0, width, axis=dim)
        tail = lax.slice_in_dim(cells, cells.shape[dim] - width, cells.shape[dim], axis=dim)
        cells = jnp.concatenate(
            [
                lax.ppermute(tail, axis, [(i, (i + 1) % count) for i in range(ends)]),
                cells,
                lax.ppermute(head, axis, [((i + 1) % count, i) for i in range(ends)]),
            ],
            axis=dim,
        )
    return cells


def swapped(value, axis, bit):
    mask = 2**bit
    pairs = [(source, source ^ mask) for source in range(lax.axis_size(axis))]
    return lax.ppermute(value, axis, pairs)


def stencil_parts(rimmed):
    padded = jnp.pad(rimmed, [(0, 0)] * (rimmed.ndim - 1) + [(1, 1)])
    row_above = padded[..., :-2, 1:-1]
    row_below = padded[..., 2:, 1:-1]
    col_left = padded[..., 1:-1, :-2]
    col_right = padded[..., 1:-1, 2:]
    beside_all = row_above + row_below + col_left + col_right
    return (beside_all, col_right - col_left, row_below - row_above)


def residual_of(state, previous, source, velocity, rimmed, time_scale):
    beside_all, along_x, along_y = stencil_parts(rimmed)
    advect = (velocity[0] + state) * along_x + (velocity[1] + state) * along_y
    return (
        source
        - time_scale * (state - previous)
        - diffusion * (4.0 * state - beside_all)
        - 0.5 * advect
    )


def off_diagonal(rimmed, velocity):
    beside_all, along_x, along_y = stencil_parts(rimmed)
    return -diffusion * beside_all + 0.5 * (velocity[0] * along_x + velocity[1] * along_y)


def diagonal_of(freqs, time_total):
    time_scale = 0.5 * time_total
    angles = 2.0 * math.pi / time_total * freqs.astype(jnp.float32)
    root_rate = math.exp(math.log(wrap_weight) / time_total)
    diag_real = time_scale * (1.0 - root_rate * jnp.cos(angles)) + 4.0 * diffusion
    diag_imag = time_scale * root_rate * jnp.sin(angles)
    return (diag_real.reshape(-1, 1, 1), diag_imag.reshape(-1, 1, 1))


def divide(num_real, num_imag, den_real, den_imag):
    modulus = den_real * den_real + den_imag * den_imag
    return (
        (num_real * den_real + num_imag * den_imag) / modulus,
        (num_imag * den_real - num_real * den_imag) / modulus,
    )


def forward_tables(length):
    index = lax.iota(jnp.int32, length)
    product = index[:, None] * index[None, :] % length
    angles = 2.0 * math.pi / length * product.astype(jnp.float32)
    return (jnp.cos(angles), jnp.sin(angles))


def apply_table(table, values):
    return jnp.dot(
        table, values, precision=lax.Precision.HIGHEST, preferred_element_type=jnp.float32
    )


def twiddle(tm_pos, bit_pos, local_index, steps_dev):
    offset = tm_pos % (1 << bit_pos) * steps_dev + local_index
    angles = 2.0 * math.pi / (steps_dev * 2 ** (bit_pos + 1)) * offset.astype(jnp.float32)
    return (jnp.cos(angles)[:, None], jnp.sin(angles)[:, None])


def on_device(state, source, start, velocity):
    steps_dev, rows_dev, columns = state.shape
    tm_count = lax.axis_size("tm")
    tm_pos = lax.axis_index("tm")
    time_total = steps_dev * tm_count
    time_scale = 0.5 * time_total
    cell_count = rows_dev * columns
    last_step = from_behind(state[-1], "tm", 1)
    first_prev = jnp.where(tm_pos == 0, start, last_step)
    previous = jnp.concatenate([first_prev[None], state[:-1]], axis=0)
    rimmed = extended(state, (("rows", 1),), 1)
    residual = residual_of(state, previous, source, velocity, rimmed, time_scale)
    local_index = lax.iota(jnp.int32, steps_dev)
    global_steps = (tm_pos * steps_dev + local_index).astype(jnp.float32)
    weight = jnp.exp(math.log(wrap_weight) * global_steps / time_total)[:, None, None]
    scaled = weight * residual
    bit_count = tm_count.bit_length() - 1
    small_cos, small_sin = forward_tables(steps_dev)
    flattened = scaled.reshape(steps_dev, cell_count)
    current = jnp.stack([flattened, jnp.zeros_like(flattened)])
    for section in range(bit_count):
        bit_pos = bit_count - 1 - section
        partner = swapped(current, "tm", bit_pos)
        is_upper = jnp.bitwise_and(jnp.right_shift(tm_pos, bit_pos), 1) == 1
        cosine, sine_part = twiddle(tm_pos, bit_pos, local_index, steps_dev)
        difference = partner - current
        twisted = jnp.stack(
            [
                difference[0] * cosine + difference[1] * sine_part,
                difference[1] * cosine - difference[0] * sine_part,
            ]
        )
        current = jnp.where(is_upper, twisted, current + partner)
    spec_real = (apply_table(small_cos, current[0]) + apply_table(small_sin, current[1])).reshape(
        state.shape
    )
    spec_imag = (apply_table(small_cos, current[1]) - apply_table(small_sin, current[0])).reshape(
        state.shape
    )
    reverse = jnp.zeros((), jnp.int32)
    for bit_pos in range(bit_count):
        reverse = reverse + jnp.left_shift(
            jnp.bitwise_and(jnp.right_shift(tm_pos, bit_pos), 1), bit_count - 1 - bit_pos
        )
    freqs = reverse + tm_count * local_index
    diag_real, diag_imag = diagonal_of(freqs, time_total)
    guess_real, guess_imag = divide(spec_real, spec_imag, diag_real, diag_imag)
    stacked = jnp.stack([guess_real, guess_imag])
    rim_guess = extended(stacked, (("rows", 2),), 1)
    coupled = off_diagonal(rim_guess, velocity)
    fix_real, fix_imag = divide(coupled[0], coupled[1], diag_real, diag_imag)
    sweep_real = guess_real - fix_real
    sweep_imag = guess_imag - fix_imag
    flat_real = sweep_real.reshape(steps_dev, cell_count)
    flat_imag = sweep_imag.reshape(steps_dev, cell_count)
    inv_real = (apply_table(small_cos, flat_real) - apply_table(small_sin, flat_imag)) / steps_dev
    inv_imag = (apply_table(small_cos, flat_imag) + apply_table(small_sin, flat_real)) / steps_dev
    current = jnp.stack([inv_real, inv_imag])
    for bit_pos in range(bit_count):
        is_upper = jnp.bitwise_and(jnp.right_shift(tm_pos, bit_pos), 1) == 1
        cosine, sine_part = twiddle(tm_pos, bit_pos, local_index, steps_dev)
        rotated = jnp.stack(
            [
                current[0] * cosine - current[1] * sine_part,
                current[1] * cosine + current[0] * sine_part,
            ]
        )
        current = jnp.where(is_upper, rotated, current)
        partner = swapped(current, "tm", bit_pos)
        current = jnp.where(is_upper, partner - current, partner + current) * 0.5
    back = current[0].reshape(state.shape)
    return state + back / weight


def solution(mesh):
    placed = (P("tm", "rows", None), P("tm", "rows", None), P("rows", None), P(None, "rows", None))
    return jax.shard_map(
        on_device, mesh=mesh, in_specs=placed, out_specs=P("tm", "rows", None), check_vma=False
    )
```

profile of v0, /device:TPU:0, one launch (start us, length us, event | category | flops | bytes accessed | tf_op | source)
XLA Modules:
  0.0 92.2 jit_solution(3742260279655658800)
XLA Ops:
  0.0 0.9 %slice_bitcast_fusion.10 = (f32[32,512]{1,0:T(8,128)S(1)}, f32[1,32,512]{2,1,0:T(8,128)S(1)}) fusion(f32[2,32,512]{2,1,0:T(8,128)} %param.4), kind=kLoop, calls=%fused_computation.72 | loop fusion | bytes 262144 | tf_op jit(solution)/shard_map/squeeze | solution.py:110
  0.9 4.9 %collective-permute-start = (f32[32,512]{1,0:T(8,128)S(1)}, f32[32,512]{1,0:T(8,128)S(1)}, u32[]{:S(2)}, u32[]{:S(2)}) collective-permute-start(f32[32,512]{1,0:T(8,128)S(1)} %get-tuple-element.31), channel_id=1, source_target_pairs={{0,4},{4,8},{8,12},{12,16},{16,20},{20,24},{24,28},{1,5},{5,9},{9,... | collective-permute-start | bytes 196616 | tf_op jit(solution)/shard_map/ppermute | solution.py:15
  5.8 1.5 %collective-permute-start.1 = (f32[2,1,512]{2,1,0:T(1,128)S(1)}, f32[2,1,512]{2,1,0:T(1,128)S(1)}, u32[]{:S(2)}, u32[]{:S(2)}) collective-permute-start(f32[2,1,512]{2,1,0:T(1,128)S(1)} %get-tuple-element.29), channel_id=1, source_target_pairs={{0,1},{1,2},{2,3},{4,5},{5,6},{6,7},{8,9},{9,10},{10,11},{12,13},{... | collective-permute-start | bytes 12296 | tf_op jit(solution)/shard_map/ppermute | solution.py:26
  7.3 1.3 %collective-permute-start.2 = (f32[2,1,512]{2,1,0:T(1,128)S(1)}, f32[2,1,512]{2,1,0:T(1,128)S(1)}, u32[]{:S(2)}, u32[]{:S(2)}) collective-permute-start(f32[2,1,512]{2,1,0:T(1,128)S(1)} %get-tuple-element.30), channel_id=1, source_target_pairs={{1,0},{2,1},{3,2},{5,4},{6,5},{7,6},{9,8},{10,9},{11,10},{13,12},{... | collective-permute-start | bytes 12296 | tf_op jit(solution)/shard_map/ppermute | solution.py:28
  8.7 0.0 copy-start.3
  8.7 0.0 collective-permute-done.1
  8.7 3.2 %collective-permute-done.2 = f32[2,1,512]{2,1,0:T(1,128)S(1)} collective-permute-done((f32[2,1,512]{2,1,0:T(1,128)S(1)}, f32[2,1,512]{2,1,0:T(1,128)S(1)}, u32[]{:S(2)}, u32[]{:S(2)}) %collective-permute-start.2) | collective-permute-done | bytes 4128 | tf_op jit(solution)/shard_map/ppermute | solution.py:28
  11.9 0.1 select_maximum_fusion.3
  12.1 0.0 copy-start.1
  12.1 0.0 collective-permute-done
  12.1 0.0 copy-done.3
  12.1 0.9 copy-done.1
  13.0 0.1 fusion.11
  13.1 0.1 stack_reshape.3
  13.2 0.1 stack.51
  13.3 2.7 %collective-permute-start.3 = (f32[2,2,16384]{2,1,0:T(2,128)S(1)}, f32[2,2,16384]{2,1,0:T(2,128)S(1)}, u32[]{:S(2)}, u32[]{:S(2)}) collective-permute-start(f32[2,2,16384]{2,1,0:T(2,128)S(1)} %stack.51), channel_id=1, source_target_pairs={{0,16},{4,20},{8,24},{12,28},{16,0},{20,4},{24,8},{28,12},{1,17},{... | collective-permute-start | bytes 786440 | tf_op jit(solution)/shard_map/ppermute | solution.py:38
  16.0 11.9 %collective-permute-done.3 = f32[2,2,16384]{2,1,0:T(2,128)S(1)} collective-permute-done((f32[2,2,16384]{2,1,0:T(2,128)S(1)}, f32[2,2,16384]{2,1,0:T(2,128)S(1)}, u32[]{:S(2)}, u32[]{:S(2)}) %collective-permute-start.3) | collective-permute-done | bytes 262176 | tf_op jit(solution)/shard_map/ppermute | solution.py:38
  27.9 0.1 pad_subtract_fusion
  28.0 0.2 multiply_add_fusion.5
  28.2 0.2 maximum_select_fusion
  28.4 1.8 %collective-permute-start.4 = (f32[2,2,16384]{2,1,0:T(2,128)S(1)}, f32[2,2,16384]{2,1,0:T(2,128)S(1)}, u32[]{:S(2)}, u32[]{:S(2)}) collective-permute-start(f32[2,2,16384]{2,1,0:T(2,128)S(1)} %maximum_select_fusion), channel_id=1, source_target_pairs={{0,8},{4,12},{8,0},{12,4},{16,24},{20,28},{24,16},{28,20},{1,9},{5... | collective-permute-start | bytes 786440 | tf_op jit(solution)/shard_map/ppermute | solution.py:38
  30.2 7.4 %collective-permute-done.4 = f32[2,2,16384]{2,1,0:T(2,128)S(1)} collective-permute-done((f32[2,2,16384]{2,1,0:T(2,128)S(1)}, f32[2,2,16384]{2,1,0:T(2,128)S(1)}, u32[]{:S(2)}, u32[]{:S(2)}) %collective-permute-start.4) | collective-permute-done | bytes 262176 | tf_op jit(solution)/shard_map/ppermute | solution.py:38
  37.6 0.2 fusion.74
  37.8 0.2 multiply_add_fusion.4
  38.0 0.3 maximum_select_fusion.1
  38.4 1.6 %collective-permute-start.5 = (f32[2,2,16384]{2,1,0:T(2,128)S(1)}, f32[2,2,16384]{2,1,0:T(2,128)S(1)}, u32[]{:S(2)}, u32[]{:S(2)}) collective-permute-start(f32[2,2,16384]{2,1,0:T(2,128)S(1)} %maximum_select_fusion.1), channel_id=1, source_target_pairs={{0,4},{4,0},{8,12},{12,8},{16,20},{20,16},{24,28},{28,24},{1,5},{5... | collective-permute-start | bytes 786440 | tf_op jit(solution)/shard_map/ppermute | solution.py:38
  40.1 0.1 multiply_add_fusion.6
  40.1 6.7 %collective-permute-done.5 = f32[2,2,16384]{2,1,0:T(2,128)S(1)} collective-permute-done((f32[2,2,16384]{2,1,0:T(2,128)S(1)}, f32[2,2,16384]{2,1,0:T(2,128)S(1)}, u32[]{:S(2)}, u32[]{:S(2)}) %collective-permute-start.5) | collective-permute-done | bytes 262176 | tf_op jit(solution)/shard_map/ppermute | solution.py:38
  46.8 0.1 sub.120
  46.9 0.2 multiply_add_fusion.3
  47.1 0.2 maximum_select_fusion.2
  47.3 0.6 fusion.13
  47.9 0.6 fusion.12
  48.6 0.6 convolution_add_fusion.1
  49.2 0.6 convolution_subtract_fusion.1
  49.8 0.1 fusion.4
  50.0 1.3 %collective-permute-start.6 = (f32[2,2,1,512]{3,2,1,0:T(1,128)S(1)}, f32[2,2,1,512]{3,2,1,0:T(1,128)S(1)}, u32[]{:S(2)}, u32[]{:S(2)}) collective-permute-start(f32[2,2,1,512]{3,2,1,0:T(1,128)S(1)} %get-tuple-element.23), channel_id=1, source_target_pairs={{0,1},{1,2},{2,3},{4,5},{5,6},{6,7},{8,9},{9,10},{10,11},{12,13},{... | collective-permute-start | bytes 24584 | tf_op jit(solution)/shard_map/ppermute | solution.py:26
  51.3 1.3 %collective-permute-start.7 = (f32[2,2,1,512]{3,2,1,0:T(1,128)S(1)}, f32[2,2,1,512]{3,2,1,0:T(1,128)S(1)}, u32[]{:S(2)}, u32[]{:S(2)}) collective-permute-start(f32[2,2,1,512]{3,2,1,0:T(1,128)S(1)} %get-tuple-element.24), channel_id=1, source_target_pairs={{1,0},{2,1},{3,2},{5,4},{6,5},{7,6},{9,8},{10,9},{11,10},{13,12},{... | collective-permute-start | bytes 24584 | tf_op jit(solution)/shard_map/ppermute | solution.py:28
  52.6 0.0 collective-permute-done.6
  52.6 1.7 %collective-permute-done.7 = f32[2,2,1,512]{3,2,1,0:T(1,128)S(1)} collective-permute-done((f32[2,2,1,512]{3,2,1,0:T(1,128)S(1)}, f32[2,2,1,512]{3,2,1,0:T(1,128)S(1)}, u32[]{:S(2)}, u32[]{:S(2)}) %collective-permute-start.7) | collective-permute-done | bytes 8224 | tf_op jit(solution)/shard_map/ppermute | solution.py:28
  54.3 0.2 select_maximum_fusion
  54.5 0.2 multiply_add_fusion
  54.8 0.1 copy.7
  54.9 0.1 copy.8
  55.0 0.4 divide_subtract_fusion
  55.4 0.6 fusion.21
  56.0 0.6 fusion.23
  56.6 0.6 convolution_add_fusion
  57.3 0.8 subtract_bitcast_fusion
  58.0 0.2 maximum_select_fusion.3
  58.2 1.6 %collective-permute-start.8 = (f32[2,2,16384]{2,1,0:T(2,128)S(1)}, f32[2,2,16384]{2,1,0:T(2,128)S(1)}, u32[]{:S(2)}, u32[]{:S(2)}) collective-permute-start(f32[2,2,16384]{2,1,0:T(2,128)S(1)} %maximum_select_fusion.3), channel_id=1, source_target_pairs={{0,4},{4,0},{8,12},{12,8},{16,20},{20,16},{24,28},{28,24},{1,5},{5... | collective-permute-start | bytes 786440 | tf_op jit(solution)/shard_map/ppermute | solution.py:38
  59.8 6.8 %collective-permute-done.8 = f32[2,2,16384]{2,1,0:T(2,128)S(1)} collective-permute-done((f32[2,2,16384]{2,1,0:T(2,128)S(1)}, f32[2,2,16384]{2,1,0:T(2,128)S(1)}, u32[]{:S(2)}, u32[]{:S(2)}) %collective-permute-start.8) | collective-permute-done | bytes 262176 | tf_op jit(solution)/shard_map/ppermute | solution.py:38
  66.7 0.3 select_multiply_fusion.1
  66.9 0.2 multiply_subtract_fusion.1
  67.1 0.2 maximum_select_fusion.4
  67.3 0.7 collective-permute-start.9
  68.0 8.3 %collective-permute-done.9 = f32[2,2,16384]{2,1,0:T(2,128)S(1)} collective-permute-done((f32[2,2,16384]{2,1,0:T(2,128)S(1)}, f32[2,2,16384]{2,1,0:T(2,128)S(1)}, u32[]{:S(2)}, u32[]{:S(2)}) %collective-permute-start.9) | collective-permute-done | bytes 262176 | tf_op jit(solution)/shard_map/ppermute | solution.py:38
  76.2 0.2 select_multiply_fusion
  76.5 0.2 multiply_subtract_fusion
  76.6 0.2 maximum_select_fusion.5
  76.8 2.0 %collective-permute-start.10 = (f32[2,2,16384]{2,1,0:T(2,128)S(1)}, f32[2,2,16384]{2,1,0:T(2,128)S(1)}, u32[]{:S(2)}, u32[]{:S(2)}) collective-permute-start(f32[2,2,16384]{2,1,0:T(2,128)S(1)} %maximum_select_fusion.5), channel_id=1, source_target_pairs={{0,16},{4,20},{8,24},{12,28},{16,0},{20,4},{24,8},{28,12},{1,17},{... | collective-permute-start | bytes 786440 | tf_op jit(solution)/shard_map/ppermute | solution.py:38
  78.8 12.6 %collective-permute-done.10 = f32[2,2,16384]{2,1,0:T(2,128)S(1)} collective-permute-done((f32[2,2,16384]{2,1,0:T(2,128)S(1)}, f32[2,2,16384]{2,1,0:T(2,128)S(1)}, u32[]{:S(2)}, u32[]{:S(2)}) %collective-permute-start.10) | collective-permute-done | bytes 262176 | tf_op jit(solution)/shard_map/ppermute | solution.py:38
  91.4 0.1 select_multiply_fusion.2
  91.5 0.7 fusion.2
  (15 shorter events, 0.3 us)
Async XLA Ops:
  0.0 5.8 %copy-start = (f32[2,32,512]{2,1,0:T(8,128)S(1)}, f32[2,32,512]{2,1,0:T(8,128)}, u32[]{:S(2)}) copy-start(f32[2,32,512]{2,1,0:T(8,128)} %param.4) | copy-start | bytes 393220
  0.0 8.6 %copy-start.2 = (f32[2,32,512]{2,1,0:T(8,128)S(1)}, f32[2,32,512]{2,1,0:T(8,128)}, u32[]{:S(2)}) copy-start(f32[2,32,512]{2,1,0:T(8,128)} %param.7) | copy-start | bytes 393220
  0.9 11.2 %collective-permute-start = (f32[32,512]{1,0:T(8,128)S(1)}, f32[32,512]{1,0:T(8,128)S(1)}, u32[]{:S(2)}, u32[]{:S(2)}) collective-permute-start(f32[32,512]{1,0:T(8,128)S(1)} %get-tuple-element.31), channel_id=1, source_target_pairs={{0,4},{4,8},{8,12},{12,16},{16,20},{20,24},{24,28},{1,5},{5,9},{9,... | collective-permute-start | bytes 196616 | tf_op jit(solution)/shard_map/ppermute | solution.py:15
  5.8 2.8 %collective-permute-start.1 = (f32[2,1,512]{2,1,0:T(1,128)S(1)}, f32[2,1,512]{2,1,0:T(1,128)S(1)}, u32[]{:S(2)}, u32[]{:S(2)}) collective-permute-start(f32[2,1,512]{2,1,0:T(1,128)S(1)} %get-tuple-element.29), channel_id=1, source_target_pairs={{0,1},{1,2},{2,3},{4,5},{5,6},{6,7},{8,9},{9,10},{10,11},{12,13},{... | collective-permute-start | bytes 12296 | tf_op jit(solution)/shard_map/ppermute | solution.py:26
  7.3 4.6 %collective-permute-start.2 = (f32[2,1,512]{2,1,0:T(1,128)S(1)}, f32[2,1,512]{2,1,0:T(1,128)S(1)}, u32[]{:S(2)}, u32[]{:S(2)}) collective-permute-start(f32[2,1,512]{2,1,0:T(1,128)S(1)} %get-tuple-element.30), channel_id=1, source_target_pairs={{1,0},{2,1},{3,2},{5,4},{6,5},{7,6},{9,8},{10,9},{11,10},{13,12},{... | collective-permute-start | bytes 12296 | tf_op jit(solution)/shard_map/ppermute | solution.py:28
  8.7 3.4 %copy-start.3 = (f32[32,512]{1,0:T(8,128)S(1)}, f32[32,512]{1,0:T(8,128)}, u32[]{:S(2)}) copy-start(f32[32,512]{1,0:T(8,128)} %param.6) | copy-start | bytes 196612
  12.1 0.9 copy-start.1
  13.3 14.6 %collective-permute-start.3 = (f32[2,2,16384]{2,1,0:T(2,128)S(1)}, f32[2,2,16384]{2,1,0:T(2,128)S(1)}, u32[]{:S(2)}, u32[]{:S(2)}) collective-permute-start(f32[2,2,16384]{2,1,0:T(2,128)S(1)} %stack.51), channel_id=1, source_target_pairs={{0,16},{4,20},{8,24},{12,28},{16,0},{20,4},{24,8},{28,12},{1,17},{... | collective-permute-start | bytes 786440 | tf_op jit(solution)/shard_map/ppermute | solution.py:38
  28.4 9.2 %collective-permute-start.4 = (f32[2,2,16384]{2,1,0:T(2,128)S(1)}, f32[2,2,16384]{2,1,0:T(2,128)S(1)}, u32[]{:S(2)}, u32[]{:S(2)}) collective-permute-start(f32[2,2,16384]{2,1,0:T(2,128)S(1)} %maximum_select_fusion), channel_id=1, source_target_pairs={{0,8},{4,12},{8,0},{12,4},{16,24},{20,28},{24,16},{28,20},{1,9},{5... | collective-permute-start | bytes 786440 | tf_op jit(solution)/shard_map/ppermute | solution.py:38
  38.4 8.4 %collective-permute-start.5 = (f32[2,2,16384]{2,1,0:T(2,128)S(1)}, f32[2,2,16384]{2,1,0:T(2,128)S(1)}, u32[]{:S(2)}, u32[]{:S(2)}) collective-permute-start(f32[2,2,16384]{2,1,0:T(2,128)S(1)} %maximum_select_fusion.1), channel_id=1, source_target_pairs={{0,4},{4,0},{8,12},{12,8},{16,20},{20,16},{24,28},{28,24},{1,5},{5... | collective-permute-start | bytes 786440 | tf_op jit(solution)/shard_map/ppermute | solution.py:38
  50.0 2.6 %collective-permute-start.6 = (f32[2,2,1,512]{3,2,1,0:T(1,128)S(1)}, f32[2,2,1,512]{3,2,1,0:T(1,128)S(1)}, u32[]{:S(2)}, u32[]{:S(2)}) collective-permute-start(f32[2,2,1,512]{3,2,1,0:T(1,128)S(1)} %get-tuple-element.23), channel_id=1, source_target_pairs={{0,1},{1,2},{2,3},{4,5},{5,6},{6,7},{8,9},{9,10},{10,11},{12,13},{... | collective-permute-start | bytes 24584 | tf_op jit(solution)/shard_map/ppermute | solution.py:26
  51.3 3.1 %collective-permute-start.7 = (f32[2,2,1,512]{3,2,1,0:T(1,128)S(1)}, f32[2,2,1,512]{3,2,1,0:T(1,128)S(1)}, u32[]{:S(2)}, u32[]{:S(2)}) collective-permute-start(f32[2,2,1,512]{3,2,1,0:T(1,128)S(1)} %get-tuple-element.24), channel_id=1, source_target_pairs={{1,0},{2,1},{3,2},{5,4},{6,5},{7,6},{9,8},{10,9},{11,10},{13,12},{... | collective-permute-start | bytes 24584 | tf_op jit(solution)/shard_map/ppermute | solution.py:28
  58.2 8.4 %collective-permute-start.8 = (f32[2,2,16384]{2,1,0:T(2,128)S(1)}, f32[2,2,16384]{2,1,0:T(2,128)S(1)}, u32[]{:S(2)}, u32[]{:S(2)}) collective-permute-start(f32[2,2,16384]{2,1,0:T(2,128)S(1)} %maximum_select_fusion.3), channel_id=1, source_target_pairs={{0,4},{4,0},{8,12},{12,8},{16,20},{20,16},{24,28},{28,24},{1,5},{5... | collective-permute-start | bytes 786440 | tf_op jit(solution)/shard_map/ppermute | solution.py:38
  67.3 8.9 %collective-permute-start.9 = (f32[2,2,16384]{2,1,0:T(2,128)S(1)}, f32[2,2,16384]{2,1,0:T(2,128)S(1)}, u32[]{:S(2)}, u32[]{:S(2)}) collective-permute-start(f32[2,2,16384]{2,1,0:T(2,128)S(1)} %maximum_select_fusion.4), channel_id=1, source_target_pairs={{0,8},{4,12},{8,0},{12,4},{16,24},{20,28},{24,16},{28,20},{1,9},{5... | collective-permute-start | bytes 786440 | tf_op jit(solution)/shard_map/ppermute | solution.py:38
  76.8 14.6 %collective-permute-start.10 = (f32[2,2,16384]{2,1,0:T(2,128)S(1)}, f32[2,2,16384]{2,1,0:T(2,128)S(1)}, u32[]{:S(2)}, u32[]{:S(2)}) collective-permute-start(f32[2,2,16384]{2,1,0:T(2,128)S(1)} %maximum_select_fusion.5), channel_id=1, source_target_pairs={{0,16},{4,20},{8,24},{12,28},{16,0},{20,4},{24,8},{28,12},{1,17},{... | collective-permute-start | bytes 786440 | tf_op jit(solution)/shard_map/ppermute | solution.py:38
where the time goes:
time: 92.5 us; the launch traced here: 92.2 us
  waiting for transfers between devices  58.5 us (63%)
  starting transfers between devices  20.5 us (22%)
  other arithmetic  5.47 us (6%)
  matrix products  5.09 us (6%)
  local copies, waits for them, and re-layouts  2.22 us (2%)
    ppermute x6, waiting for transfers between devices, swapped(): return lax.ppermute(value, axis, pairs)  53.6 us
    ppermute x6, starting transfers between devices, swapped(): return lax.ppermute(value, axis, pairs)  10.3 us
    dot_general x8, matrix products, apply_table(): jnp.dot(table, values, precision=lax.Precision.HIGHEST, preferred_element...  5.09 us
    ppermute x2, waiting for transfers between devices, extended(): lax.ppermute(head, axis, [((i + 1) % count, i) for i in range(ends)])  4.95 us
    ppermute x1, starting transfers between devices, from_behind(): return lax.ppermute(array, axis, pairs)  4.87 us
    ppermute x2, starting transfers between devices, extended(): lax.ppermute(tail, axis, [(i, (i + 1) % count) for i in range(ends)])  2.75 us
    ppermute x2, starting transfers between devices, extended(): lax.ppermute(head, axis, [((i + 1) % count, i) for i in range(ends)])  2.58 us
  transfers between devices with their start and end apart: 11, of which 8 were waited for; matrix products, arithmetic and copies ran while one was open for 0% of the time, Pallas kernels for 0%

commit v1 on v0

v1 whole, which is shorter than its diff:
```python
import math

import jax
import jax.numpy as jnp
from jax import lax
from jax.sharding import PartitionSpec as P

diffusion = 0.25
wrap_weight = 0.05


def swapped(value, axis, bit):
    mask = 2**bit
    pairs = [(source, source ^ mask) for source in range(lax.axis_size(axis))]
    return lax.ppermute(value, axis, pairs)


def edge_packs(state, source, start, velocity):
    columns = state.shape[-1]

    def pack(two, one):
        parts = [
            state[:, two].reshape(-1, columns),
            source[:, one],
            velocity[:, one],
            start[one][None],
        ]
        return jnp.concatenate(parts, axis=0)

    return pack(slice(0, 2), 0), pack(slice(-2, None), -1)


def neighbour_rows(top, bottom):
    count = lax.axis_size("rows")
    odd = lax.axis_index("rows") % 2 == 1
    first = [(i, i ^ 1) for i in range(count) if i ^ 1 < count]
    second = [(i, j) for i in range(count) for j in [i - 1 if i % 2 == 0 else i + 1] if 0 <= j < count]
    inside = lax.ppermute(jnp.where(odd, top, bottom), "rows", first)
    across = lax.ppermute(jnp.where(odd, bottom, top), "rows", second)
    return jnp.where(odd, inside, across), jnp.where(odd, across, inside)


def unpack(packed, steps, columns):
    state = packed[: 2 * steps].reshape(steps, 2, columns)
    source = packed[2 * steps : 3 * steps].reshape(steps, 1, columns)
    velocity = packed[3 * steps : 3 * steps + 2].reshape(2, 1, columns)
    return state, source, velocity, packed[3 * steps + 2 :]


def stencil_parts(rimmed):
    padded = jnp.pad(rimmed, [(0, 0)] * (rimmed.ndim - 1) + [(1, 1)])
    row_above = padded[..., :-2, 1:-1]
    row_below = padded[..., 2:, 1:-1]
    col_left = padded[..., 1:-1, :-2]
    col_right = padded[..., 1:-1, 2:]
    beside_all = row_above + row_below + col_left + col_right
    return beside_all, col_right - col_left, row_below - row_above


def on_device(state, source, start, velocity):
    steps, rows, columns = state.shape
    tm_count = lax.axis_size("tm")
    tm_pos = lax.axis_index("tm")
    rows_pos = lax.axis_index("rows")
    time_total = steps * tm_count
    time_scale = 0.5 * time_total
    gain = 1.0 / (time_scale + 4.0 * diffusion)
    rate = time_scale * gain

    before, after = neighbour_rows(*edge_packs(state, source, start, velocity))
    state_b, source_b, velocity_b, start_b = unpack(before, steps, columns)
    state_a, source_a, velocity_a, start_a = unpack(after, steps, columns)
    state_2 = jnp.concatenate([state_b, state, state_a], axis=1)
    state_1 = state_2[:, 1:-1]
    source_1 = jnp.concatenate([source_b, source, source_a], axis=1)
    velocity_1 = jnp.concatenate([velocity_b, velocity, velocity_a], axis=1)
    start_1 = jnp.concatenate([start_b, start, start_a], axis=0)

    beside_all, along_x, along_y = stencil_parts(state_2)
    advect = (velocity_1[0] + state_1) * along_x + (velocity_1[1] + state_1) * along_y
    forced = source_1 + diffusion * beside_all - 0.5 * advect

    own_y, own_z = [], []
    y = z = 0.0
    for j in range(steps):
        y = rate * y + gain * forced[j]
        z = rate * z + gain * (y - state_1[j])
        own_y.append(y)
        own_z.append(z)

    ends = ((tm_pos + 1) * steps).astype(jnp.float32)
    back_rate = jnp.exp(-math.log(rate) * ends)
    is_last = tm_pos == tm_count - 1
    wrap = wrap_weight * rate**time_total
    jump = jnp.where(is_last, (start_1 - wrap_weight * state_1[-1]) / wrap, 0.0)
    carry_y = back_rate * y + jump
    carry_z = back_rate * (z - (ends * gain) * y) - (time_total * gain) * jump

    total = jnp.concatenate([carry_y, carry_z], axis=0)
    ahead = jnp.zeros_like(total)
    for bit in range(tm_count.bit_length() - 1):
        partner = swapped(total, "tm", bit)
        is_upper = jnp.bitwise_and(jnp.right_shift(tm_pos, bit), 1) == 1
        ahead = ahead + jnp.where(is_upper, partner, 0.0)
        total = total + partner

    height = rows + 2
    total_y, total_z = total[:height], total[height:]
    ahead_y, ahead_z = ahead[:height], ahead[height:]
    turn = wrap / (1.0 - wrap)
    shear = time_total * gain * wrap / (1.0 - wrap) ** 2
    begins = (tm_pos * steps).astype(jnp.float32)
    front_rate = jnp.exp(math.log(rate) * begins)
    enter_y = front_rate * (ahead_y + turn * total_y)
    enter_z = front_rate * (ahead_z + turn * total_z + shear * total_y) + (begins * gain) * enter_y

    row = lax.broadcasted_iota(jnp.int32, (height, columns), 0) + rows_pos * rows
    inside = (row >= 1) & (row <= rows * lax.axis_size("rows"))
    out = []
    for j in range(steps):
        decay = rate ** (j + 1)
        y = own_y[j] + decay * enter_y
        z = own_z[j] + decay * (enter_z + ((j + 1) * gain) * enter_y)
        z = jnp.where(inside, z, 0.0)
        beside_all, along_x, along_y = stencil_parts(z)
        coupled = -diffusion * beside_all + 0.5 * (velocity[0] * along_x + velocity[1] * along_y)
        out.append(y[1:-1] - coupled)
    return jnp.stack(out)


def solution(mesh):
    placed = (P("tm", "rows", None), P("tm", "rows", None), P("rows", None), P(None, "rows", None))
    return jax.shard_map(
        on_device, mesh=mesh, in_specs=placed, out_specs=P("tm", "rows", None), check_vma=False
    )
```

time: 92.5 us -> 30.2 us (0.33)
  the two profiles are of different devices: /device:TPU:0 before, /device:TPU:2 now
where the time goes in v1:
time: 30.2 us; the launch traced here: 29.9 us
  waiting for transfers between devices  17.7 us (59%)
  starting transfers between devices  6.97 us (23%)
  local copies, waits for them, and re-layouts  3.39 us (11%)
  other arithmetic  1.53 us (5%)
  between operations  0.38 us (1%)
    ppermute x3, waiting for transfers between devices, swapped(): return lax.ppermute(value, axis, pairs)  14.5 us
    ppermute x3, starting transfers between devices, swapped(): return lax.ppermute(value, axis, pairs)  4.98 us
    ppermute x1, waiting for transfers between devices, neighbour_rows(): across = lax.ppermute(jnp.where(odd, bottom, top), 'rows', second)  3.2 us
    ppermute x1, starting transfers between devices, neighbour_rows(): across = lax.ppermute(jnp.where(odd, bottom, top), 'rows', second)  1.92 us
    unnamed x9, local copies, waits for them, and re-layouts  0.85 us
    another operation x2, other arithmetic, on_device(): return jnp.stack(out)  0.83 us
    slice x1, local copies, waits for them, and re-layouts, pack(): source[:, one]  0.82 us
    slice x1, local copies, waits for them, and re-layouts, pack(): velocity[:, one]  0.78 us
  transfers between devices with their start and end apart: 5, of which 4 were waited for; matrix products, arithmetic and copies ran while one was open for 0% of the time, Pallas kernels for 0%

profile of v1, /device:TPU:2, one launch (start us, length us, event | category | flops | bytes accessed | tf_op | source)
XLA Modules:
  0.0 29.9 jit_solution(2663446774460886633)
XLA Ops:
  0.0 0.0 copy-start.2
  0.0 0.0 copy-start
  0.0 0.8 %fusion.26 = (f32[2,1,512]{2,1,0:T(1,128)S(1)}, f32[2,1,512]{2,1,0:T(1,128)S(1)}) fusion(f32[2,32,512]{2,1,0:T(8,128)} %param.5), kind=kLoop, calls=%fused_computation.72 | loop fusion | bytes 16384 | tf_op jit(solution)/shard_map/slice | solution.py:24
  0.8 0.8 %fusion.27 = (f32[2,1,512]{2,1,0:T(1,128)S(1)}, f32[2,1,512]{2,1,0:T(1,128)S(1)}) fusion(f32[2,32,512]{2,1,0:T(8,128)} %param.7), kind=kLoop, calls=%fused_computation.73 | loop fusion | bytes 16384 | tf_op jit(solution)/shard_map/slice | solution.py:25
  1.6 0.8 %fusion.25 = (f32[2,2,512]{2,1,0:T(2,128)S(1)}, f32[2,2,512]{2,1,0:T(2,128)S(1)}) fusion(f32[2,32,512]{2,1,0:T(8,128)} %param.4), kind=kLoop, calls=%fused_computation.71 | loop fusion | bytes 32768 | tf_op jit(solution)/shard_map/slice | solution.py:23
  2.4 0.0 copy-done.2
  2.5 0.1 collective-permute-start
  2.6 1.9 %collective-permute-start.1 = (f32[9,512]{1,0:T(8,128)S(1)}, f32[9,512]{1,0:T(8,128)S(1)}, u32[]{:S(2)}, u32[]{:S(2)}) collective-permute-start(f32[9,512]{1,0:T(8,128)S(1)} %get-tuple-element.26), channel_id=1, source_target_pairs={{1,2},{2,1},{5,6},{6,5},{9,10},{10,9},{13,14},{14,13},{17,18},{18,... | collective-permute-start | bytes 55304 | tf_op jit(solution)/shard_map/ppermute | solution.py:39
  4.5 0.0 copy-done
  4.5 0.0 copy-start.1
  4.6 0.0 collective-permute-done
  4.6 3.2 %collective-permute-done.1 = f32[9,512]{1,0:T(8,128)S(1)} collective-permute-done((f32[9,512]{1,0:T(8,128)S(1)}, f32[9,512]{1,0:T(8,128)S(1)}, u32[]{:S(2)}, u32[]{:S(2)}) %collective-permute-start.1) | collective-permute-done | bytes 18464 | tf_op jit(solution)/shard_map/ppermute | solution.py:39
  7.9 0.0 copy-done.1
  8.0 0.0 copy-start.3
  8.1 0.8 %copy-done.3 = f32[2,32,512]{2,1,0:T(8,128)S(1)} copy-done((f32[2,32,512]{2,1,0:T(8,128)S(1)}, f32[2,32,512]{2,1,0:T(8,128)}, u32[]{:S(2)}) %copy-start.3) | copy-done | bytes 131096
  8.9 0.2 fusion
  9.1 0.1 multiply_add_fusion.1
  9.2 0.1 multiply_subtract_fusion
  9.3 1.6 %collective-permute-start.2 = (f32[68,512]{1,0:T(8,128)S(1)}, f32[68,512]{1,0:T(8,128)S(1)}, u32[]{:S(2)}, u32[]{:S(2)}) collective-permute-start(f32[68,512]{1,0:T(8,128)S(1)} %pad_maximum_fusion.3), channel_id=1, source_target_pairs={{0,4},{4,0},{8,12},{12,8},{16,20},{20,16},{24,28},{28,24},{1,5},{5... | collective-permute-start | bytes 417800 | tf_op jit(solution)/shard_map/ppermute | solution.py:15
  10.9 3.6 %collective-permute-done.2 = f32[68,512]{1,0:T(8,128)S(1)} collective-permute-done((f32[68,512]{1,0:T(8,128)S(1)}, f32[68,512]{1,0:T(8,128)S(1)}, u32[]{:S(2)}, u32[]{:S(2)}) %collective-permute-start.2) | collective-permute-done | bytes 139296 | tf_op jit(solution)/shard_map/ppermute | solution.py:15
  14.5 1.6 %collective-permute-start.3 = (f32[68,512]{1,0:T(8,128)S(1)}, f32[68,512]{1,0:T(8,128)S(1)}, u32[]{:S(2)}, u32[]{:S(2)}) collective-permute-start(f32[68,512]{1,0:T(8,128)S(1)} %fusion.29), channel_id=1, source_target_pairs={{0,8},{4,12},{8,0},{12,4},{16,24},{20,28},{24,16},{28,20},{1,9},{5... | collective-permute-start | bytes 417800 | tf_op jit(solution)/shard_map/ppermute | solution.py:15
  16.2 4.9 %collective-permute-done.3 = f32[68,512]{1,0:T(8,128)S(1)} collective-permute-done((f32[68,512]{1,0:T(8,128)S(1)}, f32[68,512]{1,0:T(8,128)S(1)}, u32[]{:S(2)}, u32[]{:S(2)}) %collective-permute-start.3) | collective-permute-done | bytes 139296 | tf_op jit(solution)/shard_map/ppermute | solution.py:15
  21.2 1.7 %collective-permute-start.4 = (f32[68,512]{1,0:T(8,128)S(1)}, f32[68,512]{1,0:T(8,128)S(1)}, u32[]{:S(2)}, u32[]{:S(2)}) collective-permute-start(f32[68,512]{1,0:T(8,128)S(1)} %add.161), channel_id=1, source_target_pairs={{0,16},{4,20},{8,24},{12,28},{16,0},{20,4},{24,8},{28,12},{1,17},{... | collective-permute-start | bytes 417800 | tf_op jit(solution)/shard_map/ppermute | solution.py:15
  22.9 5.9 %collective-permute-done.4 = f32[68,512]{1,0:T(8,128)S(1)} collective-permute-done((f32[68,512]{1,0:T(8,128)S(1)}, f32[68,512]{1,0:T(8,128)S(1)}, u32[]{:S(2)}, u32[]{:S(2)}) %collective-permute-start.4) | collective-permute-done | bytes 139296 | tf_op jit(solution)/shard_map/ppermute | solution.py:15
  28.9 0.1 select_add_fusion
  28.9 0.1 add_select_fusion.1
  29.0 0.1 add_select_fusion
  29.1 0.2 fusion.14
  29.3 0.7 %pad_maximum_fusion.4 = f32[2,32,512]{2,1,0:T(8,128)} fusion(f32[1,32,512]{2,1,0:T(8,128)S(1)} %get-tuple-element.10, f32[1,32,512]{2,1,0:T(8,128)S(1)} %get-tuple-element.9), kind=kLoop, calls=%fused_computation.9 | loop fusion | flops 32768 | bytes 262144 | tf_op jit(solution)/shard_map/stack | solution.py:128
  (29 shorter events, 0.3 us)
Async XLA Ops:
  0.0 2.4 %copy-start.2 = (f32[32,512]{1,0:T(8,128)S(1)}, f32[32,512]{1,0:T(8,128)}, u32[]{:S(2)}) copy-start(f32[32,512]{1,0:T(8,128)} %param.6) | copy-start | bytes 196612
  0.0 4.5 %copy-start = (f32[2,32,512]{2,1,0:T(8,128)S(1)}, f32[2,32,512]{2,1,0:T(8,128)}, u32[]{:S(2)}) copy-start(f32[2,32,512]{2,1,0:T(8,128)} %param.4) | copy-start | bytes 393220
  2.5 2.1 %collective-permute-start = (f32[9,512]{1,0:T(8,128)S(1)}, f32[9,512]{1,0:T(8,128)S(1)}, u32[]{:S(2)}, u32[]{:S(2)}) collective-permute-start(f32[9,512]{1,0:T(8,128)S(1)} %get-tuple-element.25), channel_id=1, source_target_pairs={{0,1},{1,0},{2,3},{3,2},{4,5},{5,4},{6,7},{7,6},{8,9},{9,8},{10,11... | collective-permute-start | bytes 55304 | tf_op jit(solution)/shard_map/ppermute | solution.py:38
  2.6 5.2 %collective-permute-start.1 = (f32[9,512]{1,0:T(8,128)S(1)}, f32[9,512]{1,0:T(8,128)S(1)}, u32[]{:S(2)}, u32[]{:S(2)}) collective-permute-start(f32[9,512]{1,0:T(8,128)S(1)} %get-tuple-element.26), channel_id=1, source_target_pairs={{1,2},{2,1},{5,6},{6,5},{9,10},{10,9},{13,14},{14,13},{17,18},{18,... | collective-permute-start | bytes 55304 | tf_op jit(solution)/shard_map/ppermute | solution.py:39
  4.5 3.4 %copy-start.1 = (f32[2,32,512]{2,1,0:T(8,128)S(1)}, f32[2,32,512]{2,1,0:T(8,128)}, u32[]{:S(2)}) copy-start(f32[2,32,512]{2,1,0:T(8,128)} %param.7) | copy-start | bytes 393220
  8.0 0.9 %copy-start.3 = (f32[2,32,512]{2,1,0:T(8,128)S(1)}, f32[2,32,512]{2,1,0:T(8,128)}, u32[]{:S(2)}) copy-start(f32[2,32,512]{2,1,0:T(8,128)} %param.5) | copy-start | bytes 393220
  9.3 5.2 %collective-permute-start.2 = (f32[68,512]{1,0:T(8,128)S(1)}, f32[68,512]{1,0:T(8,128)S(1)}, u32[]{:S(2)}, u32[]{:S(2)}) collective-permute-start(f32[68,512]{1,0:T(8,128)S(1)} %pad_maximum_fusion.3), channel_id=1, source_target_pairs={{0,4},{4,0},{8,12},{12,8},{16,20},{20,16},{24,28},{28,24},{1,5},{5... | collective-permute-start | bytes 417800 | tf_op jit(solution)/shard_map/ppermute | solution.py:15
  14.5 6.6 %collective-permute-start.3 = (f32[68,512]{1,0:T(8,128)S(1)}, f32[68,512]{1,0:T(8,128)S(1)}, u32[]{:S(2)}, u32[]{:S(2)}) collective-permute-start(f32[68,512]{1,0:T(8,128)S(1)} %fusion.29), channel_id=1, source_target_pairs={{0,8},{4,12},{8,0},{12,4},{16,24},{20,28},{24,16},{28,20},{1,9},{5... | collective-permute-start | bytes 417800 | tf_op jit(solution)/shard_map/ppermute | solution.py:15
  21.2 7.7 %collective-permute-start.4 = (f32[68,512]{1,0:T(8,128)S(1)}, f32[68,512]{1,0:T(8,128)S(1)}, u32[]{:S(2)}, u32[]{:S(2)}) collective-permute-start(f32[68,512]{1,0:T(8,128)S(1)} %add.161), channel_id=1, source_target_pairs={{0,16},{4,20},{8,24},{12,28},{16,0},{20,4},{24,8},{28,12},{1,17},{... | collective-permute-start | bytes 417800 | tf_op jit(solution)/shard_map/ppermute | solution.py:15

commit v2 on v1

v2 whole, which is shorter than its diff:
```python
import functools
import math

import jax
import jax.numpy as jnp
from jax import lax
from jax.experimental import pallas as pl
from jax.experimental.pallas import tpu as pltpu
from jax.sharding import PartitionSpec as P

diffusion = 0.25
wrap_weight = 0.05
tile = 8
vmem_limit = 32 * 1024 * 1024


def dims_of(state, tm_count):
    steps = state.shape[0]
    time_total = steps * tm_count
    time_scale = 0.5 * time_total
    gain = 1.0 / (time_scale + 4.0 * diffusion)
    return steps, time_total, gain, time_scale * gain


def power_of(base, exponent, limit):
    result = jnp.float32(1.0)
    for bit in range(limit.bit_length()):
        is_set = jnp.bitwise_and(jnp.right_shift(exponent, bit), 1) == 1
        result = result * jnp.where(is_set, jnp.float32(base ** (2**bit)), jnp.float32(1.0))
    return result


def slots_of(steps):
    pairs = [("state", j) for j in range(steps)]
    singles = [("source", j) for j in range(steps)] + [("velocity", 0), ("velocity", 1), ("start", 0)]
    place, at = {}, 0
    for name in pairs:
        place[name] = at
        at += 2
    for name in singles:
        place[name] = at
        at += 1
    return place, -(-at // tile)


def load_kernel(state, source, start, velocity, state_v, source_v, start_v, velocity_v, inside, across, sems):
    copies = [
        pltpu.make_async_copy(a, b, sems.at[i])
        for i, (a, b) in enumerate(
            [(state, state_v), (source, source_v), (start, start_v), (velocity, velocity_v)]
        )
    ]
    for copy in copies:
        copy.start()
    for copy in copies:
        copy.wait()
    steps, rows, columns = state.shape
    place, tiles = slots_of(steps)
    odd = lax.axis_index("rows") % 2 == 1
    sub = lax.broadcasted_iota(jnp.int32, (tile, columns), 0)

    def item(name, edge):
        kind, j = name
        if kind == "start":
            return start_v[edge, :]
        return {"state": state_v, "source": source_v, "velocity": velocity_v}[kind][j, edge, :]

    for t in range(tiles):
        top = jnp.zeros((tile, columns), jnp.float32)
        bottom = jnp.zeros((tile, columns), jnp.float32)
        for name, at in place.items():
            if at // tile != t:
                continue
            slot, width = at % tile, 2 if name[0] == "state" else 1
            first = item(name, pl.ds(0, tile))
            last = item(name, pl.ds(rows - tile, tile))
            if slot:
                first = pltpu.roll(first, slot, 0)
                last = pltpu.roll(last, tile - slot, 0)
            top = jnp.where((sub >= slot) & (sub < slot + width), first, top)
            bottom = jnp.where((sub <= tile - 1 - slot) & (sub > tile - 1 - slot - width), last, bottom)
        here = pl.ds(t * tile, tile)
        inside[here, :] = jnp.where(odd, top, bottom)
        across[here, :] = jnp.where(odd, bottom, top)


def sides(value, row):
    columns = value.shape[1]
    col = lax.broadcasted_iota(jnp.int32, value.shape, 1)
    left = jnp.where(col == 0, 0.0, pltpu.roll(value, 1, 1))
    right = jnp.where(col == columns - 1, 0.0, pltpu.roll(value, columns - 1, 1))
    return left, right


def carry_kernel(tm_count, state, source, start, velocity, inside, across, total, own_y, own_z, own_edge):
    steps, time_total, gain, rate = dims_of(state, tm_count)
    rows, columns = state.shape[1:]
    place, _ = slots_of(steps)
    rows_pos = lax.axis_index("rows")
    tm_pos = lax.axis_index("tm")
    odd = rows_pos % 2 == 1
    not_first = jnp.where(rows_pos > 0, jnp.float32(1.0), jnp.float32(0.0))
    not_last = jnp.where(rows_pos < lax.axis_size("rows") - 1, jnp.float32(1.0), jnp.float32(0.0))

    def packed(t):
        here = pl.ds(t * tile, tile)
        first, second = inside[here, :], across[here, :]
        return jnp.where(odd, first, second) * not_first, jnp.where(odd, second, first) * not_last

    packs = {t: packed(t) for t in sorted({at // tile for at in place.values()})}

    def extended(name, main):
        t, slot = place[name] // tile, place[name] % tile
        before, after = packs[t]
        if slot:
            before = pltpu.roll(before, slot, 0)
            after = pltpu.roll(after, tile - slot, 0)
        return jnp.concatenate([before, main, after], axis=0)

    tall = rows + 2 * tile
    vel = [extended(("velocity", i), velocity[i]) for i in range(2)]
    begun = extended(("start", 0), start[...])
    y = z = None
    sub = lax.broadcasted_iota(jnp.int32, (tile, columns), 0)
    for j in range(steps):
        here = extended(("state", j), state[j])
        above, below = pltpu.roll(here, 1, 0), pltpu.roll(here, tall - 1, 0)
        left, right = sides(here, None)
        beside_all = above + below + left + right
        advect = (vel[0] + here) * (right - left) + (vel[1] + here) * (below - above)
        forced = extended(("source", j), source[j]) + diffusion * beside_all - 0.5 * advect
        y = gain * forced if y is None else rate * y + gain * forced
        z = gain * (y - here) if z is None else rate * z + gain * (y - here)
        own_y[j] = y[tile : tile + rows]
        own_z[j] = z[tile : tile + rows]
        own_edge[j] = jnp.where(sub == tile - 1, z[:tile], z[tile + rows :])

    ends = (tm_pos + 1) * steps
    back_rate = power_of(1.0 / rate, ends, time_total)
    back_shear = ends.astype(jnp.float32) * gain
    wrap = wrap_weight * rate**time_total
    is_last = jnp.where(tm_pos == tm_count - 1, jnp.float32(1.0 / wrap), jnp.float32(0.0))
    jump = is_last * (begun - wrap_weight * here)
    carry_z = back_rate * (z - back_shear * y) - (time_total * gain) * jump
    carry_y = back_rate * y + jump
    total[0:rows, :] = carry_y[tile : tile + rows]
    total[rows : 2 * rows, :] = carry_z[tile : tile + rows]
    ends_y = jnp.where(sub == 0, carry_y[tile + rows :], carry_y[:tile])
    ends_z = jnp.where(
        sub == 1,
        pltpu.roll(carry_z[tile + rows :], 1, 0),
        pltpu.roll(carry_z[:tile], tile - 1, 0),
    )
    total[2 * rows :, :] = jnp.where((sub == 0) | (sub == tile - 1), ends_y, ends_z)


def final_kernel(tm_count, velocity, own_y, own_z, own_edge, total, *rest):
    partners, out, done, sems = rest[:-3], rest[-3], rest[-2], rest[-1]
    steps, time_total, gain, rate = dims_of(own_y, tm_count)
    rows, columns = own_y.shape[1:]
    rows_pos = lax.axis_index("rows")
    tm_pos = lax.axis_index("tm")
    wrap = wrap_weight * rate**time_total
    turn = wrap / (1.0 - wrap)
    shear = time_total * gain * wrap / (1.0 - wrap) ** 2

    def sums(here):
        whole = total[here, :]
        ahead = jnp.zeros_like(whole)
        for bit, partner in enumerate(partners):
            value = partner[here, :]
            whole = whole + value
            is_upper = jnp.bitwise_and(jnp.right_shift(tm_pos, bit), 1) == 1
            ahead = ahead + jnp.where(is_upper, jnp.float32(1.0), jnp.float32(0.0)) * value
        return whole, ahead

    begins = tm_pos * steps
    front_rate = power_of(rate, begins, time_total)
    front_shear = begins.astype(jnp.float32) * gain

    def entering(whole_y, whole_z, ahead_y, ahead_z):
        enter_y = front_rate * (ahead_y + turn * whole_y)
        enter_z = front_rate * (ahead_z + turn * whole_z + shear * whole_y) + front_shear * enter_y
        return enter_y, enter_z

    whole_y, ahead_y = sums(pl.ds(0, rows))
    whole_z, ahead_z = sums(pl.ds(rows, rows))
    enter_y, enter_z = entering(whole_y, whole_z, ahead_y, ahead_z)
    whole_e, ahead_e = sums(pl.ds(2 * rows, tile))
    sub = lax.broadcasted_iota(jnp.int32, (tile, columns), 0)

    def as_z(value):
        return jnp.where(sub == 0, pltpu.roll(value, tile - 1, 0), pltpu.roll(value, 1, 0))

    edge_y, edge_z = entering(whole_e, as_z(whole_e), ahead_e, as_z(ahead_e))
    not_first = jnp.where(rows_pos > 0, jnp.float32(1.0), jnp.float32(0.0))
    not_last = jnp.where(rows_pos < lax.axis_size("rows") - 1, jnp.float32(1.0), jnp.float32(0.0))
    kept = jnp.where(sub == 0, not_last, not_first)
    row = lax.broadcasted_iota(jnp.int32, (rows, columns), 0)
    copies = []
    for j in range(steps):
        decay = rate ** (j + 1)
        y = own_y[j] + decay * enter_y
        z = own_z[j] + decay * (enter_z + ((j + 1) * gain) * enter_y)
        edge = kept * (own_edge[j] + decay * (edge_z + ((j + 1) * gain) * edge_y))
        above = jnp.where(row == 0, edge[tile - 1 :], pltpu.roll(z, 1, 0))
        below = jnp.where(row == rows - 1, edge[:1], pltpu.roll(z, rows - 1, 0))
        left, right = sides(z, None)
        coupled = -diffusion * (above + below + left + right) + 0.5 * (
            velocity[0] * (right - left) + velocity[1] * (below - above)
        )
        done[j] = y - coupled
        copies.append(pltpu.make_async_copy(done.at[j], out.at[j], sems.at[j]))
        copies[-1].start()
    for copy in copies:
        copy.wait()


def swapped(value, axis, partner):
    return lax.ppermute(value, axis, [(i, partner(i)) for i in range(lax.axis_size(axis))])


def on_device(state, source, start, velocity):
    steps, rows, columns = state.shape
    tm_count = lax.axis_size("tm")
    rows_count = lax.axis_size("rows")
    f32 = jnp.float32
    in_vmem = pl.BlockSpec(memory_space=pltpu.VMEM)
    in_hbm = pl.BlockSpec(memory_space=pl.ANY)
    params = pltpu.CompilerParams(vmem_limit_bytes=vmem_limit)
    pack = pltpu.VMEM((slots_of(steps)[1] * tile, columns), f32)
    state, source, start, velocity, inside, across = pl.pallas_call(
        load_kernel,
        out_shape=[pltpu.VMEM(a.shape, f32) for a in (state, source, start, velocity)] + [pack, pack],
        in_specs=[in_hbm] * 4,
        out_specs=[in_vmem] * 6,
        scratch_shapes=[pltpu.SemaphoreType.DMA((4,))],
        compiler_params=params,
        name="load_and_pack",
    )(*[pltpu.with_memory_space_constraint(a, pltpu.HBM) for a in (state, source, start, velocity)])

    across = swapped(across, "rows", lambda i: (i + (1 if i % 2 else -1)) % rows_count)
    inside = swapped(inside, "rows", lambda i: i ^ 1)

    total, own_y, own_z, own_edge = pl.pallas_call(
        functools.partial(carry_kernel, tm_count),
        out_shape=[
            pltpu.VMEM((2 * rows + tile, columns), f32),
            pltpu.VMEM((steps, rows, columns), f32),
            pltpu.VMEM((steps, rows, columns), f32),
            pltpu.VMEM((steps, tile, columns), f32),
        ],
        in_specs=[in_vmem] * 6,
        out_specs=[in_vmem] * 4,
        compiler_params=params,
        name="own_carry",
    )(state, source, start, velocity, inside, across)

    partners, so_far = [], total
    for bit in range(tm_count.bit_length() - 1):
        mask = 3 << (bit - 1) if bit > 1 else 1 << bit
        partners.append(swapped(so_far, "tm", lambda i: i ^ mask))
        so_far = so_far + partners[-1]

    return pl.pallas_call(
        functools.partial(final_kernel, tm_count),
        out_shape=jax.ShapeDtypeStruct((steps, rows, columns), f32),
        in_specs=[in_vmem] * (5 + len(partners)),
        out_specs=in_hbm,
        scratch_shapes=[pltpu.VMEM((steps, rows, columns), f32), pltpu.SemaphoreType.DMA((steps,))],
        compiler_params=params,
        name="enter_and_couple",
    )(velocity, own_y, own_z, own_edge, total, *partners)


def solution(mesh):
    placed = (P("tm", "rows", None), P("tm", "rows", None), P("rows", None), P(None, "rows", None))
    return jax.shard_map(
        on_device, mesh=mesh, in_specs=placed, out_specs=P("tm", "rows", None), check_vma=False
    )
```

time: 30.2 us -> 26 us (0.86)
  the two profiles are of different devices: /device:TPU:2 before, /device:TPU:0 now
where the time goes in v2:
time: 26 us; the launch traced here: 25.9 us
  waiting for transfers between devices  13 us (50%)
  starting transfers between devices  10.5 us (40%)
  Pallas kernels  2.26 us (9%)
    ppermute x5, waiting for transfers between devices, swapped(): lax.ppermute(value, axis, [(i, partner(i)) for i in range(lax.axis_size(a...  13 us
    ppermute x5, starting transfers between devices, swapped(): lax.ppermute(value, axis, [(i, partner(i)) for i in range(lax.axis_size(a...  10.5 us
    pallas_call x1, Pallas kernels, on_device(): pl.pallas_call(load_kernel, out_shape=[pltpu.VMEM(a.shape, f32) for a in...  1.12 us
    pallas_call x1, Pallas kernels, on_device(): pl.pallas_call(functools.partial(final_kernel, tm_count), out_shape=jax.S...  0.86 us
  transfers between devices with their start and end apart: 5, of which 4 were waited for; matrix products, arithmetic and copies ran while one was open for 0% of the time, Pallas kernels for 0%

profile of v2, /device:TPU:0, one launch (start us, length us, event | category | flops | bytes accessed | tf_op | source)
XLA Modules:
  0.0 25.9 jit_solution(101424577658669165)
XLA Ops:
  0.0 1.1 %load_and_pack.1 = (f32[2,32,512]{2,1,0:T(8,128)S(1)}, f32[2,32,512]{2,1,0:T(8,128)S(1)}, f32[32,512]{1,0:T(8,128)S(1)}, f32[2,32,512]{2,1,0:T(8,128)S(1)}, f32[...) custom-call(f32[2,32,512]{2,1,0:T(8,128)} %state.1, f32[2,32,512]{2,1,0:T(8,128)} %source.1, f32[32,512]{1,0:T(8,128)} %start.1, ...), custom_call_target="tpu_custom_call" | custom-call | tf_op jit(solution)/shard_map/load_and_pack/pallas_call | solution.py:232
  1.1 0.5 %collective-permute-start = (f32[16,512]{1,0:T(8,128)S(1)}, f32[16,512]{1,0:T(8,128)S(1)}, u32[]{:S(2)}, u32[]{:S(2)}) collective-permute-start(f32[16,512]{1,0:T(8,128)S(1)} %get-tuple-element.19), channel_id=1, source_target_pairs={{0,1},{1,0},{2,3},{3,2},{4,5},{5,4},{6,7},{7,6},{8,9},{9,8},{10,11... | collective-permute-start | bytes 98312 | tf_op jit(solution)/shard_map/ppermute | solution.py:220
  1.6 2.6 %collective-permute-start.1 = (f32[16,512]{1,0:T(8,128)S(1)}, f32[16,512]{1,0:T(8,128)S(1)}, u32[]{:S(2)}, u32[]{:S(2)}) collective-permute-start(f32[16,512]{1,0:T(8,128)S(1)} %get-tuple-element.20), channel_id=1, source_target_pairs={{0,3},{1,2},{2,1},{3,0},{4,7},{5,6},{6,5},{7,4},{8,11},{9,10},{10,... | collective-permute-start | bytes 98312 | tf_op jit(solution)/shard_map/ppermute | solution.py:220
  4.3 0.0 collective-permute-done.inside
  4.3 1.7 %collective-permute-done.1.across = f32[16,512]{1,0:T(8,128)S(1)} collective-permute-done((f32[16,512]{1,0:T(8,128)S(1)}, f32[16,512]{1,0:T(8,128)S(1)}, u32[]{:S(2)}, u32[]{:S(2)}) %collective-permute-start.1) | collective-permute-done | bytes 32800 | tf_op jit(solution)/shard_map/ppermute | solution.py:220
  5.9 0.3 %own_carry.1 = (f32[72,512]{1,0:T(8,128)S(1)}, f32[2,32,512]{2,1,0:T(8,128)S(1)}, f32[2,32,512]{2,1,0:T(8,128)S(1)}, f32[2,8,512]{2,1,0:T(8,128)S(1)}) custom-call(f32[2,32,512]{2,1,0:T(8,128)S(1)} %get-tuple-element.16.state, f32[2,32,512]{2,1,0:T(8,128)S(1)} %get-tuple-element.17.source, f32[32,512]{1,0:T(8,128)S(1)} %get-tuple-element.18.start, ...), custom_call_target="tpu_custom_call" | custom-call | tf_op jit(solution)/shard_map/own_carry/pallas_call | solution.py:245
  6.2 1.7 %collective-permute-start.2 = (f32[72,512]{1,0:T(8,128)S(1)}, f32[72,512]{1,0:T(8,128)S(1)}, u32[]{:S(2)}, u32[]{:S(2)}) collective-permute-start(f32[72,512]{1,0:T(8,128)S(1)} %get-tuple-element.24.total), channel_id=1, source_target_pairs={{0,4},{4,0},{8,12},{12,8},{16,20},{20,16},{24,28},{28,24},{1,5},{5... | collective-permute-start | bytes 442376 | tf_op jit(solution)/shard_map/ppermute | solution.py:220
  7.9 4.5 %collective-permute-done.2.rest_0_ = f32[72,512]{1,0:T(8,128)S(1)} collective-permute-done((f32[72,512]{1,0:T(8,128)S(1)}, f32[72,512]{1,0:T(8,128)S(1)}, u32[]{:S(2)}, u32[]{:S(2)}) %collective-permute-start.2) | collective-permute-done | bytes 147488 | tf_op jit(solution)/shard_map/ppermute | solution.py:220
  12.4 1.9 %collective-permute-start.3 = (f32[72,512]{1,0:T(8,128)S(1)}, f32[72,512]{1,0:T(8,128)S(1)}, u32[]{:S(2)}, u32[]{:S(2)}) collective-permute-start(f32[72,512]{1,0:T(8,128)S(1)} %add.6), channel_id=1, source_target_pairs={{0,8},{4,12},{8,0},{12,4},{16,24},{20,28},{24,16},{28,20},{1,9},{5... | collective-permute-start | bytes 442376 | tf_op jit(solution)/shard_map/ppermute | solution.py:220
  14.3 3.7 %collective-permute-done.3.rest_1_ = f32[72,512]{1,0:T(8,128)S(1)} collective-permute-done((f32[72,512]{1,0:T(8,128)S(1)}, f32[72,512]{1,0:T(8,128)S(1)}, u32[]{:S(2)}, u32[]{:S(2)}) %collective-permute-start.3) | collective-permute-done | bytes 147488 | tf_op jit(solution)/shard_map/ppermute | solution.py:220
  18.0 3.8 %collective-permute-start.4 = (f32[72,512]{1,0:T(8,128)S(1)}, f32[72,512]{1,0:T(8,128)S(1)}, u32[]{:S(2)}, u32[]{:S(2)}) collective-permute-start(f32[72,512]{1,0:T(8,128)S(1)} %add.7), channel_id=1, source_target_pairs={{0,24},{4,28},{8,16},{12,20},{16,8},{20,12},{24,0},{28,4},{1,25},{... | collective-permute-start | bytes 442376 | tf_op jit(solution)/shard_map/ppermute | solution.py:220
  21.8 3.2 %collective-permute-done.4.rest_2_ = f32[72,512]{1,0:T(8,128)S(1)} collective-permute-done((f32[72,512]{1,0:T(8,128)S(1)}, f32[72,512]{1,0:T(8,128)S(1)}, u32[]{:S(2)}, u32[]{:S(2)}) %collective-permute-start.4) | collective-permute-done | bytes 147488 | tf_op jit(solution)/shard_map/ppermute | solution.py:220
  25.0 0.9 %enter_and_couple.1 = f32[2,32,512]{2,1,0:T(8,128)} custom-call(f32[2,32,512]{2,1,0:T(8,128)S(1)} %get-tuple-element.15.velocity, f32[2,32,512]{2,1,0:T(8,128)S(1)} %get-tuple-element.21.own_y, f32[2,32,512]{2,1,0:T(8,128)S(1)} %get-tuple-element.22.own_z, f32[2,8,512]{2,1,0:T(8,128)S(1)} %get-tuple-element.23.own_edge, ...), custom_call_target="tpu_custom_call" | custom-call | tf_op jit(solution)/shard_map/enter_and_couple/pallas_call | solution.py:265
  (2 shorter events, 0.0 us)
Async XLA Ops:
  1.1 3.1 %collective-permute-start = (f32[16,512]{1,0:T(8,128)S(1)}, f32[16,512]{1,0:T(8,128)S(1)}, u32[]{:S(2)}, u32[]{:S(2)}) collective-permute-start(f32[16,512]{1,0:T(8,128)S(1)} %get-tuple-element.19), channel_id=1, source_target_pairs={{0,1},{1,0},{2,3},{3,2},{4,5},{5,4},{6,7},{7,6},{8,9},{9,8},{10,11... | collective-permute-start | bytes 98312 | tf_op jit(solution)/shard_map/ppermute | solution.py:220
  1.6 4.3 %collective-permute-start.1 = (f32[16,512]{1,0:T(8,128)S(1)}, f32[16,512]{1,0:T(8,128)S(1)}, u32[]{:S(2)}, u32[]{:S(2)}) collective-permute-start(f32[16,512]{1,0:T(8,128)S(1)} %get-tuple-element.20), channel_id=1, source_target_pairs={{0,3},{1,2},{2,1},{3,0},{4,7},{5,6},{6,5},{7,4},{8,11},{9,10},{10,... | collective-permute-start | bytes 98312 | tf_op jit(solution)/shard_map/ppermute | solution.py:220
  6.2 6.2 %collective-permute-start.2 = (f32[72,512]{1,0:T(8,128)S(1)}, f32[72,512]{1,0:T(8,128)S(1)}, u32[]{:S(2)}, u32[]{:S(2)}) collective-permute-start(f32[72,512]{1,0:T(8,128)S(1)} %get-tuple-element.24.total), channel_id=1, source_target_pairs={{0,4},{4,0},{8,12},{12,8},{16,20},{20,16},{24,28},{28,24},{1,5},{5... | collective-permute-start | bytes 442376 | tf_op jit(solution)/shard_map/ppermute | solution.py:220
  12.4 5.5 %collective-permute-start.3 = (f32[72,512]{1,0:T(8,128)S(1)}, f32[72,512]{1,0:T(8,128)S(1)}, u32[]{:S(2)}, u32[]{:S(2)}) collective-permute-start(f32[72,512]{1,0:T(8,128)S(1)} %add.6), channel_id=1, source_target_pairs={{0,8},{4,12},{8,0},{12,4},{16,24},{20,28},{24,16},{28,20},{1,9},{5... | collective-permute-start | bytes 442376 | tf_op jit(solution)/shard_map/ppermute | solution.py:220
  18.0 7.1 %collective-permute-start.4 = (f32[72,512]{1,0:T(8,128)S(1)}, f32[72,512]{1,0:T(8,128)S(1)}, u32[]{:S(2)}, u32[]{:S(2)}) collective-permute-start(f32[72,512]{1,0:T(8,128)S(1)} %add.7), channel_id=1, source_target_pairs={{0,24},{4,28},{8,16},{12,20},{16,8},{20,12},{24,0},{28,4},{1,25},{... | collective-permute-start | bytes 442376 | tf_op jit(solution)/shard_map/ppermute | solution.py:220

commit v3 on v2

--- a/solution.py
+++ b/solution.py
@@ -84,7 +84,7 @@
         across[here, :] = jnp.where(odd, bottom, top)
 
 
-def sides(value, row):
+def sides(value):
     columns = value.shape[1]
     col = lax.broadcasted_iota(jnp.int32, value.shape, 1)
     left = jnp.where(col == 0, 0.0, pltpu.roll(value, 1, 1))
@@ -92,15 +92,71 @@
     return left, right
 
 
-def carry_kernel(tm_count, state, source, start, velocity, inside, across, total, own_y, own_z, own_edge):
+def pack_edges(sub, halo_y, halo_z, more_y, more_z):
+    parts = [
+        halo_y,
+        jnp.where(sub < 4, pltpu.roll(halo_z, 1, 0), pltpu.roll(halo_z, 7, 0)),
+        jnp.where(sub < 4, pltpu.roll(more_y, 2, 0), pltpu.roll(more_y, 6, 0)),
+        jnp.where(sub < 4, pltpu.roll(more_z, 3, 0), pltpu.roll(more_z, 5, 0)),
+    ]
+    result = parts[3]
+    for i in (2, 1, 0):
+        result = jnp.where((sub == i) | (sub == tile - 1 - i), parts[i], result)
+    return result
+
+
+def unpack_edges(sub, packed):
+    return packed, *[
+        jnp.where(sub < 4, pltpu.roll(packed, tile - i, 0), pltpu.roll(packed, i, 0)) for i in (1, 2, 3)
+    ]
+
+
+def carried(tm_count, steps, time_total, gain, rate, y, z, jumped):
+    tm_pos = lax.axis_index("tm")
+    ends = (tm_pos + 1) * steps
+    back_rate = power_of(1.0 / rate, ends, time_total)
+    back_shear = ends.astype(jnp.float32) * gain
+    carry_y, carry_z = back_rate * y, back_rate * (z - back_shear * y)
+    if jumped is not None:
+        wrap = wrap_weight * rate**time_total
+        is_last = jnp.where(tm_pos == tm_count - 1, jnp.float32(1.0 / wrap), jnp.float32(0.0))
+        jump = is_last * jumped
+        carry_y, carry_z = carry_y + jump, carry_z - (time_total * gain) * jump
+    return carry_y, carry_z
+
+
+def carry_kernel(tm_count, state, source, start, velocity, total, own_y, own_z):
+    steps, time_total, gain, rate = dims_of(state, tm_count)
+    rows, columns = state.shape[1:]
+    row = lax.broadcasted_iota(jnp.int32, (rows, columns), 0)
+    y = z = None
+    for j in range(steps):
+        here = state[j]
+        above = jnp.where(row == 0, 0.0, pltpu.roll(here, 1, 0))
+        below = jnp.where(row == rows - 1, 0.0, pltpu.roll(here, rows - 1, 0))
+        left, right = sides(here)
+        beside_all = above + below + left + right
+        advect = (velocity[0] + here) * (right - left) + (velocity[1] + here) * (below - above)
+        forced = source[j] + diffusion * beside_all - 0.5 * advect
+        y = gain * forced if y is None else rate * y + gain * forced
+        z = gain * (y - here) if z is None else rate * z + gain * (y - here)
+        own_y[j] = y
+        own_z[j] = z
+    jumped = start[...] - wrap_weight * here
+    carry_y, carry_z = carried(tm_count, steps, time_total, gain, rate, y, z, jumped)
+    total[0:rows, :] = carry_y
+    total[rows : 2 * rows, :] = carry_z
+
+
+def edge_kernel(tm_count, state, velocity, inside, across, total, own_edge):
     steps, time_total, gain, rate = dims_of(state, tm_count)
     rows, columns = state.shape[1:]
     place, _ = slots_of(steps)
     rows_pos = lax.axis_index("rows")
-    tm_pos = lax.axis_index("tm")
     odd = rows_pos % 2 == 1
     not_first = jnp.where(rows_pos > 0, jnp.float32(1.0), jnp.float32(0.0))
     not_last = jnp.where(rows_pos < lax.axis_size("rows") - 1, jnp.float32(1.0), jnp.float32(0.0))
+    sub = lax.broadcasted_iota(jnp.int32, (tile, columns), 0)
 
     def packed(t):
         here = pl.ds(t * tile, tile)
@@ -109,52 +165,39 @@
 
     packs = {t: packed(t) for t in sorted({at // tile for at in place.values()})}
 
-    def extended(name, main):
+    def halo(*name):
         t, slot = place[name] // tile, place[name] % tile
         before, after = packs[t]
         if slot:
-            before = pltpu.roll(before, slot, 0)
-            after = pltpu.roll(after, tile - slot, 0)
-        return jnp.concatenate([before, main, after], axis=0)
-
-    tall = rows + 2 * tile
-    vel = [extended(("velocity", i), velocity[i]) for i in range(2)]
-    begun = extended(("start", 0), start[...])
-    y = z = None
-    sub = lax.broadcasted_iota(jnp.int32, (tile, columns), 0)
+            before, after = pltpu.roll(before, slot, 0), pltpu.roll(after, tile - slot, 0)
+        return jnp.where(sub < 4, after, before)
+
+    top, bottom = pl.ds(0, tile), pl.ds(rows - tile, tile)
+    vel = [halo("velocity", i) for i in range(2)]
+    side = jnp.where(sub < 4, jnp.float32(0.5), jnp.float32(-0.5))
+    across_vel = jnp.where(sub < 4, velocity[1, top, :], velocity[1, bottom, :])
+    y = z = more_y = more_z = jnp.zeros((tile, columns), jnp.float32)
     for j in range(steps):
-        here = extended(("state", j), state[j])
-        above, below = pltpu.roll(here, 1, 0), pltpu.roll(here, tall - 1, 0)
-        left, right = sides(here, None)
-        beside_all = above + below + left + right
+        here, first, last = halo("state", j), state[j, top, :], state[j, bottom, :]
+        next_row, previous_row = pltpu.roll(here, tile - 1, 0), pltpu.roll(here, 1, 0)
+        above = jnp.where(sub < 4, pltpu.roll(last, 1, 0), previous_row)
+        below = jnp.where(sub < 4, next_row, pltpu.roll(first, tile - 1, 0))
+        left, right = sides(here)
         advect = (vel[0] + here) * (right - left) + (vel[1] + here) * (below - above)
-        forced = extended(("source", j), source[j]) + diffusion * beside_all - 0.5 * advect
-        y = gain * forced if y is None else rate * y + gain * forced
-        z = gain * (y - here) if z is None else rate * z + gain * (y - here)
-        own_y[j] = y[tile : tile + rows]
-        own_z[j] = z[tile : tile + rows]
-        own_edge[j] = jnp.where(sub == tile - 1, z[:tile], z[tile + rows :])
-
-    ends = (tm_pos + 1) * steps
-    back_rate = power_of(1.0 / rate, ends, time_total)
-    back_shear = ends.astype(jnp.float32) * gain
-    wrap = wrap_weight * rate**time_total
-    is_last = jnp.where(tm_pos == tm_count - 1, jnp.float32(1.0 / wrap), jnp.float32(0.0))
-    jump = is_last * (begun - wrap_weight * here)
-    carry_z = back_rate * (z - back_shear * y) - (time_total * gain) * jump
-    carry_y = back_rate * y + jump
-    total[0:rows, :] = carry_y[tile : tile + rows]
-    total[rows : 2 * rows, :] = carry_z[tile : tile + rows]
-    ends_y = jnp.where(sub == 0, carry_y[tile + rows :], carry_y[:tile])
-    ends_z = jnp.where(
-        sub == 1,
-        pltpu.roll(carry_z[tile + rows :], 1, 0),
-        pltpu.roll(carry_z[:tile], tile - 1, 0),
-    )
-    total[2 * rows :, :] = jnp.where((sub == 0) | (sub == tile - 1), ends_y, ends_z)
-
-
-def final_kernel(tm_count, velocity, own_y, own_z, own_edge, total, *rest):
+        forced = halo("source", j) + diffusion * (above + below + left + right) - 0.5 * advect
+        y = rate * y + gain * forced
+        z = rate * z + gain * (y - here)
+        outside = jnp.where(sub < 4, previous_row, next_row)
+        mine = jnp.where(sub < 4, first, last)
+        more_y = rate * more_y + gain * (outside * (diffusion + side * (across_vel + mine)))
+        more_z = rate * more_z + gain * more_y
+        own_edge[j] = pack_edges(sub, y, z, more_y, more_z)
+    jumped = halo("start", 0) - wrap_weight * here
+    scales = (tm_count, steps, time_total, gain, rate)
+    total[...] = pack_edges(sub, *carried(*scales, y, z, jumped), *carried(*scales, more_y, more_z, None))
+
+
+def final_kernel(tm_count, velocity, own_y, own_z, own_edge, main, edge, main_partner, edge_partner, *rest):
     partners, out, done, sems = rest[:-3], rest[-3], rest[-2], rest[-1]
     steps, time_total, gain, rate = dims_of(own_y, tm_count)
     rows, columns = own_y.shape[1:]
@@ -163,15 +206,15 @@
     wrap = wrap_weight * rate**time_total
     turn = wrap / (1.0 - wrap)
     shear = time_total * gain * wrap / (1.0 - wrap) ** 2
-
-    def sums(here):
-        whole = total[here, :]
-        ahead = jnp.zeros_like(whole)
-        for bit, partner in enumerate(partners):
-            value = partner[here, :]
+    sub = lax.broadcasted_iota(jnp.int32, (tile, columns), 0)
+
+    def sums(own, first, here):
+        whole, ahead = own, None
+        for bit, value in enumerate([first] + [partner[here, :] for partner in partners]):
             whole = whole + value
             is_upper = jnp.bitwise_and(jnp.right_shift(tm_pos, bit), 1) == 1
-            ahead = ahead + jnp.where(is_upper, jnp.float32(1.0), jnp.float32(0.0)) * value
+            part = jnp.where(is_upper, jnp.float32(1.0), jnp.float32(0.0)) * value
+            ahead = part if ahead is None else ahead + part
         return whole, ahead
 
     begins = tm_pos * steps
@@ -183,29 +226,39 @@
         enter_z = front_rate * (ahead_z + turn * whole_z + shear * whole_y) + front_shear * enter_y
         return enter_y, enter_z
 
-    whole_y, ahead_y = sums(pl.ds(0, rows))
-    whole_z, ahead_z = sums(pl.ds(rows, rows))
+    def main_sums(here):
+        return sums(main[here, :], main_partner[here, :], here)
+
+    whole_y, ahead_y = main_sums(pl.ds(0, rows))
+    whole_z, ahead_z = main_sums(pl.ds(rows, rows))
     enter_y, enter_z = entering(whole_y, whole_z, ahead_y, ahead_z)
-    whole_e, ahead_e = sums(pl.ds(2 * rows, tile))
-    sub = lax.broadcasted_iota(jnp.int32, (tile, columns), 0)
-
-    def as_z(value):
-        return jnp.where(sub == 0, pltpu.roll(value, tile - 1, 0), pltpu.roll(value, 1, 0))
-
-    edge_y, edge_z = entering(whole_e, as_z(whole_e), ahead_e, as_z(ahead_e))
+    whole_e, ahead_e = sums(edge[...], edge_partner[...], pl.ds(2 * rows, tile))
+    whole_e, ahead_e = unpack_edges(sub, whole_e), unpack_edges(sub, ahead_e)
+    halo_y, halo_z = entering(*whole_e[:2], *ahead_e[:2])
+    more_y, more_z = entering(*whole_e[2:], *ahead_e[2:])
     not_first = jnp.where(rows_pos > 0, jnp.float32(1.0), jnp.float32(0.0))
     not_last = jnp.where(rows_pos < lax.axis_size("rows") - 1, jnp.float32(1.0), jnp.float32(0.0))
-    kept = jnp.where(sub == 0, not_last, not_first)
+    kept = jnp.where(sub < 4, not_last, not_first)
     row = lax.broadcasted_iota(jnp.int32, (rows, columns), 0)
+
+    def with_edges(value, more):
+        parts = [value[:tile]] if rows == tile else [value[:tile], value[tile:-tile], value[-tile:]]
+        parts[0] = parts[0] + jnp.where(sub == 0, more, 0.0)
+        parts[-1] = parts[-1] + jnp.where(sub == tile - 1, more, 0.0)
+        return jnp.concatenate([part for part in parts if part.shape[0]], axis=0)
+
     copies = []
     for j in range(steps):
-        decay = rate ** (j + 1)
-        y = own_y[j] + decay * enter_y
-        z = own_z[j] + decay * (enter_z + ((j + 1) * gain) * enter_y)
-        edge = kept * (own_edge[j] + decay * (edge_z + ((j + 1) * gain) * edge_y))
-        above = jnp.where(row == 0, edge[tile - 1 :], pltpu.roll(z, 1, 0))
-        below = jnp.where(row == rows - 1, edge[:1], pltpu.roll(z, rows - 1, 0))
-        left, right = sides(z, None)
+        decay, lag = rate ** (j + 1), (j + 1) * gain
+        _, edge_z, edge_more_y, edge_more_z = unpack_edges(sub, own_edge[j])
+        y = with_edges(own_y[j] + decay * enter_y, edge_more_y + decay * more_y)
+        z = with_edges(
+            own_z[j] + decay * (enter_z + lag * enter_y), edge_more_z + decay * (more_z + lag * more_y)
+        )
+        outside = kept * (edge_z + decay * (halo_z + lag * halo_y))
+        above = jnp.where(row == 0, outside[tile - 1 :], pltpu.roll(z, 1, 0))
+        below = jnp.where(row == rows - 1, outside[:1], pltpu.roll(z, rows - 1, 0))
+        left, right = sides(z)
         coupled = -diffusion * (above + below + left + right) + 0.5 * (
             velocity[0] * (right - left) + velocity[1] * (below - above)
         )
@@ -242,35 +295,48 @@
     across = swapped(across, "rows", lambda i: (i + (1 if i % 2 else -1)) % rows_count)
     inside = swapped(inside, "rows", lambda i: i ^ 1)
 
-    total, own_y, own_z, own_edge = pl.pallas_call(
+    main, own_y, own_z = pl.pallas_call(
         functools.partial(carry_kernel, tm_count),
         out_shape=[
-            pltpu.VMEM((2 * rows + tile, columns), f32),
+            pltpu.VMEM((2 * rows, columns), f32),
             pltpu.VMEM((steps, rows, columns), f32),
             pltpu.VMEM((steps, rows, columns), f32),
-            pltpu.VMEM((steps, tile, columns), f32),
         ],
-        in_specs=[in_vmem] * 6,
-        out_specs=[in_vmem] * 4,
+        in_specs=[in_vmem] * 4,
+        out_specs=[in_vmem] * 3,
         compiler_params=params,
         name="own_carry",
-    )(state, source, start, velocity, inside, across)
-
-    partners, so_far = [], total
-    for bit in range(tm_count.bit_length() - 1):
+    )(state, source, start, velocity)
+    main_partner = swapped(main, "tm", lambda i: i ^ 1)
+
+    edge, own_edge = pl.pallas_call(
+        functools.partial(edge_kernel, tm_count),
+        out_shape=[pltpu.VMEM((tile, columns), f32), pltpu.VMEM((steps, tile, columns), f32)],
+        in_specs=[in_vmem] * 4,
+        out_specs=[in_vmem] * 2,
+        compiler_params=params,
+        cost_estimate=pl.CostEstimate(flops=10**10, bytes_accessed=10**8, transcendentals=0),
+        name="edge_carry",
+    )(state, velocity, inside, across)
+    edge_partner = swapped(edge, "tm", lambda i: i ^ 1)
+
+    partners = []
+    so_far = jnp.concatenate([main + main_partner, edge + edge_partner], axis=0)
+    for bit in range(1, tm_count.bit_length() - 1):
+        if partners:
+            so_far = so_far + partners[-1]
         mask = 3 << (bit - 1) if bit > 1 else 1 << bit
         partners.append(swapped(so_far, "tm", lambda i: i ^ mask))
-        so_far = so_far + partners[-1]
 
     return pl.pallas_call(
         functools.partial(final_kernel, tm_count),
         out_shape=jax.ShapeDtypeStruct((steps, rows, columns), f32),
-        in_specs=[in_vmem] * (5 + len(partners)),
+        in_specs=[in_vmem] * (8 + len(partners)),
         out_specs=in_hbm,
         scratch_shapes=[pltpu.VMEM((steps, rows, columns), f32), pltpu.SemaphoreType.DMA((steps,))],
         compiler_params=params,
         name="enter_and_couple",
-    )(velocity, own_y, own_z, own_edge, total, *partners)
+    )(velocity, own_y, own_z, own_edge, main, edge, main_partner, edge_partner, *partners)
 
 
 def solution(mesh):

time: 26 us -> 23.8 us (0.915)
  waiting for transfers between devices: 13 us -> 9.54 us
  starting transfers between devices: 10.5 us -> 11.7 us
    ppermute x5 -> x6, waiting for transfers between devices: 13 us -> 9.54 us  [swapped(): lax.ppermute(value, axis, [(i, partner(i)) for i in range(lax.axis_size(a...]
    ppermute x5 -> x6, starting transfers between devices: 10.5 us -> 11.7 us  [swapped(): lax.ppermute(value, axis, [(i, partner(i)) for i in range(lax.axis_size(a...]
  transfers between devices with their start and end apart: 5 -> 6, of which waited for: 4 -> 3; matrix products, arithmetic and copies ran while one was open for 0% -> 0% of each run, Pallas kernels for 0% -> 1%
where the time goes in v3:
time: 23.8 us; the launch traced here: 23.6 us
  starting transfers between devices  11.7 us (49%)
  waiting for transfers between devices  9.54 us (40%)
  Pallas kernels  2.31 us (10%)
    ppermute x6, starting transfers between devices, swapped(): lax.ppermute(value, axis, [(i, partner(i)) for i in range(lax.axis_size(a...  11.7 us
    ppermute x6, waiting for transfers between devices, swapped(): lax.ppermute(value, axis, [(i, partner(i)) for i in range(lax.axis_size(a...  9.54 us
    pallas_call x1, Pallas kernels, on_device(): pl.pallas_call(load_kernel, out_shape=[pltpu.VMEM(a.shape, f32) for a in...  1.12 us
    pallas_call x1, Pallas kernels, on_device(): pl.pallas_call(functools.partial(final_kernel, tm_count), out_shape=jax.S...  0.89 us
  transfers between devices with their start and end apart: 6, of which 3 were waited for; matrix products, arithmetic and copies ran while one was open for 0% of the time, Pallas kernels for 1%

profile of v3, /device:TPU:0, one launch (start us, length us, event | category | flops | bytes accessed | tf_op | source)
XLA Modules:
  0.0 23.6 jit_solution(6689342136545838110)
XLA Ops:
  0.0 1.1 %load_and_pack.1 = (f32[2,32,512]{2,1,0:T(8,128)S(1)}, f32[2,32,512]{2,1,0:T(8,128)S(1)}, f32[32,512]{1,0:T(8,128)S(1)}, f32[2,32,512]{2,1,0:T(8,128)S(1)}, f32[...) custom-call(f32[2,32,512]{2,1,0:T(8,128)} %state.1, f32[2,32,512]{2,1,0:T(8,128)} %source.1, f32[32,512]{1,0:T(8,128)} %start.1, ...), custom_call_target="tpu_custom_call" | custom-call | tf_op jit(solution)/shard_map/load_and_pack/pallas_call | solution.py:285
  1.1 0.5 %collective-permute-start = (f32[16,512]{1,0:T(8,128)S(1)}, f32[16,512]{1,0:T(8,128)S(1)}, u32[]{:S(2)}, u32[]{:S(2)}) collective-permute-start(f32[16,512]{1,0:T(8,128)S(1)} %get-tuple-element.22), channel_id=1, source_target_pairs={{0,1},{1,0},{2,3},{3,2},{4,5},{5,4},{6,7},{7,6},{8,9},{9,8},{10,11... | collective-permute-start | bytes 98312 | tf_op jit(solution)/shard_map/ppermute | solution.py:273
  1.6 2.6 %collective-permute-start.1 = (f32[16,512]{1,0:T(8,128)S(1)}, f32[16,512]{1,0:T(8,128)S(1)}, u32[]{:S(2)}, u32[]{:S(2)}) collective-permute-start(f32[16,512]{1,0:T(8,128)S(1)} %get-tuple-element.23), channel_id=1, source_target_pairs={{0,3},{1,2},{2,1},{3,0},{4,7},{5,6},{6,5},{7,4},{8,11},{9,10},{10,... | collective-permute-start | bytes 98312 | tf_op jit(solution)/shard_map/ppermute | solution.py:273
  4.3 0.2 own_carry.1
  4.4 1.6 %collective-permute-start.2 = (f32[64,512]{1,0:T(8,128)S(1)}, f32[64,512]{1,0:T(8,128)S(1)}, u32[]{:S(2)}, u32[]{:S(2)}) collective-permute-start(f32[64,512]{1,0:T(8,128)S(1)} %get-tuple-element.25.main), channel_id=1, source_target_pairs={{0,4},{4,0},{8,12},{12,8},{16,20},{20,16},{24,28},{28,24},{1,5},{5... | collective-permute-start | bytes 393224 | tf_op jit(solution)/shard_map/ppermute | solution.py:273
  6.0 0.0 collective-permute-done.inside
  6.0 0.0 collective-permute-done.1.across
  6.0 0.1 edge_carry.1
  6.2 1.6 %collective-permute-start.3 = (f32[8,512]{1,0:T(8,128)S(1)}, f32[8,512]{1,0:T(8,128)S(1)}, u32[]{:S(2)}, u32[]{:S(2)}) collective-permute-start(f32[8,512]{1,0:T(8,128)S(1)} %get-tuple-element.26.edge), channel_id=1, source_target_pairs={{0,4},{4,0},{8,12},{12,8},{16,20},{20,16},{24,28},{28,24},{1,5},{5... | collective-permute-start | bytes 49160 | tf_op jit(solution)/shard_map/ppermute | solution.py:273
  7.8 2.6 %collective-permute-done.3.edge_partner = f32[8,512]{1,0:T(8,128)S(1)} collective-permute-done((f32[8,512]{1,0:T(8,128)S(1)}, f32[8,512]{1,0:T(8,128)S(1)}, u32[]{:S(2)}, u32[]{:S(2)}) %collective-permute-start.3) | collective-permute-done | bytes 16416 | tf_op jit(solution)/shard_map/ppermute | solution.py:273
  10.3 0.0 collective-permute-done.2.main_partner
  10.4 1.6 %collective-permute-start.4 = (f32[72,512]{1,0:T(8,128)S(1)}, f32[72,512]{1,0:T(8,128)S(1)}, u32[]{:S(2)}, u32[]{:S(2)}) collective-permute-start(f32[72,512]{1,0:T(8,128)S(1)} %pad_maximum_fusion), channel_id=1, source_target_pairs={{0,8},{4,12},{8,0},{12,4},{16,24},{20,28},{24,16},{28,20},{1,9},{5... | collective-permute-start | bytes 442376 | tf_op jit(solution)/shard_map/ppermute | solution.py:273
  12.0 3.6 %collective-permute-done.4.rest_0_ = f32[72,512]{1,0:T(8,128)S(1)} collective-permute-done((f32[72,512]{1,0:T(8,128)S(1)}, f32[72,512]{1,0:T(8,128)S(1)}, u32[]{:S(2)}, u32[]{:S(2)}) %collective-permute-start.4) | collective-permute-done | bytes 147488 | tf_op jit(solution)/shard_map/ppermute | solution.py:273
  15.6 3.7 %collective-permute-start.5 = (f32[72,512]{1,0:T(8,128)S(1)}, f32[72,512]{1,0:T(8,128)S(1)}, u32[]{:S(2)}, u32[]{:S(2)}) collective-permute-start(f32[72,512]{1,0:T(8,128)S(1)} %fusion), channel_id=1, source_target_pairs={{0,24},{4,28},{8,16},{12,20},{16,8},{20,12},{24,0},{28,4},{1,25},{... | collective-permute-start | bytes 442376 | tf_op jit(solution)/shard_map/ppermute | solution.py:273
  19.3 3.4 %collective-permute-done.5.rest_1_ = f32[72,512]{1,0:T(8,128)S(1)} collective-permute-done((f32[72,512]{1,0:T(8,128)S(1)}, f32[72,512]{1,0:T(8,128)S(1)}, u32[]{:S(2)}, u32[]{:S(2)}) %collective-permute-start.5) | collective-permute-done | bytes 147488 | tf_op jit(solution)/shard_map/ppermute | solution.py:273
  22.7 0.9 %enter_and_couple.1 = f32[2,32,512]{2,1,0:T(8,128)} custom-call(f32[2,32,512]{2,1,0:T(8,128)S(1)} %get-tuple-element.16.velocity, f32[2,32,512]{2,1,0:T(8,128)S(1)} %get-tuple-element.20.own_y, f32[2,32,512]{2,1,0:T(8,128)S(1)} %get-tuple-element.21.own_z, f32[2,8,512]{2,1,0:T(8,128)S(1)} %get-tuple-element.24.own_edge, ...), custom_call_target="tpu_custom_call" | custom-call | tf_op jit(solution)/shard_map/enter_and_couple/pallas_call | solution.py:331
  (4 shorter events, 0.1 us)
Async XLA Ops:
  1.1 4.9 %collective-permute-start = (f32[16,512]{1,0:T(8,128)S(1)}, f32[16,512]{1,0:T(8,128)S(1)}, u32[]{:S(2)}, u32[]{:S(2)}) collective-permute-start(f32[16,512]{1,0:T(8,128)S(1)} %get-tuple-element.22), channel_id=1, source_target_pairs={{0,1},{1,0},{2,3},{3,2},{4,5},{5,4},{6,7},{7,6},{8,9},{9,8},{10,11... | collective-permute-start | bytes 98312 | tf_op jit(solution)/shard_map/ppermute | solution.py:273
  1.6 4.4 %collective-permute-start.1 = (f32[16,512]{1,0:T(8,128)S(1)}, f32[16,512]{1,0:T(8,128)S(1)}, u32[]{:S(2)}, u32[]{:S(2)}) collective-permute-start(f32[16,512]{1,0:T(8,128)S(1)} %get-tuple-element.23), channel_id=1, source_target_pairs={{0,3},{1,2},{2,1},{3,0},{4,7},{5,6},{6,5},{7,4},{8,11},{9,10},{10,... | collective-permute-start | bytes 98312 | tf_op jit(solution)/shard_map/ppermute | solution.py:273
  4.4 5.9 %collective-permute-start.2 = (f32[64,512]{1,0:T(8,128)S(1)}, f32[64,512]{1,0:T(8,128)S(1)}, u32[]{:S(2)}, u32[]{:S(2)}) collective-permute-start(f32[64,512]{1,0:T(8,128)S(1)} %get-tuple-element.25.main), channel_id=1, source_target_pairs={{0,4},{4,0},{8,12},{12,8},{16,20},{20,16},{24,28},{28,24},{1,5},{5... | collective-permute-start | bytes 393224 | tf_op jit(solution)/shard_map/ppermute | solution.py:273
  6.2 4.2 %collective-permute-start.3 = (f32[8,512]{1,0:T(8,128)S(1)}, f32[8,512]{1,0:T(8,128)S(1)}, u32[]{:S(2)}, u32[]{:S(2)}) collective-permute-start(f32[8,512]{1,0:T(8,128)S(1)} %get-tuple-element.26.edge), channel_id=1, source_target_pairs={{0,4},{4,0},{8,12},{12,8},{16,20},{20,16},{24,28},{28,24},{1,5},{5... | collective-permute-start | bytes 49160 | tf_op jit(solution)/shard_map/ppermute | solution.py:273
  10.4 5.2 %collective-permute-start.4 = (f32[72,512]{1,0:T(8,128)S(1)}, f32[72,512]{1,0:T(8,128)S(1)}, u32[]{:S(2)}, u32[]{:S(2)}) collective-permute-start(f32[72,512]{1,0:T(8,128)S(1)} %pad_maximum_fusion), channel_id=1, source_target_pairs={{0,8},{4,12},{8,0},{12,4},{16,24},{20,28},{24,16},{28,20},{1,9},{5... | collective-permute-start | bytes 442376 | tf_op jit(solution)/shard_map/ppermute | solution.py:273
  15.6 7.1 %collective-permute-start.5 = (f32[72,512]{1,0:T(8,128)S(1)}, f32[72,512]{1,0:T(8,128)S(1)}, u32[]{:S(2)}, u32[]{:S(2)}) collective-permute-start(f32[72,512]{1,0:T(8,128)S(1)} %fusion), channel_id=1, source_target_pairs={{0,24},{4,28},{8,16},{12,20},{16,8},{20,12},{24,0},{28,4},{1,25},{... | collective-permute-start | bytes 442376 | tf_op jit(solution)/shard_map/ppermute | solution.py:273

commit v4 on v3

--- a/solution.py
+++ b/solution.py
@@ -43,27 +43,27 @@
     return place, -(-at // tile)
 
 
-def load_kernel(state, source, start, velocity, state_v, source_v, start_v, velocity_v, inside, across, sems):
-    copies = [
-        pltpu.make_async_copy(a, b, sems.at[i])
-        for i, (a, b) in enumerate(
-            [(state, state_v), (source, source_v), (start, start_v), (velocity, velocity_v)]
-        )
-    ]
-    for copy in copies:
-        copy.start()
+def pack_kernel(state, source, start, velocity, inside, across, state_v, source_v, start_v, velocity_v, sems):
+    far = state.shape[-2] - tile
+    copies = []
+    for a, b in ((state, state_v), (source, source_v), (velocity, velocity_v), (start, start_v)):
+        for end in range(2):
+            here = pl.ds(end * far, tile)
+            from_ref = a.at[here, :] if a is start else a.at[:, here, :]
+            copies.append(pltpu.make_async_copy(from_ref, b.at[end], sems.at[len(copies)]))
+            copies[-1].start()
     for copy in copies:
         copy.wait()
-    steps, rows, columns = state.shape
+    steps, _, columns = state.shape
     place, tiles = slots_of(steps)
     odd = lax.axis_index("rows") % 2 == 1
     sub = lax.broadcasted_iota(jnp.int32, (tile, columns), 0)
 
-    def item(name, edge):
+    def item(name, end):
         kind, j = name
         if kind == "start":
-            return start_v[edge, :]
-        return {"state": state_v, "source": source_v, "velocity": velocity_v}[kind][j, edge, :]
+            return start_v[end]
+        return {"state": state_v, "source": source_v, "velocity": velocity_v}[kind][end, j]
 
     for t in range(tiles):
         top = jnp.zeros((tile, columns), jnp.float32)
@@ -72,8 +72,7 @@
             if at // tile != t:
                 continue
             slot, width = at % tile, 2 if name[0] == "state" else 1
-            first = item(name, pl.ds(0, tile))
-            last = item(name, pl.ds(rows - tile, tile))
+            first, last = item(name, 0), item(name, 1)
             if slot:
                 first = pltpu.roll(first, slot, 0)
                 last = pltpu.roll(last, tile - slot, 0)
@@ -197,6 +196,53 @@
     total[...] = pack_edges(sub, *carried(*scales, y, z, jumped), *carried(*scales, more_y, more_z, None))
 
 
+def with_edges(value, more):
+    sub = lax.broadcasted_iota(jnp.int32, more.shape, 0)
+    parts = [value] if value.shape[0] == tile else [value[:tile], value[tile:-tile], value[-tile:]]
+    parts[0] = parts[0] + jnp.where(sub == 0, more, 0.0)
+    parts[-1] = parts[-1] + jnp.where(sub == tile - 1, more, 0.0)
+    return jnp.concatenate([part for part in parts if part.shape[0]], axis=0)
+
+
+def join_kernel(main, edge, main_partner, edge_partner, total):
+    rows, half = main.shape[0] // 2, main.shape[1] // 2
+    edges = edge[...] + edge_partner[...]
+    sub = lax.broadcasted_iota(jnp.int32, edges.shape, 0)
+    _, _, *more = unpack_edges(sub, edges)
+    for i in range(2):
+        here = pl.ds(i * rows, rows)
+        value = with_edges(main[here, :] + main_partner[here, :], more[i])
+        for side in range(2):
+            total[pl.ds((2 * i + side) * rows, rows), :] = value[:, side * half : (side + 1) * half]
+    left, right = edges[:, :half], edges[:, half:]
+    sub = lax.broadcasted_iota(jnp.int32, left.shape, 0)
+    outer = jnp.where(sub == 0, left, pltpu.roll(right, 1, 0))
+    last = jnp.where(sub == tile - 1, right, pltpu.roll(left, tile - 1, 0))
+    inner = jnp.where(sub == 2, pltpu.roll(left, 1, 0), pltpu.roll(right, 2, 0))
+    before = jnp.where(sub == 4, pltpu.roll(left, tile - 2, 0), pltpu.roll(right, tile - 1, 0))
+    total[pl.ds(4 * rows, tile), :] = jnp.where(
+        sub < 2, outer, jnp.where(sub < 4, inner, jnp.where(sub < 6, before, last))
+    )
+
+
+def split_halo(packed):
+    def whole(at):
+        value = []
+        for side in range(2):
+            after, before = at + side, tile - 2 - at + side
+            value.append(
+                jnp.where(
+                    sub < 4,
+                    pltpu.roll(packed, (tile - after) % tile, 0),
+                    pltpu.roll(packed, (tile - 1 - before) % tile, 0),
+                )
+            )
+        return jnp.concatenate(value, axis=1)
+
+    sub = lax.broadcasted_iota(jnp.int32, packed.shape, 0)
+    return whole(0), whole(2)
+
+
 def final_kernel(tm_count, velocity, own_y, own_z, own_edge, main, edge, main_partner, edge_partner, *rest):
     partners, out, done, sems = rest[:-3], rest[-3], rest[-2], rest[-1]
     steps, time_total, gain, rate = dims_of(own_y, tm_count)
@@ -208,13 +254,18 @@
     shear = time_total * gain * wrap / (1.0 - wrap) ** 2
     sub = lax.broadcasted_iota(jnp.int32, (tile, columns), 0)
 
-    def sums(own, first, here):
+    uppers = [
+        jnp.where(
+            jnp.bitwise_and(jnp.right_shift(tm_pos, bit), 1) == 1, jnp.float32(1.0), jnp.float32(0.0)
+        )
+        for bit in range(1 + len(partners))
+    ]
+
+    def sums(own, *others):
         whole, ahead = own, None
-        for bit, value in enumerate([first] + [partner[here, :] for partner in partners]):
+        for upper, value in zip(uppers, others):
             whole = whole + value
-            is_upper = jnp.bitwise_and(jnp.right_shift(tm_pos, bit), 1) == 1
-            part = jnp.where(is_upper, jnp.float32(1.0), jnp.float32(0.0)) * value
-            ahead = part if ahead is None else ahead + part
+            ahead = upper * value if ahead is None else ahead + upper * value
         return whole, ahead
 
     begins = tm_pos * steps
@@ -226,26 +277,25 @@
         enter_z = front_rate * (ahead_z + turn * whole_z + shear * whole_y) + front_shear * enter_y
         return enter_y, enter_z
 
-    def main_sums(here):
-        return sums(main[here, :], main_partner[here, :], here)
-
-    whole_y, ahead_y = main_sums(pl.ds(0, rows))
-    whole_z, ahead_z = main_sums(pl.ds(rows, rows))
+    def main_sums(i):
+        here = pl.ds(i * rows, rows)
+        left, right = pl.ds(2 * i * rows, rows), pl.ds((2 * i + 1) * rows, rows)
+        others = [jnp.concatenate([partner[left, :], partner[right, :]], axis=1) for partner in partners]
+        return sums(main[here, :], main_partner[here, :], *others)
+
+    (whole_y, ahead_y), (whole_z, ahead_z) = main_sums(0), main_sums(1)
     enter_y, enter_z = entering(whole_y, whole_z, ahead_y, ahead_z)
-    whole_e, ahead_e = sums(edge[...], edge_partner[...], pl.ds(2 * rows, tile))
-    whole_e, ahead_e = unpack_edges(sub, whole_e), unpack_edges(sub, ahead_e)
-    halo_y, halo_z = entering(*whole_e[:2], *ahead_e[:2])
-    more_y, more_z = entering(*whole_e[2:], *ahead_e[2:])
+    pair = [unpack_edges(sub, part[...]) for part in (edge, edge_partner)]
+    halos = [part[:2] for part in pair]
+    halos += [split_halo(partner[pl.ds(4 * rows, tile), :]) for partner in partners]
+    (whole_y, ahead_y), (whole_z, ahead_z) = [sums(*field) for field in zip(*halos)]
+    halo_y, halo_z = entering(whole_y, whole_z, ahead_y, ahead_z)
+    (whole_y, ahead_y), (whole_z, ahead_z) = [sums(*field) for field in zip(*[part[2:] for part in pair])]
+    more_y, more_z = entering(whole_y, whole_z, ahead_y, ahead_z)
     not_first = jnp.where(rows_pos > 0, jnp.float32(1.0), jnp.float32(0.0))
     not_last = jnp.where(rows_pos < lax.axis_size("rows") - 1, jnp.float32(1.0), jnp.float32(0.0))
     kept = jnp.where(sub < 4, not_last, not_first)
     row = lax.broadcasted_iota(jnp.int32, (rows, columns), 0)
-
-    def with_edges(value, more):
-        parts = [value[:tile]] if rows == tile else [value[:tile], value[tile:-tile], value[-tile:]]
-        parts[0] = parts[0] + jnp.where(sub == 0, more, 0.0)
-        parts[-1] = parts[-1] + jnp.where(sub == tile - 1, more, 0.0)
-        return jnp.concatenate([part for part in parts if part.shape[0]], axis=0)
 
     copies = []
     for j in range(steps):
@@ -281,19 +331,26 @@
     in_vmem = pl.BlockSpec(memory_space=pltpu.VMEM)
     in_hbm = pl.BlockSpec(memory_space=pl.ANY)
     params = pltpu.CompilerParams(vmem_limit_bytes=vmem_limit)
+    late = pl.CostEstimate(flops=10**10, bytes_accessed=10**8, transcendentals=0)
     pack = pltpu.VMEM((slots_of(steps)[1] * tile, columns), f32)
-    state, source, start, velocity, inside, across = pl.pallas_call(
-        load_kernel,
-        out_shape=[pltpu.VMEM(a.shape, f32) for a in (state, source, start, velocity)] + [pack, pack],
+    inside, across = pl.pallas_call(
+        pack_kernel,
+        out_shape=[pack, pack],
         in_specs=[in_hbm] * 4,
-        out_specs=[in_vmem] * 6,
-        scratch_shapes=[pltpu.SemaphoreType.DMA((4,))],
+        out_specs=[in_vmem] * 2,
+        scratch_shapes=[
+            pltpu.VMEM((2, steps, tile, columns), f32),
+            pltpu.VMEM((2, steps, tile, columns), f32),
+            pltpu.VMEM((2, tile, columns), f32),
+            pltpu.VMEM((2, 2, tile, columns), f32),
+            pltpu.SemaphoreType.DMA((8,)),
+        ],
         compiler_params=params,
-        name="load_and_pack",
+        name="pack_edge_rows",
     )(*[pltpu.with_memory_space_constraint(a, pltpu.HBM) for a in (state, source, start, velocity)])
 
+    inside = swapped(inside, "rows", lambda i: i ^ 1)
     across = swapped(across, "rows", lambda i: (i + (1 if i % 2 else -1)) % rows_count)
-    inside = swapped(inside, "rows", lambda i: i ^ 1)
 
     main, own_y, own_z = pl.pallas_call(
         functools.partial(carry_kernel, tm_count),
@@ -315,18 +372,24 @@
         in_specs=[in_vmem] * 4,
         out_specs=[in_vmem] * 2,
         compiler_params=params,
-        cost_estimate=pl.CostEstimate(flops=10**10, bytes_accessed=10**8, transcendentals=0),
+        cost_estimate=late,
         name="edge_carry",
     )(state, velocity, inside, across)
     edge_partner = swapped(edge, "tm", lambda i: i ^ 1)
 
-    partners = []
-    so_far = jnp.concatenate([main + main_partner, edge + edge_partner], axis=0)
-    for bit in range(1, tm_count.bit_length() - 1):
-        if partners:
-            so_far = so_far + partners[-1]
+    partners, bits = [], tm_count.bit_length() - 1
+    so_far = pl.pallas_call(
+        join_kernel,
+        out_shape=pltpu.VMEM((4 * rows + tile, columns // 2), f32),
+        in_specs=[in_vmem] * 4,
+        out_specs=in_vmem,
+        compiler_params=params,
+        name="join_edges",
+    )(main, edge, main_partner, edge_partner)
+    for bit in range(1, bits):
         mask = 3 << (bit - 1) if bit > 1 else 1 << bit
         partners.append(swapped(so_far, "tm", lambda i: i ^ mask))
+        so_far = so_far + partners[-1]
 
     return pl.pallas_call(
         functools.partial(final_kernel, tm_count),

time: 23.8 us -> 23.5 us (0.987)
    pallas_call x1 -> x2, Pallas kernels: 1.12 us -> 1.01 us  [the longest x1 0.98 us: on_device(): pl.pallas_call(pack_kernel, out_shape=[pack, pack], in_specs=[in_hbm] * 4...]
where the time goes in v4:
time: 23.5 us; the launch traced here: 23.3 us
  starting transfers between devices  11.6 us (49%)
  waiting for transfers between devices  9.43 us (40%)
  Pallas kernels  2.22 us (9%)
    ppermute x6, starting transfers between devices, swapped(): lax.ppermute(value, axis, [(i, partner(i)) for i in range(lax.axis_size(a...  11.6 us
    ppermute x6, waiting for transfers between devices, swapped(): lax.ppermute(value, axis, [(i, partner(i)) for i in range(lax.axis_size(a...  9.43 us
    pallas_call x1, Pallas kernels, on_device(): pl.pallas_call(pack_kernel, out_shape=[pack, pack], in_specs=[in_hbm] * 4...  0.98 us
    pallas_call x1, Pallas kernels, on_device(): pl.pallas_call(functools.partial(final_kernel, tm_count), out_shape=jax.S...  0.9 us
  transfers between devices with their start and end apart: 6, of which 3 were waited for; matrix products, arithmetic and copies ran while one was open for 0% of the time, Pallas kernels for 1%

profile of v4, /device:TPU:0, one launch (start us, length us, event | category | flops | bytes accessed | tf_op | source)
XLA Modules:
  0.0 23.3 jit_solution(13698793027723023559)
XLA Ops:
  0.0 0.0 copy-start
  0.0 0.0 copy-start.2
  0.0 0.0 copy-start.3
  0.0 0.0 copy-start.1
  0.0 1.0 %pack_edge_rows.1 = (f32[16,512]{1,0:T(8,128)S(1)}, f32[16,512]{1,0:T(8,128)S(1)}) custom-call(f32[2,32,512]{2,1,0:T(8,128)} %state.5, f32[2,32,512]{2,1,0:T(8,128)} %source.3, f32[32,512]{1,0:T(8,128)} %start.3, f32[2,32,512]{2,1,0:T(8,128)} %velocity.7), custom_call_target="tpu_custom_call" | custom-call | tf_op jit(solution)/shard_map/pack_edge_rows/pallas_call | solution.py:336
  1.0 0.5 %collective-permute-start = (f32[16,512]{1,0:T(8,128)S(1)}, f32[16,512]{1,0:T(8,128)S(1)}, u32[]{:S(2)}, u32[]{:S(2)}) collective-permute-start(f32[16,512]{1,0:T(8,128)S(1)} %get-tuple-element.14), channel_id=1, source_target_pairs={{0,1},{1,0},{2,3},{3,2},{4,5},{5,4},{6,7},{7,6},{8,9},{9,8},{10,11... | collective-permute-start | bytes 98312 | tf_op jit(solution)/shard_map/ppermute | solution.py:323
  1.5 2.6 %collective-permute-start.1 = (f32[16,512]{1,0:T(8,128)S(1)}, f32[16,512]{1,0:T(8,128)S(1)}, u32[]{:S(2)}, u32[]{:S(2)}) collective-permute-start(f32[16,512]{1,0:T(8,128)S(1)} %get-tuple-element.15), channel_id=1, source_target_pairs={{0,3},{1,2},{2,1},{3,0},{4,7},{5,6},{6,5},{7,4},{8,11},{9,10},{10,... | collective-permute-start | bytes 98312 | tf_op jit(solution)/shard_map/ppermute | solution.py:323
  4.1 0.0 copy-done
  4.1 0.0 copy-done.2
  4.2 0.0 copy-done.3
  4.2 0.0 copy-done.1
  4.2 0.2 own_carry.1
  4.4 1.6 %collective-permute-start.2 = (f32[64,512]{1,0:T(8,128)S(1)}, f32[64,512]{1,0:T(8,128)S(1)}, u32[]{:S(2)}, u32[]{:S(2)}) collective-permute-start(f32[64,512]{1,0:T(8,128)S(1)} %get-tuple-element.17.main), channel_id=1, source_target_pairs={{0,4},{4,0},{8,12},{12,8},{16,20},{20,16},{24,28},{28,24},{1,5},{5... | collective-permute-start | bytes 393224 | tf_op jit(solution)/shard_map/ppermute | solution.py:323
  5.9 0.0 collective-permute-done.inside
  5.9 0.0 collective-permute-done.1.across
  5.9 0.1 edge_carry.1
  6.1 1.6 %collective-permute-start.3 = (f32[8,512]{1,0:T(8,128)S(1)}, f32[8,512]{1,0:T(8,128)S(1)}, u32[]{:S(2)}, u32[]{:S(2)}) collective-permute-start(f32[8,512]{1,0:T(8,128)S(1)} %get-tuple-element.18.edge), channel_id=1, source_target_pairs={{0,4},{4,0},{8,12},{12,8},{16,20},{20,16},{24,28},{28,24},{1,5},{5... | collective-permute-start | bytes 49160 | tf_op jit(solution)/shard_map/ppermute | solution.py:323
  7.7 2.6 %collective-permute-done.3.edge_partner = f32[8,512]{1,0:T(8,128)S(1)} collective-permute-done((f32[8,512]{1,0:T(8,128)S(1)}, f32[8,512]{1,0:T(8,128)S(1)}, u32[]{:S(2)}, u32[]{:S(2)}) %collective-permute-start.3) | collective-permute-done | bytes 16416 | tf_op jit(solution)/shard_map/ppermute | solution.py:323
  10.2 0.0 collective-permute-done.2.main_partner
  10.3 1.6 %collective-permute-start.4 = (f32[136,256]{1,0:T(8,128)S(1)}, f32[136,256]{1,0:T(8,128)S(1)}, u32[]{:S(2)}, u32[]{:S(2)}) collective-permute-start(f32[136,256]{1,0:T(8,128)S(1)} %join_edges.1), channel_id=1, source_target_pairs={{0,8},{4,12},{8,0},{12,4},{16,24},{20,28},{24,16},{28,20},{1,9},{5... | collective-permute-start | bytes 417800 | tf_op jit(solution)/shard_map/ppermute | solution.py:323
  11.9 3.5 %collective-permute-done.4.rest_0_ = f32[136,256]{1,0:T(8,128)S(1)} collective-permute-done((f32[136,256]{1,0:T(8,128)S(1)}, f32[136,256]{1,0:T(8,128)S(1)}, u32[]{:S(2)}, u32[]{:S(2)}) %collective-permute-start.4) | collective-permute-done | bytes 139296 | tf_op jit(solution)/shard_map/ppermute | solution.py:323
  15.4 3.7 %collective-permute-start.5 = (f32[136,256]{1,0:T(8,128)S(1)}, f32[136,256]{1,0:T(8,128)S(1)}, u32[]{:S(2)}, u32[]{:S(2)}) collective-permute-start(f32[136,256]{1,0:T(8,128)S(1)} %add.3), channel_id=1, source_target_pairs={{0,24},{4,28},{8,16},{12,20},{16,8},{20,12},{24,0},{28,4},{1,25},{... | collective-permute-start | bytes 417800 | tf_op jit(solution)/shard_map/ppermute | solution.py:323
  19.1 3.4 %collective-permute-done.5.rest_1_ = f32[136,256]{1,0:T(8,128)S(1)} collective-permute-done((f32[136,256]{1,0:T(8,128)S(1)}, f32[136,256]{1,0:T(8,128)S(1)}, u32[]{:S(2)}, u32[]{:S(2)}) %collective-permute-start.5) | collective-permute-done | bytes 139296 | tf_op jit(solution)/shard_map/ppermute | solution.py:323
  22.4 0.9 %enter_and_couple.1 = f32[2,32,512]{2,1,0:T(8,128)} custom-call(f32[2,32,512]{2,1,0:T(8,128)S(1)} %copy-done, f32[2,32,512]{2,1,0:T(8,128)S(1)} %get-tuple-element.12.own_y, f32[2,32,512]{2,1,0:T(8,128)S(1)} %get-tuple-element.13.own_z, f32[2,8,512]{2,1,0:T(8,128)S(1)} %get-tuple-element.16.own_edge, f32[64,512]{1,0:T(8,128)S(1)} %get-tuple-element.17.main, ...), custom_call_target="tpu_custom_call" | custom-call | tf_op jit(solution)/shard_map/enter_and_couple/pallas_call | solution.py:394
  (2 shorter events, 0.0 us)
Async XLA Ops:
  0.0 4.1 %copy-start = (f32[2,32,512]{2,1,0:T(8,128)S(1)}, f32[2,32,512]{2,1,0:T(8,128)}, u32[]{:S(2)}) copy-start(f32[2,32,512]{2,1,0:T(8,128)} %velocity.7) | copy-start | bytes 393220
  0.0 4.1 %copy-start.2 = (f32[2,32,512]{2,1,0:T(8,128)S(1)}, f32[2,32,512]{2,1,0:T(8,128)}, u32[]{:S(2)}) copy-start(f32[2,32,512]{2,1,0:T(8,128)} %state.5) | copy-start | bytes 393220
  0.0 4.1 %copy-start.3 = (f32[32,512]{1,0:T(8,128)S(1)}, f32[32,512]{1,0:T(8,128)}, u32[]{:S(2)}) copy-start(f32[32,512]{1,0:T(8,128)} %start.3) | copy-start | bytes 196612
  0.0 4.2 %copy-start.1 = (f32[2,32,512]{2,1,0:T(8,128)S(1)}, f32[2,32,512]{2,1,0:T(8,128)}, u32[]{:S(2)}) copy-start(f32[2,32,512]{2,1,0:T(8,128)} %source.3) | copy-start | bytes 393220
  1.0 4.9 %collective-permute-start = (f32[16,512]{1,0:T(8,128)S(1)}, f32[16,512]{1,0:T(8,128)S(1)}, u32[]{:S(2)}, u32[]{:S(2)}) collective-permute-start(f32[16,512]{1,0:T(8,128)S(1)} %get-tuple-element.14), channel_id=1, source_target_pairs={{0,1},{1,0},{2,3},{3,2},{4,5},{5,4},{6,7},{7,6},{8,9},{9,8},{10,11... | collective-permute-start | bytes 98312 | tf_op jit(solution)/shard_map/ppermute | solution.py:323
  1.5 4.4 %collective-permute-start.1 = (f32[16,512]{1,0:T(8,128)S(1)}, f32[16,512]{1,0:T(8,128)S(1)}, u32[]{:S(2)}, u32[]{:S(2)}) collective-permute-start(f32[16,512]{1,0:T(8,128)S(1)} %get-tuple-element.15), channel_id=1, source_target_pairs={{0,3},{1,2},{2,1},{3,0},{4,7},{5,6},{6,5},{7,4},{8,11},{9,10},{10,... | collective-permute-start | bytes 98312 | tf_op jit(solution)/shard_map/ppermute | solution.py:323
  4.4 5.9 %collective-permute-start.2 = (f32[64,512]{1,0:T(8,128)S(1)}, f32[64,512]{1,0:T(8,128)S(1)}, u32[]{:S(2)}, u32[]{:S(2)}) collective-permute-start(f32[64,512]{1,0:T(8,128)S(1)} %get-tuple-element.17.main), channel_id=1, source_target_pairs={{0,4},{4,0},{8,12},{12,8},{16,20},{20,16},{24,28},{28,24},{1,5},{5... | collective-permute-start | bytes 393224 | tf_op jit(solution)/shard_map/ppermute | solution.py:323
  6.1 4.2 %collective-permute-start.3 = (f32[8,512]{1,0:T(8,128)S(1)}, f32[8,512]{1,0:T(8,128)S(1)}, u32[]{:S(2)}, u32[]{:S(2)}) collective-permute-start(f32[8,512]{1,0:T(8,128)S(1)} %get-tuple-element.18.edge), channel_id=1, source_target_pairs={{0,4},{4,0},{8,12},{12,8},{16,20},{20,16},{24,28},{28,24},{1,5},{5... | collective-permute-start | bytes 49160 | tf_op jit(solution)/shard_map/ppermute | solution.py:323
  10.3 5.1 %collective-permute-start.4 = (f32[136,256]{1,0:T(8,128)S(1)}, f32[136,256]{1,0:T(8,128)S(1)}, u32[]{:S(2)}, u32[]{:S(2)}) collective-permute-start(f32[136,256]{1,0:T(8,128)S(1)} %join_edges.1), channel_id=1, source_target_pairs={{0,8},{4,12},{8,0},{12,4},{16,24},{20,28},{24,16},{28,20},{1,9},{5... | collective-permute-start | bytes 417800 | tf_op jit(solution)/shard_map/ppermute | solution.py:323
  15.4 7.0 %collective-permute-start.5 = (f32[136,256]{1,0:T(8,128)S(1)}, f32[136,256]{1,0:T(8,128)S(1)}, u32[]{:S(2)}, u32[]{:S(2)}) collective-permute-start(f32[136,256]{1,0:T(8,128)S(1)} %add.3), channel_id=1, source_target_pairs={{0,24},{4,28},{8,16},{12,20},{16,8},{20,12},{24,0},{28,4},{1,25},{... | collective-permute-start | bytes 417800 | tf_op jit(solution)/shard_map/ppermute | solution.py:323

commit v5 on v4

--- a/solution.py
+++ b/solution.py
@@ -14,8 +14,7 @@
 vmem_limit = 32 * 1024 * 1024
 
 
-def dims_of(state, tm_count):
-    steps = state.shape[0]
+def dims_of(steps, tm_count):
     time_total = steps * tm_count
     time_scale = 0.5 * time_total
     gain = 1.0 / (time_scale + 4.0 * diffusion)
@@ -28,6 +27,21 @@
         is_set = jnp.bitwise_and(jnp.right_shift(exponent, bit), 1) == 1
         result = result * jnp.where(is_set, jnp.float32(base ** (2**bit)), jnp.float32(1.0))
     return result
+
+
+def bit_is_set(number, bit):
+    is_set = jnp.bitwise_and(jnp.right_shift(number, bit), 1) == 1
+    return jnp.where(is_set, jnp.float32(1.0), jnp.float32(0.0))
+
+
+def swaps_order(bits):
+    return bits > 2
+
+
+def bit_of(level, bits, parity):
+    if parity and swaps_order(bits) and level >= bits - 2:
+        return 2 * bits - 3 - level
+    return level
 
 
 def slots_of(steps):
@@ -125,7 +139,7 @@
 
 
 def carry_kernel(tm_count, state, source, start, velocity, total, own_y, own_z):
-    steps, time_total, gain, rate = dims_of(state, tm_count)
+    steps, time_total, gain, rate = dims_of(state.shape[0], tm_count)
     rows, columns = state.shape[1:]
     row = lax.broadcasted_iota(jnp.int32, (rows, columns), 0)
     y = z = None
@@ -148,7 +162,7 @@
 
 
 def edge_kernel(tm_count, state, velocity, inside, across, total, own_edge):
-    steps, time_total, gain, rate = dims_of(state, tm_count)
+    steps, time_total, gain, rate = dims_of(state.shape[0], tm_count)
     rows, columns = state.shape[1:]
     place, _ = slots_of(steps)
     rows_pos = lax.axis_index("rows")
@@ -225,6 +239,33 @@
     )
 
 
+def weigh_kernel(tm_count, steps, own, partner, total):
+    bits = tm_count.bit_length() - 1
+    _, time_total, gain, rate = dims_of(steps, tm_count)
+    tm_pos = lax.axis_index("tm")
+    plain = lax.axis_index("rows") % 2 == 0
+    wrap = wrap_weight * rate**time_total
+    after_own, after_partner = bit_is_set(tm_pos, bits - 2), 1.0 - bit_is_set(tm_pos, bits - 1)
+
+    def weights(is_after):
+        is_after = jnp.where(plain, jnp.float32(0.0), is_after)
+        same = jnp.where(is_after > 0.5, jnp.float32(wrap), jnp.float32(1.0))
+        return same, is_after * (wrap * time_total * gain)
+
+    (same_own, mixed_own), (same_partner, mixed_partner) = weights(after_own), weights(after_partner)
+    deep = (own.shape[0] - tile) // 2
+    of_y, of_z, halo = pl.ds(0, deep), pl.ds(deep, deep), pl.ds(2 * deep, tile)
+    total[of_y, :] = same_own * own[of_y, :] + same_partner * partner[of_y, :]
+    total[of_z, :] = (same_own * own[of_z, :] + same_partner * partner[of_z, :]) + (
+        mixed_own * own[of_y, :] + mixed_partner * partner[of_y, :]
+    )
+    mixed = mixed_own * own[halo, :] + mixed_partner * partner[halo, :]
+    sub = lax.broadcasted_iota(jnp.int32, mixed.shape, 0)
+    mixed = jnp.where(sub < 4, pltpu.roll(mixed, 2, 0), pltpu.roll(mixed, tile - 2, 0))
+    is_z = (sub >= 2) & (sub < tile - 2)
+    total[halo, :] = (same_own * own[halo, :] + same_partner * partner[halo, :]) + jnp.where(is_z, mixed, 0.0)
+
+
 def split_halo(packed):
     def whole(at):
         value = []
@@ -245,7 +286,7 @@
 
 def final_kernel(tm_count, velocity, own_y, own_z, own_edge, main, edge, main_partner, edge_partner, *rest):
     partners, out, done, sems = rest[:-3], rest[-3], rest[-2], rest[-1]
-    steps, time_total, gain, rate = dims_of(own_y, tm_count)
+    steps, time_total, gain, rate = dims_of(own_y.shape[0], tm_count)
     rows, columns = own_y.shape[1:]
     rows_pos = lax.axis_index("rows")
     tm_pos = lax.axis_index("tm")
@@ -254,12 +295,15 @@
     shear = time_total * gain * wrap / (1.0 - wrap) ** 2
     sub = lax.broadcasted_iota(jnp.int32, (tile, columns), 0)
 
-    uppers = [
-        jnp.where(
-            jnp.bitwise_and(jnp.right_shift(tm_pos, bit), 1) == 1, jnp.float32(1.0), jnp.float32(0.0)
-        )
-        for bit in range(1 + len(partners))
-    ]
+    odd, bits = rows_pos % 2 == 1, tm_count.bit_length() - 1
+
+    def is_upper(level):
+        upper = [bit_is_set(tm_pos, bit_of(level, bits, parity)) for parity in range(2)]
+        if swaps_order(bits) and level == bits - 1:
+            upper[1] = jnp.float32(1.0)
+        return jnp.where(odd, upper[1], upper[0])
+
+    uppers = [is_upper(level) for level in range(bits)]
 
     def sums(own, *others):
         whole, ahead = own, None
@@ -386,10 +430,24 @@
         compiler_params=params,
         name="join_edges",
     )(main, edge, main_partner, edge_partner)
-    for bit in range(1, bits):
-        mask = 3 << (bit - 1) if bit > 1 else 1 << bit
-        partners.append(swapped(so_far, "tm", lambda i: i ^ mask))
-        so_far = so_far + partners[-1]
+    for level in range(1, bits):
+        if level > 1 and level == bits - 1:
+            so_far = pl.pallas_call(
+                functools.partial(weigh_kernel, tm_count, steps),
+                out_shape=pltpu.VMEM(so_far.shape, f32),
+                in_specs=[in_vmem] * 2,
+                out_specs=in_vmem,
+                compiler_params=params,
+                name="weigh_groups",
+            )(so_far, partners[-1])
+        elif level > 1:
+            so_far = so_far + partners[-1]
+        pairs = [
+            (i * rows_count + r, (i ^ 1 << bit_of(level, bits, r % 2)) * rows_count + r)
+            for i in range(tm_count)
+            for r in range(rows_count)
+        ]
+        partners.append(lax.ppermute(so_far, ("tm", "rows"), pairs))
 
     return pl.pallas_call(
         functools.partial(final_kernel, tm_count),

time: 23.5 us -> 23 us (0.979)
  starting transfers between devices: 11.6 us -> 10.6 us
  waiting for transfers between devices: 9.43 us -> 9.88 us
    ppermute x0 -> x2, waiting for transfers between devices: none -> 7.29 us  [on_device(): partners.append(lax.ppermute(so_far, ('tm', 'rows'), pairs))]
    ppermute x6 -> x4, waiting for transfers between devices: 9.43 us -> 2.59 us  [swapped(): lax.ppermute(value, axis, [(i, partner(i)) for i in range(lax.axis_size(a...]
    ppermute x6 -> x4, starting transfers between devices: 11.6 us -> 6.31 us  [swapped(): lax.ppermute(value, axis, [(i, partner(i)) for i in range(lax.axis_size(a...]
    ppermute x0 -> x2, starting transfers between devices: none -> 4.31 us  [on_device(): partners.append(lax.ppermute(so_far, ('tm', 'rows'), pairs))]
where the time goes in v5:
time: 23 us; the launch traced here: 22.8 us
  starting transfers between devices  10.6 us (46%)
  waiting for transfers between devices  9.88 us (43%)
  Pallas kernels  2.26 us (10%)
    ppermute x2, waiting for transfers between devices, on_device(): partners.append(lax.ppermute(so_far, ('tm', 'rows'), pairs))  7.29 us
    ppermute x4, starting transfers between devices, swapped(): lax.ppermute(value, axis, [(i, partner(i)) for i in range(lax.axis_size(a...  6.31 us
    ppermute x2, starting transfers between devices, on_device(): partners.append(lax.ppermute(so_far, ('tm', 'rows'), pairs))  4.31 us
    ppermute x4, waiting for transfers between devices, swapped(): lax.ppermute(value, axis, [(i, partner(i)) for i in range(lax.axis_size(a...  2.59 us
    pallas_call x1, Pallas kernels, on_device(): pl.pallas_call(pack_kernel, out_shape=[pack, pack], in_specs=[in_hbm] * 4...  0.98 us
    pallas_call x1, Pallas kernels, on_device(): pl.pallas_call(functools.partial(final_kernel, tm_count), out_shape=jax.S...  0.9 us
  transfers between devices with their start and end apart: 6, of which 3 were waited for; matrix products, arithmetic and copies ran while one was open for 0% of the time, Pallas kernels for 1%

profile of v5, /device:TPU:0, one launch (start us, length us, event | category | flops | bytes accessed | tf_op | source)
XLA Modules:
  0.0 22.8 jit_solution(15795782724002146400)
XLA Ops:
  0.0 0.0 copy-start
  0.0 0.0 copy-start.2
  0.0 0.0 copy-start.3
  0.0 0.0 copy-start.1
  0.0 1.0 %pack_edge_rows.1 = (f32[16,512]{1,0:T(8,128)S(1)}, f32[16,512]{1,0:T(8,128)S(1)}) custom-call(f32[2,32,512]{2,1,0:T(8,128)} %state.5, f32[2,32,512]{2,1,0:T(8,128)} %source.3, f32[32,512]{1,0:T(8,128)} %start.3, f32[2,32,512]{2,1,0:T(8,128)} %velocity.7), custom_call_target="tpu_custom_call" | custom-call | tf_op jit(solution)/shard_map/pack_edge_rows/pallas_call | solution.py:380
  1.0 0.5 %collective-permute-start = (f32[16,512]{1,0:T(8,128)S(1)}, f32[16,512]{1,0:T(8,128)S(1)}, u32[]{:S(2)}, u32[]{:S(2)}) collective-permute-start(f32[16,512]{1,0:T(8,128)S(1)} %get-tuple-element.14), channel_id=1, source_target_pairs={{0,1},{1,0},{2,3},{3,2},{4,5},{5,4},{6,7},{7,6},{8,9},{9,8},{10,11... | collective-permute-start | bytes 98312 | tf_op jit(solution)/shard_map/ppermute | solution.py:367
  1.5 2.6 %collective-permute-start.1 = (f32[16,512]{1,0:T(8,128)S(1)}, f32[16,512]{1,0:T(8,128)S(1)}, u32[]{:S(2)}, u32[]{:S(2)}) collective-permute-start(f32[16,512]{1,0:T(8,128)S(1)} %get-tuple-element.15), channel_id=1, source_target_pairs={{0,3},{1,2},{2,1},{3,0},{4,7},{5,6},{6,5},{7,4},{8,11},{9,10},{10,... | collective-permute-start | bytes 98312 | tf_op jit(solution)/shard_map/ppermute | solution.py:367
  4.1 0.0 copy-done
  4.1 0.0 copy-done.2
  4.2 0.0 copy-done.3
  4.2 0.0 copy-done.1
  4.2 0.2 own_carry.1
  4.4 1.6 %collective-permute-start.2 = (f32[64,512]{1,0:T(8,128)S(1)}, f32[64,512]{1,0:T(8,128)S(1)}, u32[]{:S(2)}, u32[]{:S(2)}) collective-permute-start(f32[64,512]{1,0:T(8,128)S(1)} %get-tuple-element.17.main), channel_id=1, source_target_pairs={{0,4},{4,0},{8,12},{12,8},{16,20},{20,16},{24,28},{28,24},{1,5},{5... | collective-permute-start | bytes 393224 | tf_op jit(solution)/shard_map/ppermute | solution.py:367
  5.9 0.0 collective-permute-done.inside
  5.9 0.0 collective-permute-done.1.across
  5.9 0.1 edge_carry.1
  6.1 1.6 %collective-permute-start.3 = (f32[8,512]{1,0:T(8,128)S(1)}, f32[8,512]{1,0:T(8,128)S(1)}, u32[]{:S(2)}, u32[]{:S(2)}) collective-permute-start(f32[8,512]{1,0:T(8,128)S(1)} %get-tuple-element.18.edge), channel_id=1, source_target_pairs={{0,4},{4,0},{8,12},{12,8},{16,20},{20,16},{24,28},{28,24},{1,5},{5... | collective-permute-start | bytes 49160 | tf_op jit(solution)/shard_map/ppermute | solution.py:367
  7.7 2.6 %collective-permute-done.3.edge_partner = f32[8,512]{1,0:T(8,128)S(1)} collective-permute-done((f32[8,512]{1,0:T(8,128)S(1)}, f32[8,512]{1,0:T(8,128)S(1)}, u32[]{:S(2)}, u32[]{:S(2)}) %collective-permute-start.3) | collective-permute-done | bytes 16416 | tf_op jit(solution)/shard_map/ppermute | solution.py:367
  10.2 0.0 collective-permute-done.2.main_partner
  10.3 1.6 %collective-permute-start.4 = (f32[136,256]{1,0:T(8,128)S(1)}, f32[136,256]{1,0:T(8,128)S(1)}, u32[]{:S(2)}, u32[]{:S(2)}) collective-permute-start(f32[136,256]{1,0:T(8,128)S(1)} %join_edges.1.own), channel_id=1, source_target_pairs={{0,8},{1,17},{2,10},{3,19},{4,12},{5,21},{6,14},{7,23},{8,0},{9,25... | collective-permute-start | bytes 417800 | tf_op jit(solution)/shard_map/ppermute | solution.py:450
  11.9 3.9 %collective-permute-done.4.partner.rest_0_ = f32[136,256]{1,0:T(8,128)S(1)} collective-permute-done((f32[136,256]{1,0:T(8,128)S(1)}, f32[136,256]{1,0:T(8,128)S(1)}, u32[]{:S(2)}, u32[]{:S(2)}) %collective-permute-start.4) | collective-permute-done | bytes 139296 | tf_op jit(solution)/shard_map/ppermute | solution.py:450
  15.9 2.7 %collective-permute-start.5 = (f32[136,256]{1,0:T(8,128)S(1)}, f32[136,256]{1,0:T(8,128)S(1)}, u32[]{:S(2)}, u32[]{:S(2)}) collective-permute-start(f32[136,256]{1,0:T(8,128)S(1)} %weigh_groups.1), channel_id=1, source_target_pairs={{0,16},{1,9},{2,18},{3,11},{4,20},{5,13},{6,22},{7,15},{8,24},{9,1... | collective-permute-start | bytes 417800 | tf_op jit(solution)/shard_map/ppermute | solution.py:450
  18.6 3.4 %collective-permute-done.5.rest_1_ = f32[136,256]{1,0:T(8,128)S(1)} collective-permute-done((f32[136,256]{1,0:T(8,128)S(1)}, f32[136,256]{1,0:T(8,128)S(1)}, u32[]{:S(2)}, u32[]{:S(2)}) %collective-permute-start.5) | collective-permute-done | bytes 139296 | tf_op jit(solution)/shard_map/ppermute | solution.py:450
  21.9 0.9 %enter_and_couple.1 = f32[2,32,512]{2,1,0:T(8,128)} custom-call(f32[2,32,512]{2,1,0:T(8,128)S(1)} %copy-done, f32[2,32,512]{2,1,0:T(8,128)S(1)} %get-tuple-element.12.own_y, f32[2,32,512]{2,1,0:T(8,128)S(1)} %get-tuple-element.13.own_z, f32[2,8,512]{2,1,0:T(8,128)S(1)} %get-tuple-element.16.own_edge, f32[64,512]{1,0:T(8,128)S(1)} %get-tuple-element.17.main, ...), custom_call_target="tpu_custom_call" | custom-call | tf_op jit(solution)/shard_map/enter_and_couple/pallas_call | solution.py:452
  (2 shorter events, 0.1 us)
Async XLA Ops:
  0.0 4.1 %copy-start = (f32[2,32,512]{2,1,0:T(8,128)S(1)}, f32[2,32,512]{2,1,0:T(8,128)}, u32[]{:S(2)}) copy-start(f32[2,32,512]{2,1,0:T(8,128)} %velocity.7) | copy-start | bytes 393220
  0.0 4.1 %copy-start.2 = (f32[2,32,512]{2,1,0:T(8,128)S(1)}, f32[2,32,512]{2,1,0:T(8,128)}, u32[]{:S(2)}) copy-start(f32[2,32,512]{2,1,0:T(8,128)} %state.5) | copy-start | bytes 393220
  0.0 4.1 %copy-start.3 = (f32[32,512]{1,0:T(8,128)S(1)}, f32[32,512]{1,0:T(8,128)}, u32[]{:S(2)}) copy-start(f32[32,512]{1,0:T(8,128)} %start.3) | copy-start | bytes 196612
  0.0 4.2 %copy-start.1 = (f32[2,32,512]{2,1,0:T(8,128)S(1)}, f32[2,32,512]{2,1,0:T(8,128)}, u32[]{:S(2)}) copy-start(f32[2,32,512]{2,1,0:T(8,128)} %source.3) | copy-start | bytes 393220
  1.0 4.9 %collective-permute-start = (f32[16,512]{1,0:T(8,128)S(1)}, f32[16,512]{1,0:T(8,128)S(1)}, u32[]{:S(2)}, u32[]{:S(2)}) collective-permute-start(f32[16,512]{1,0:T(8,128)S(1)} %get-tuple-element.14), channel_id=1, source_target_pairs={{0,1},{1,0},{2,3},{3,2},{4,5},{5,4},{6,7},{7,6},{8,9},{9,8},{10,11... | collective-permute-start | bytes 98312 | tf_op jit(solution)/shard_map/ppermute | solution.py:367
  1.5 4.4 %collective-permute-start.1 = (f32[16,512]{1,0:T(8,128)S(1)}, f32[16,512]{1,0:T(8,128)S(1)}, u32[]{:S(2)}, u32[]{:S(2)}) collective-permute-start(f32[16,512]{1,0:T(8,128)S(1)} %get-tuple-element.15), channel_id=1, source_target_pairs={{0,3},{1,2},{2,1},{3,0},{4,7},{5,6},{6,5},{7,4},{8,11},{9,10},{10,... | collective-permute-start | bytes 98312 | tf_op jit(solution)/shard_map/ppermute | solution.py:367
  4.4 5.9 %collective-permute-start.2 = (f32[64,512]{1,0:T(8,128)S(1)}, f32[64,512]{1,0:T(8,128)S(1)}, u32[]{:S(2)}, u32[]{:S(2)}) collective-permute-start(f32[64,512]{1,0:T(8,128)S(1)} %get-tuple-element.17.main), channel_id=1, source_target_pairs={{0,4},{4,0},{8,12},{12,8},{16,20},{20,16},{24,28},{28,24},{1,5},{5... | collective-permute-start | bytes 393224 | tf_op jit(solution)/shard_map/ppermute | solution.py:367
  6.1 4.2 %collective-permute-start.3 = (f32[8,512]{1,0:T(8,128)S(1)}, f32[8,512]{1,0:T(8,128)S(1)}, u32[]{:S(2)}, u32[]{:S(2)}) collective-permute-start(f32[8,512]{1,0:T(8,128)S(1)} %get-tuple-element.18.edge), channel_id=1, source_target_pairs={{0,4},{4,0},{8,12},{12,8},{16,20},{20,16},{24,28},{28,24},{1,5},{5... | collective-permute-start | bytes 49160 | tf_op jit(solution)/shard_map/ppermute | solution.py:367
  10.3 5.6 %collective-permute-start.4 = (f32[136,256]{1,0:T(8,128)S(1)}, f32[136,256]{1,0:T(8,128)S(1)}, u32[]{:S(2)}, u32[]{:S(2)}) collective-permute-start(f32[136,256]{1,0:T(8,128)S(1)} %join_edges.1.own), channel_id=1, source_target_pairs={{0,8},{1,17},{2,10},{3,19},{4,12},{5,21},{6,14},{7,23},{8,0},{9,25... | collective-permute-start | bytes 417800 | tf_op jit(solution)/shard_map/ppermute | solution.py:450
  15.9 6.0 %collective-permute-start.5 = (f32[136,256]{1,0:T(8,128)S(1)}, f32[136,256]{1,0:T(8,128)S(1)}, u32[]{:S(2)}, u32[]{:S(2)}) collective-permute-start(f32[136,256]{1,0:T(8,128)S(1)} %weigh_groups.1), channel_id=1, source_target_pairs={{0,16},{1,9},{2,18},{3,11},{4,20},{5,13},{6,22},{7,15},{8,24},{9,1... | collective-permute-start | bytes 417800 | tf_op jit(solution)/shard_map/ppermute | solution.py:450

commit v6 on v5

--- a/solution.py
+++ b/solution.py
@@ -34,14 +34,8 @@
     return jnp.where(is_set, jnp.float32(1.0), jnp.float32(0.0))
 
 
-def swaps_order(bits):
-    return bits > 2
-
-
 def bit_of(level, bits, parity):
-    if parity and swaps_order(bits) and level >= bits - 2:
-        return 2 * bits - 3 - level
-    return level
+    return (level + 1) % bits if parity else level
 
 
 def slots_of(steps):
@@ -218,52 +212,66 @@
     return jnp.concatenate([part for part in parts if part.shape[0]], axis=0)
 
 
-def join_kernel(main, edge, main_partner, edge_partner, total):
+def weights_of(tm_count, steps):
+    bits = tm_count.bit_length() - 1
+    _, time_total, gain, rate = dims_of(steps, tm_count)
+    wrap = wrap_weight * rate**time_total
+    tm_pos = lax.axis_index("tm")
+    is_odd = bit_is_set(lax.axis_index("rows"), 0)
+
+    def weights(level):
+        is_after = bit_is_set(tm_pos, 0) if level is None else 1.0 - bit_is_set(tm_pos, bit_of(level, bits, 1))
+        is_after = is_odd * is_after
+        same = jnp.where(is_after > 0.5, jnp.float32(wrap), jnp.float32(1.0))
+        return same, is_after * (wrap * time_total * gain)
+
+    return weights
+
+
+def join_kernel(tm_count, steps, is_last, main, edge, main_partner, edge_partner, total):
     rows, half = main.shape[0] // 2, main.shape[1] // 2
-    edges = edge[...] + edge_partner[...]
-    sub = lax.broadcasted_iota(jnp.int32, edges.shape, 0)
-    _, _, *more = unpack_edges(sub, edges)
-    for i in range(2):
-        here = pl.ds(i * rows, rows)
-        value = with_edges(main[here, :] + main_partner[here, :], more[i])
+    sub = lax.broadcasted_iota(jnp.int32, edge.shape, 0)
+    weights = weights_of(tm_count, steps)
+    sums = None
+    for level, of_main, of_edge in ((None, main, edge), (0, main_partner, edge_partner)):
+        values = [of_main[pl.ds(0, rows), :], of_main[pl.ds(rows, rows), :], *unpack_edges(sub, of_edge[...])]
+        if is_last:
+            same, mixed = weights(level)
+            for i in range(0, len(values), 2):
+                values[i], values[i + 1] = same * values[i], same * values[i + 1] + mixed * values[i]
+        sums = values if sums is None else [a + b for a, b in zip(sums, values)]
+    main_y, main_z, halo_y, halo_z, more_y, more_z = sums
+    for i, value in enumerate((with_edges(main_y, more_y), with_edges(main_z, more_z))):
         for side in range(2):
             total[pl.ds((2 * i + side) * rows, rows), :] = value[:, side * half : (side + 1) * half]
-    left, right = edges[:, :half], edges[:, half:]
-    sub = lax.broadcasted_iota(jnp.int32, left.shape, 0)
-    outer = jnp.where(sub == 0, left, pltpu.roll(right, 1, 0))
-    last = jnp.where(sub == tile - 1, right, pltpu.roll(left, tile - 1, 0))
-    inner = jnp.where(sub == 2, pltpu.roll(left, 1, 0), pltpu.roll(right, 2, 0))
-    before = jnp.where(sub == 4, pltpu.roll(left, tile - 2, 0), pltpu.roll(right, tile - 1, 0))
-    total[pl.ds(4 * rows, tile), :] = jnp.where(
-        sub < 2, outer, jnp.where(sub < 4, inner, jnp.where(sub < 6, before, last))
-    )
-
-
-def weigh_kernel(tm_count, steps, own, partner, total):
-    bits = tm_count.bit_length() - 1
-    _, time_total, gain, rate = dims_of(steps, tm_count)
-    tm_pos = lax.axis_index("tm")
-    plain = lax.axis_index("rows") % 2 == 0
-    wrap = wrap_weight * rate**time_total
-    after_own, after_partner = bit_is_set(tm_pos, bits - 2), 1.0 - bit_is_set(tm_pos, bits - 1)
-
-    def weights(is_after):
-        is_after = jnp.where(plain, jnp.float32(0.0), is_after)
-        same = jnp.where(is_after > 0.5, jnp.float32(wrap), jnp.float32(1.0))
-        return same, is_after * (wrap * time_total * gain)
-
-    (same_own, mixed_own), (same_partner, mixed_partner) = weights(after_own), weights(after_partner)
-    deep = (own.shape[0] - tile) // 2
-    of_y, of_z, halo = pl.ds(0, deep), pl.ds(deep, deep), pl.ds(2 * deep, tile)
-    total[of_y, :] = same_own * own[of_y, :] + same_partner * partner[of_y, :]
-    total[of_z, :] = (same_own * own[of_z, :] + same_partner * partner[of_z, :]) + (
-        mixed_own * own[of_y, :] + mixed_partner * partner[of_y, :]
-    )
-    mixed = mixed_own * own[halo, :] + mixed_partner * partner[halo, :]
-    sub = lax.broadcasted_iota(jnp.int32, mixed.shape, 0)
-    mixed = jnp.where(sub < 4, pltpu.roll(mixed, 2, 0), pltpu.roll(mixed, tile - 2, 0))
+    sub = lax.broadcasted_iota(jnp.int32, (tile, half), 0)
+    result = None
+    for at, (value, side) in enumerate(((halo_y, 0), (halo_y, 1), (halo_z, 0), (halo_z, 1))):
+        value = value[:, side * half : (side + 1) * half]
+        mirror = tile - 2 - at + 2 * side
+        after = pltpu.roll(value, at, 0) if at else value
+        before = pltpu.roll(value, mirror + 1, 0) if mirror < tile - 1 else value
+        result = after if result is None else jnp.where(sub == at, after, result)
+        result = jnp.where(sub == mirror, before, result)
+    total[pl.ds(4 * rows, tile), :] = result
+
+
+def weigh_kernel(tm_count, steps, pair, *rest):
+    partners, total = rest[:-1], rest[-1]
+    weights = weights_of(tm_count, steps)
+    deep = (pair.shape[0] - tile) // 2
+    of_y, of_z, of_halo = pl.ds(0, deep), pl.ds(deep, deep), pl.ds(2 * deep, tile)
+    y, z, halo = pair[of_y, :], pair[of_z, :], pair[of_halo, :]
+    sub = lax.broadcasted_iota(jnp.int32, halo.shape, 0)
     is_z = (sub >= 2) & (sub < tile - 2)
-    total[halo, :] = (same_own * own[halo, :] + same_partner * partner[halo, :]) + jnp.where(is_z, mixed, 0.0)
+    for i, partner in enumerate(partners):
+        same, mixed = weights(i + 1)
+        y = y + same * partner[of_y, :]
+        z = z + same * partner[of_z, :] + mixed * partner[of_y, :]
+        added = partner[of_halo, :]
+        its_y = jnp.where(sub < 4, pltpu.roll(added, 2, 0), pltpu.roll(added, tile - 2, 0))
+        halo = halo + same * added + jnp.where(is_z, mixed * its_y, 0.0)
+    total[of_y, :], total[of_z, :], total[of_halo, :] = y, z, halo
 
 
 def split_halo(packed):
@@ -299,7 +307,7 @@
 
     def is_upper(level):
         upper = [bit_is_set(tm_pos, bit_of(level, bits, parity)) for parity in range(2)]
-        if swaps_order(bits) and level == bits - 1:
+        if level and level == bits - 1:
             upper[1] = jnp.float32(1.0)
         return jnp.where(odd, upper[1], upper[0])
 
@@ -376,6 +384,16 @@
     in_hbm = pl.BlockSpec(memory_space=pl.ANY)
     params = pltpu.CompilerParams(vmem_limit_bytes=vmem_limit)
     late = pl.CostEstimate(flops=10**10, bytes_accessed=10**8, transcendentals=0)
+    bits = tm_count.bit_length() - 1
+
+    def exchanged(value, level):
+        pairs = [
+            (i * rows_count + r, (i ^ 1 << bit_of(level, bits, r % 2)) * rows_count + r)
+            for i in range(tm_count)
+            for r in range(rows_count)
+        ]
+        return lax.ppermute(value, ("tm", "rows"), pairs)
+
     pack = pltpu.VMEM((slots_of(steps)[1] * tile, columns), f32)
     inside, across = pl.pallas_call(
         pack_kernel,
@@ -408,7 +426,7 @@
         compiler_params=params,
         name="own_carry",
     )(state, source, start, velocity)
-    main_partner = swapped(main, "tm", lambda i: i ^ 1)
+    main_partner = exchanged(main, 0)
 
     edge, own_edge = pl.pallas_call(
         functools.partial(edge_kernel, tm_count),
@@ -419,35 +437,34 @@
         cost_estimate=late,
         name="edge_carry",
     )(state, velocity, inside, across)
-    edge_partner = swapped(edge, "tm", lambda i: i ^ 1)
-
-    partners, bits = [], tm_count.bit_length() - 1
-    so_far = pl.pallas_call(
-        join_kernel,
-        out_shape=pltpu.VMEM((4 * rows + tile, columns // 2), f32),
-        in_specs=[in_vmem] * 4,
-        out_specs=in_vmem,
-        compiler_params=params,
-        name="join_edges",
-    )(main, edge, main_partner, edge_partner)
+    edge_partner = exchanged(edge, 0)
+
+    joined = pltpu.VMEM((4 * rows + tile, columns // 2), f32)
+
+    def pair_sum(is_last):
+        return pl.pallas_call(
+            functools.partial(join_kernel, tm_count, steps, is_last),
+            out_shape=joined,
+            in_specs=[in_vmem] * 4,
+            out_specs=in_vmem,
+            compiler_params=params,
+            name="join_weighted" if is_last else "join_edges",
+        )(main, edge, main_partner, edge_partner)
+
+    partners, so_far = [], pair_sum(False)
     for level in range(1, bits):
-        if level > 1 and level == bits - 1:
+        if level == bits - 1:
             so_far = pl.pallas_call(
                 functools.partial(weigh_kernel, tm_count, steps),
-                out_shape=pltpu.VMEM(so_far.shape, f32),
-                in_specs=[in_vmem] * 2,
+                out_shape=joined,
+                in_specs=[in_vmem] * (1 + len(partners)),
                 out_specs=in_vmem,
                 compiler_params=params,
                 name="weigh_groups",
-            )(so_far, partners[-1])
+            )(pair_sum(True), *partners)
         elif level > 1:
             so_far = so_far + partners[-1]
-        pairs = [
-            (i * rows_count + r, (i ^ 1 << bit_of(level, bits, r % 2)) * rows_count + r)
-            for i in range(tm_count)
-            for r in range(rows_count)
-        ]
-        partners.append(lax.ppermute(so_far, ("tm", "rows"), pairs))
+        partners.append(exchanged(so_far, level))
 
     return pl.pallas_call(
         functools.partial(final_kernel, tm_count),

time: 23 us -> 22.8 us (level)
    ppermute x4 -> x2, starting transfers between devices: 6.31 us -> 3.14 us  [swapped(): lax.ppermute(value, axis, [(i, partner(i)) for i in range(lax.axis_size(a...]
    ppermute x2 -> x4, starting transfers between devices: 4.31 us -> 7.29 us  [exchanged(): return lax.ppermute(value, ('tm', 'rows'), pairs)]
    ppermute x4 -> x2, waiting for transfers between devices: 2.59 us -> 0.01 us  [swapped(): lax.ppermute(value, axis, [(i, partner(i)) for i in range(lax.axis_size(a...]
    ppermute x2 -> x4, waiting for transfers between devices: 7.29 us -> 9.8 us  [exchanged(): return lax.ppermute(value, ('tm', 'rows'), pairs)]
  transfers between devices with their start and end apart: 6 -> 6, of which waited for: 3 -> 3; matrix products, arithmetic and copies ran while one was open for 0% -> 0% of each run, Pallas kernels for 1% -> 2%
where the time goes in v6:
time: 22.8 us; the launch traced here: 22.6 us
  starting transfers between devices  10.4 us (46%)
  waiting for transfers between devices  9.81 us (43%)
  Pallas kernels  2.3 us (10%)
    ppermute x4, waiting for transfers between devices, exchanged(): return lax.ppermute(value, ('tm', 'rows'), pairs)  9.8 us
    ppermute x4, starting transfers between devices, exchanged(): return lax.ppermute(value, ('tm', 'rows'), pairs)  7.29 us
    ppermute x2, starting transfers between devices, swapped(): lax.ppermute(value, axis, [(i, partner(i)) for i in range(lax.axis_size(a...  3.14 us
    pallas_call x1, Pallas kernels, on_device(): pl.pallas_call(pack_kernel, out_shape=[pack, pack], in_specs=[in_hbm] * 4...  0.98 us
    pallas_call x1, Pallas kernels, on_device(): pl.pallas_call(functools.partial(final_kernel, tm_count), out_shape=jax.S...  0.89 us
  transfers between devices with their start and end apart: 6, of which 3 were waited for; matrix products, arithmetic and copies ran while one was open for 0% of the time, Pallas kernels for 2%

profile of v6, /device:TPU:0, one launch (start us, length us, event | category | flops | bytes accessed | tf_op | source)
XLA Modules:
  0.0 22.6 jit_solution(14956807687554032704)
XLA Ops:
  0.0 0.0 copy-start
  0.0 0.0 copy-start.2
  0.0 0.0 copy-start.3
  0.0 0.0 copy-start.1
  0.0 1.0 %pack_edge_rows.1 = (f32[16,512]{1,0:T(8,128)S(1)}, f32[16,512]{1,0:T(8,128)S(1)}) custom-call(f32[2,32,512]{2,1,0:T(8,128)} %state.5, f32[2,32,512]{2,1,0:T(8,128)} %source.3, f32[32,512]{1,0:T(8,128)} %start.3, f32[2,32,512]{2,1,0:T(8,128)} %velocity.7), custom_call_target="tpu_custom_call" | custom-call | tf_op jit(solution)/shard_map/pack_edge_rows/pallas_call | solution.py:398
  1.0 0.5 %collective-permute-start = (f32[16,512]{1,0:T(8,128)S(1)}, f32[16,512]{1,0:T(8,128)S(1)}, u32[]{:S(2)}, u32[]{:S(2)}) collective-permute-start(f32[16,512]{1,0:T(8,128)S(1)} %get-tuple-element.14), channel_id=1, source_target_pairs={{0,1},{1,0},{2,3},{3,2},{4,5},{5,4},{6,7},{7,6},{8,9},{9,8},{10,11... | collective-permute-start | bytes 98312 | tf_op jit(solution)/shard_map/ppermute | solution.py:375
  1.5 2.6 %collective-permute-start.1 = (f32[16,512]{1,0:T(8,128)S(1)}, f32[16,512]{1,0:T(8,128)S(1)}, u32[]{:S(2)}, u32[]{:S(2)}) collective-permute-start(f32[16,512]{1,0:T(8,128)S(1)} %get-tuple-element.15), channel_id=1, source_target_pairs={{0,3},{1,2},{2,1},{3,0},{4,7},{5,6},{6,5},{7,4},{8,11},{9,10},{10,... | collective-permute-start | bytes 98312 | tf_op jit(solution)/shard_map/ppermute | solution.py:375
  4.1 0.0 copy-done
  4.1 0.0 copy-done.2
  4.2 0.0 copy-done.3
  4.2 0.0 copy-done.1
  4.2 0.2 own_carry.1
  4.4 1.6 %collective-permute-start.2 = (f32[64,512]{1,0:T(8,128)S(1)}, f32[64,512]{1,0:T(8,128)S(1)}, u32[]{:S(2)}, u32[]{:S(2)}) collective-permute-start(f32[64,512]{1,0:T(8,128)S(1)} %get-tuple-element.17.main), channel_id=1, source_target_pairs={{0,4},{1,9},{2,6},{3,11},{4,0},{5,13},{6,2},{7,15},{8,12},{9,1},{1... | collective-permute-start | bytes 393224 | tf_op jit(solution)/shard_map/ppermute | solution.py:395
  5.9 0.0 collective-permute-done.inside
  5.9 0.0 collective-permute-done.1.across
  5.9 0.1 edge_carry.1
  6.1 1.6 %collective-permute-start.3 = (f32[8,512]{1,0:T(8,128)S(1)}, f32[8,512]{1,0:T(8,128)S(1)}, u32[]{:S(2)}, u32[]{:S(2)}) collective-permute-start(f32[8,512]{1,0:T(8,128)S(1)} %get-tuple-element.18.edge), channel_id=1, source_target_pairs={{0,4},{1,9},{2,6},{3,11},{4,0},{5,13},{6,2},{7,15},{8,12},{9,1},{1... | collective-permute-start | bytes 49160 | tf_op jit(solution)/shard_map/ppermute | solution.py:395
  7.7 2.2 %collective-permute-done.3.edge_partner = f32[8,512]{1,0:T(8,128)S(1)} collective-permute-done((f32[8,512]{1,0:T(8,128)S(1)}, f32[8,512]{1,0:T(8,128)S(1)}, u32[]{:S(2)}, u32[]{:S(2)}) %collective-permute-start.3) | collective-permute-done | bytes 16416 | tf_op jit(solution)/shard_map/ppermute | solution.py:395
  9.9 0.0 collective-permute-done.2.main_partner
  9.9 1.6 %collective-permute-start.4 = (f32[136,256]{1,0:T(8,128)S(1)}, f32[136,256]{1,0:T(8,128)S(1)}, u32[]{:S(2)}, u32[]{:S(2)}) collective-permute-start(f32[136,256]{1,0:T(8,128)S(1)} %join_edges.1), channel_id=1, source_target_pairs={{0,8},{1,17},{2,10},{3,19},{4,12},{5,21},{6,14},{7,23},{8,0},{9,25... | collective-permute-start | bytes 417800 | tf_op jit(solution)/shard_map/ppermute | solution.py:395
  11.6 0.1 join_weighted.1.pair
  11.6 4.0 %collective-permute-done.4.rest_0_ = f32[136,256]{1,0:T(8,128)S(1)} collective-permute-done((f32[136,256]{1,0:T(8,128)S(1)}, f32[136,256]{1,0:T(8,128)S(1)}, u32[]{:S(2)}, u32[]{:S(2)}) %collective-permute-start.4) | collective-permute-done | bytes 139296 | tf_op jit(solution)/shard_map/ppermute | solution.py:395
  15.7 2.5 %collective-permute-start.5 = (f32[136,256]{1,0:T(8,128)S(1)}, f32[136,256]{1,0:T(8,128)S(1)}, u32[]{:S(2)}, u32[]{:S(2)}) collective-permute-start(f32[136,256]{1,0:T(8,128)S(1)} %weigh_groups.1), channel_id=1, source_target_pairs={{0,16},{1,5},{2,18},{3,7},{4,20},{5,1},{6,22},{7,3},{8,24},{9,13},... | collective-permute-start | bytes 417800 | tf_op jit(solution)/shard_map/ppermute | solution.py:395
  18.2 3.5 %collective-permute-done.5.rest_1_ = f32[136,256]{1,0:T(8,128)S(1)} collective-permute-done((f32[136,256]{1,0:T(8,128)S(1)}, f32[136,256]{1,0:T(8,128)S(1)}, u32[]{:S(2)}, u32[]{:S(2)}) %collective-permute-start.5) | collective-permute-done | bytes 139296 | tf_op jit(solution)/shard_map/ppermute | solution.py:395
  21.7 0.9 %enter_and_couple.1 = f32[2,32,512]{2,1,0:T(8,128)} custom-call(f32[2,32,512]{2,1,0:T(8,128)S(1)} %copy-done, f32[2,32,512]{2,1,0:T(8,128)S(1)} %get-tuple-element.12.own_y, f32[2,32,512]{2,1,0:T(8,128)S(1)} %get-tuple-element.13.own_z, f32[2,8,512]{2,1,0:T(8,128)S(1)} %get-tuple-element.16.own_edge, f32[64,512]{1,0:T(8,128)S(1)} %get-tuple-element.17.main, ...), custom_call_target="tpu_custom_call" | custom-call | tf_op jit(solution)/shard_map/enter_and_couple/pallas_call | solution.py:469
  (2 shorter events, 0.1 us)
Async XLA Ops:
  0.0 4.1 %copy-start = (f32[2,32,512]{2,1,0:T(8,128)S(1)}, f32[2,32,512]{2,1,0:T(8,128)}, u32[]{:S(2)}) copy-start(f32[2,32,512]{2,1,0:T(8,128)} %velocity.7) | copy-start | bytes 393220
  0.0 4.1 %copy-start.2 = (f32[2,32,512]{2,1,0:T(8,128)S(1)}, f32[2,32,512]{2,1,0:T(8,128)}, u32[]{:S(2)}) copy-start(f32[2,32,512]{2,1,0:T(8,128)} %state.5) | copy-start | bytes 393220
  0.0 4.1 %copy-start.3 = (f32[32,512]{1,0:T(8,128)S(1)}, f32[32,512]{1,0:T(8,128)}, u32[]{:S(2)}) copy-start(f32[32,512]{1,0:T(8,128)} %start.3) | copy-start | bytes 196612
  0.0 4.2 %copy-start.1 = (f32[2,32,512]{2,1,0:T(8,128)S(1)}, f32[2,32,512]{2,1,0:T(8,128)}, u32[]{:S(2)}) copy-start(f32[2,32,512]{2,1,0:T(8,128)} %source.3) | copy-start | bytes 393220
  1.0 4.9 %collective-permute-start = (f32[16,512]{1,0:T(8,128)S(1)}, f32[16,512]{1,0:T(8,128)S(1)}, u32[]{:S(2)}, u32[]{:S(2)}) collective-permute-start(f32[16,512]{1,0:T(8,128)S(1)} %get-tuple-element.14), channel_id=1, source_target_pairs={{0,1},{1,0},{2,3},{3,2},{4,5},{5,4},{6,7},{7,6},{8,9},{9,8},{10,11... | collective-permute-start | bytes 98312 | tf_op jit(solution)/shard_map/ppermute | solution.py:375
  1.5 4.4 %collective-permute-start.1 = (f32[16,512]{1,0:T(8,128)S(1)}, f32[16,512]{1,0:T(8,128)S(1)}, u32[]{:S(2)}, u32[]{:S(2)}) collective-permute-start(f32[16,512]{1,0:T(8,128)S(1)} %get-tuple-element.15), channel_id=1, source_target_pairs={{0,3},{1,2},{2,1},{3,0},{4,7},{5,6},{6,5},{7,4},{8,11},{9,10},{10,... | collective-permute-start | bytes 98312 | tf_op jit(solution)/shard_map/ppermute | solution.py:375
  4.4 5.5 %collective-permute-start.2 = (f32[64,512]{1,0:T(8,128)S(1)}, f32[64,512]{1,0:T(8,128)S(1)}, u32[]{:S(2)}, u32[]{:S(2)}) collective-permute-start(f32[64,512]{1,0:T(8,128)S(1)} %get-tuple-element.17.main), channel_id=1, source_target_pairs={{0,4},{1,9},{2,6},{3,11},{4,0},{5,13},{6,2},{7,15},{8,12},{9,1},{1... | collective-permute-start | bytes 393224 | tf_op jit(solution)/shard_map/ppermute | solution.py:395
  6.1 3.8 %collective-permute-start.3 = (f32[8,512]{1,0:T(8,128)S(1)}, f32[8,512]{1,0:T(8,128)S(1)}, u32[]{:S(2)}, u32[]{:S(2)}) collective-permute-start(f32[8,512]{1,0:T(8,128)S(1)} %get-tuple-element.18.edge), channel_id=1, source_target_pairs={{0,4},{1,9},{2,6},{3,11},{4,0},{5,13},{6,2},{7,15},{8,12},{9,1},{1... | collective-permute-start | bytes 49160 | tf_op jit(solution)/shard_map/ppermute | solution.py:395
  9.9 5.7 %collective-permute-start.4 = (f32[136,256]{1,0:T(8,128)S(1)}, f32[136,256]{1,0:T(8,128)S(1)}, u32[]{:S(2)}, u32[]{:S(2)}) collective-permute-start(f32[136,256]{1,0:T(8,128)S(1)} %join_edges.1), channel_id=1, source_target_pairs={{0,8},{1,17},{2,10},{3,19},{4,12},{5,21},{6,14},{7,23},{8,0},{9,25... | collective-permute-start | bytes 417800 | tf_op jit(solution)/shard_map/ppermute | solution.py:395
  15.7 6.0 %collective-permute-start.5 = (f32[136,256]{1,0:T(8,128)S(1)}, f32[136,256]{1,0:T(8,128)S(1)}, u32[]{:S(2)}, u32[]{:S(2)}) collective-permute-start(f32[136,256]{1,0:T(8,128)S(1)} %weigh_groups.1), channel_id=1, source_target_pairs={{0,16},{1,5},{2,18},{3,7},{4,20},{5,1},{6,22},{7,3},{8,24},{9,13},... | collective-permute-start | bytes 417800 | tf_op jit(solution)/shard_map/ppermute | solution.py:395

commit v7 on v6

--- a/solution.py
+++ b/solution.py
@@ -155,7 +155,8 @@
     total[rows : 2 * rows, :] = carry_z
 
 
-def edge_kernel(tm_count, state, velocity, inside, across, total, own_edge):
+def edge_kernel(tm_count, state, velocity, inside, across, main, total, own_edge, main_out):
+    main_out[...] = main[...]
     steps, time_total, gain, rate = dims_of(state.shape[0], tm_count)
     rows, columns = state.shape[1:]
     place, _ = slots_of(steps)
@@ -228,17 +229,21 @@
     return weights
 
 
-def join_kernel(tm_count, steps, is_last, main, edge, main_partner, edge_partner, total):
-    rows, half = main.shape[0] // 2, main.shape[1] // 2
-    sub = lax.broadcasted_iota(jnp.int32, edge.shape, 0)
+def add_kernel(first, second, total):
+    total[...] = first[...] + second[...]
+
+
+def join_kernel(tm_count, steps, *refs):
+    mains, edges, total = refs[: len(refs) // 2], refs[len(refs) // 2 : -1], refs[-1]
+    rows, half = mains[0].shape[0] // 2, mains[0].shape[1] // 2
+    sub = lax.broadcasted_iota(jnp.int32, edges[0].shape, 0)
     weights = weights_of(tm_count, steps)
     sums = None
-    for level, of_main, of_edge in ((None, main, edge), (0, main_partner, edge_partner)):
+    for i, (of_main, of_edge) in enumerate(zip(mains, edges)):
         values = [of_main[pl.ds(0, rows), :], of_main[pl.ds(rows, rows), :], *unpack_edges(sub, of_edge[...])]
-        if is_last:
-            same, mixed = weights(level)
-            for i in range(0, len(values), 2):
-                values[i], values[i + 1] = same * values[i], same * values[i + 1] + mixed * values[i]
+        same, mixed = weights(i - 1 if i else None)
+        for k in range(0, len(values), 2):
+            values[k], values[k + 1] = same * values[k], same * values[k + 1] + mixed * values[k]
         sums = values if sums is None else [a + b for a, b in zip(sums, values)]
     main_y, main_z, halo_y, halo_z, more_y, more_z = sums
     for i, value in enumerate((with_edges(main_y, more_y), with_edges(main_z, more_z))):
@@ -256,24 +261,6 @@
     total[pl.ds(4 * rows, tile), :] = result
 
 
-def weigh_kernel(tm_count, steps, pair, *rest):
-    partners, total = rest[:-1], rest[-1]
-    weights = weights_of(tm_count, steps)
-    deep = (pair.shape[0] - tile) // 2
-    of_y, of_z, of_halo = pl.ds(0, deep), pl.ds(deep, deep), pl.ds(2 * deep, tile)
-    y, z, halo = pair[of_y, :], pair[of_z, :], pair[of_halo, :]
-    sub = lax.broadcasted_iota(jnp.int32, halo.shape, 0)
-    is_z = (sub >= 2) & (sub < tile - 2)
-    for i, partner in enumerate(partners):
-        same, mixed = weights(i + 1)
-        y = y + same * partner[of_y, :]
-        z = z + same * partner[of_z, :] + mixed * partner[of_y, :]
-        added = partner[of_halo, :]
-        its_y = jnp.where(sub < 4, pltpu.roll(added, 2, 0), pltpu.roll(added, tile - 2, 0))
-        halo = halo + same * added + jnp.where(is_z, mixed * its_y, 0.0)
-    total[of_y, :], total[of_z, :], total[of_halo, :] = y, z, halo
-
-
 def split_halo(packed):
     def whole(at):
         value = []
@@ -292,8 +279,10 @@
     return whole(0), whole(2)
 
 
-def final_kernel(tm_count, velocity, own_y, own_z, own_edge, main, edge, main_partner, edge_partner, *rest):
-    partners, out, done, sems = rest[:-3], rest[-3], rest[-2], rest[-1]
+def final_kernel(tm_count, velocity, own_y, own_z, own_edge, *rest):
+    bits = tm_count.bit_length() - 1
+    mains, edges, last = rest[:bits], rest[bits : 2 * bits], rest[2 * bits]
+    out, done, sems = rest[-3:]
     steps, time_total, gain, rate = dims_of(own_y.shape[0], tm_count)
     rows, columns = own_y.shape[1:]
     rows_pos = lax.axis_index("rows")
@@ -303,7 +292,7 @@
     shear = time_total * gain * wrap / (1.0 - wrap) ** 2
     sub = lax.broadcasted_iota(jnp.int32, (tile, columns), 0)
 
-    odd, bits = rows_pos % 2 == 1, tm_count.bit_length() - 1
+    odd = rows_pos % 2 == 1
 
     def is_upper(level):
         upper = [bit_is_set(tm_pos, bit_of(level, bits, parity)) for parity in range(2)]
@@ -314,10 +303,10 @@
     uppers = [is_upper(level) for level in range(bits)]
 
     def sums(own, *others):
-        whole, ahead = own, None
+        whole, ahead = own, jnp.zeros_like(own)
         for upper, value in zip(uppers, others):
             whole = whole + value
-            ahead = upper * value if ahead is None else ahead + upper * value
+            ahead = ahead + upper * value
         return whole, ahead
 
     begins = tm_pos * steps
@@ -332,17 +321,15 @@
     def main_sums(i):
         here = pl.ds(i * rows, rows)
         left, right = pl.ds(2 * i * rows, rows), pl.ds((2 * i + 1) * rows, rows)
-        others = [jnp.concatenate([partner[left, :], partner[right, :]], axis=1) for partner in partners]
-        return sums(main[here, :], main_partner[here, :], *others)
+        return sums(*[part[here, :] for part in mains], jnp.concatenate([last[left, :], last[right, :]], axis=1))
 
     (whole_y, ahead_y), (whole_z, ahead_z) = main_sums(0), main_sums(1)
     enter_y, enter_z = entering(whole_y, whole_z, ahead_y, ahead_z)
-    pair = [unpack_edges(sub, part[...]) for part in (edge, edge_partner)]
-    halos = [part[:2] for part in pair]
-    halos += [split_halo(partner[pl.ds(4 * rows, tile), :]) for partner in partners]
+    tiles = [unpack_edges(sub, part[...]) for part in edges]
+    halos = [part[:2] for part in tiles] + [split_halo(last[pl.ds(4 * rows, tile), :])]
     (whole_y, ahead_y), (whole_z, ahead_z) = [sums(*field) for field in zip(*halos)]
     halo_y, halo_z = entering(whole_y, whole_z, ahead_y, ahead_z)
-    (whole_y, ahead_y), (whole_z, ahead_z) = [sums(*field) for field in zip(*[part[2:] for part in pair])]
+    (whole_y, ahead_y), (whole_z, ahead_z) = [sums(*field) for field in zip(*[part[2:] for part in tiles])]
     more_y, more_z = entering(whole_y, whole_z, ahead_y, ahead_z)
     not_first = jnp.where(rows_pos > 0, jnp.float32(1.0), jnp.float32(0.0))
     not_last = jnp.where(rows_pos < lax.axis_size("rows") - 1, jnp.float32(1.0), jnp.float32(0.0))
@@ -383,7 +370,7 @@
     in_vmem = pl.BlockSpec(memory_space=pltpu.VMEM)
     in_hbm = pl.BlockSpec(memory_space=pl.ANY)
     params = pltpu.CompilerParams(vmem_limit_bytes=vmem_limit)
-    late = pl.CostEstimate(flops=10**10, bytes_accessed=10**8, transcendentals=0)
+    late = pl.CostEstimate(flops=10**10, bytes_accessed=0, transcendentals=0)
     bits = tm_count.bit_length() - 1
 
     def exchanged(value, level):
@@ -426,55 +413,52 @@
         compiler_params=params,
         name="own_carry",
     )(state, source, start, velocity)
-    main_partner = exchanged(main, 0)
-
-    edge, own_edge = pl.pallas_call(
+    mains = [main, exchanged(main, 0)]
+    edge, own_edge, main = pl.pallas_call(
         functools.partial(edge_kernel, tm_count),
-        out_shape=[pltpu.VMEM((tile, columns), f32), pltpu.VMEM((steps, tile, columns), f32)],
-        in_specs=[in_vmem] * 4,
-        out_specs=[in_vmem] * 2,
+        out_shape=[
+            pltpu.VMEM((tile, columns), f32),
+            pltpu.VMEM((steps, tile, columns), f32),
+            pltpu.VMEM((2 * rows, columns), f32),
+        ],
+        in_specs=[in_vmem] * 5,
+        out_specs=[in_vmem] * 3,
         compiler_params=params,
         cost_estimate=late,
         name="edge_carry",
-    )(state, velocity, inside, across)
-    edge_partner = exchanged(edge, 0)
-
-    joined = pltpu.VMEM((4 * rows + tile, columns // 2), f32)
-
-    def pair_sum(is_last):
-        return pl.pallas_call(
-            functools.partial(join_kernel, tm_count, steps, is_last),
-            out_shape=joined,
-            in_specs=[in_vmem] * 4,
+    )(state, velocity, inside, across, main)
+    edges = [edge, exchanged(edge, 0)]
+    for level in range(1, bits - 1):
+        main = main + mains[-1]
+        edge = pl.pallas_call(
+            add_kernel,
+            out_shape=pltpu.VMEM((tile, columns), f32),
+            in_specs=[in_vmem] * 2,
             out_specs=in_vmem,
-            compiler_params=params,
-            name="join_weighted" if is_last else "join_edges",
-        )(main, edge, main_partner, edge_partner)
-
-    partners, so_far = [], pair_sum(False)
-    for level in range(1, bits):
-        if level == bits - 1:
-            so_far = pl.pallas_call(
-                functools.partial(weigh_kernel, tm_count, steps),
-                out_shape=joined,
-                in_specs=[in_vmem] * (1 + len(partners)),
-                out_specs=in_vmem,
-                compiler_params=params,
-                name="weigh_groups",
-            )(pair_sum(True), *partners)
-        elif level > 1:
-            so_far = so_far + partners[-1]
-        partners.append(exchanged(so_far, level))
+            cost_estimate=late,
+            name="add_edges",
+        )(*[pltpu.with_memory_space_constraint(part, pltpu.VMEM) for part in (edge, edges[-1])])
+        mains.append(exchanged(main, level))
+        edges.append(exchanged(edge, level))
+    joined = pl.pallas_call(
+        functools.partial(join_kernel, tm_count, steps),
+        out_shape=pltpu.VMEM((4 * rows + tile, columns // 2), f32),
+        in_specs=[in_vmem] * (2 * bits),
+        out_specs=in_vmem,
+        compiler_params=params,
+        name="join_edges",
+    )(*mains, *edges)
+    last = exchanged(joined, bits - 1)
 
     return pl.pallas_call(
         functools.partial(final_kernel, tm_count),
         out_shape=jax.ShapeDtypeStruct((steps, rows, columns), f32),
-        in_specs=[in_vmem] * (8 + len(partners)),
+        in_specs=[in_vmem] * (5 + 2 * bits),
         out_specs=in_hbm,
         scratch_shapes=[pltpu.VMEM((steps, rows, columns), f32), pltpu.SemaphoreType.DMA((steps,))],
         compiler_params=params,
         name="enter_and_couple",
-    )(velocity, own_y, own_z, own_edge, main, edge, main_partner, edge_partner, *partners)
+    )(velocity, own_y, own_z, own_edge, *mains, *edges, last)
 
 
 def solution(mesh):

time: 22.8 us -> 22.5 us (0.987)
  waiting for transfers between devices: 9.81 us -> 9.05 us
  starting transfers between devices: 10.4 us -> 11 us
    ppermute x4 -> x5, waiting for transfers between devices: 9.8 us -> 9.05 us  [exchanged(): return lax.ppermute(value, ('tm', 'rows'), pairs)]
    ppermute x4 -> x5, starting transfers between devices: 7.29 us -> 7.81 us  [exchanged(): return lax.ppermute(value, ('tm', 'rows'), pairs)]
  transfers between devices with their start and end apart: 6 -> 7, of which waited for: 3 -> 3; matrix products, arithmetic and copies ran while one was open for 0% -> 0% of each run, Pallas kernels for 2% -> 1%
where the time goes in v7:
time: 22.5 us; the launch traced here: 22.4 us
  starting transfers between devices  11 us (49%)
  waiting for transfers between devices  9.05 us (40%)
  Pallas kernels  2.28 us (10%)
    ppermute x5, waiting for transfers between devices, exchanged(): return lax.ppermute(value, ('tm', 'rows'), pairs)  9.05 us
    ppermute x5, starting transfers between devices, exchanged(): return lax.ppermute(value, ('tm', 'rows'), pairs)  7.81 us
    ppermute x2, starting transfers between devices, swapped(): lax.ppermute(value, axis, [(i, partner(i)) for i in range(lax.axis_size(a...  3.14 us
    pallas_call x1, Pallas kernels, on_device(): pl.pallas_call(pack_kernel, out_shape=[pack, pack], in_specs=[in_hbm] * 4...  0.98 us
    pallas_call x1, Pallas kernels, on_device(): pl.pallas_call(functools.partial(final_kernel, tm_count), out_shape=jax.S...  0.9 us
  transfers between devices with their start and end apart: 7, of which 3 were waited for; matrix products, arithmetic and copies ran while one was open for 0% of the time, Pallas kernels for 1%

profile of v7, /device:TPU:0, one launch (start us, length us, event | category | flops | bytes accessed | tf_op | source)
XLA Modules:
  0.0 22.4 jit_solution(5976422201992920215)
XLA Ops:
  0.0 0.0 copy-start
  0.0 0.0 copy-start.2
  0.0 0.0 copy-start.3
  0.0 0.0 copy-start.1
  0.0 1.0 %pack_edge_rows.1 = (f32[16,512]{1,0:T(8,128)S(1)}, f32[16,512]{1,0:T(8,128)S(1)}) custom-call(f32[2,32,512]{2,1,0:T(8,128)} %state.5, f32[2,32,512]{2,1,0:T(8,128)} %source.3, f32[32,512]{1,0:T(8,128)} %start.3, f32[2,32,512]{2,1,0:T(8,128)} %velocity.7), custom_call_target="tpu_custom_call" | custom-call | tf_op jit(solution)/shard_map/pack_edge_rows/pallas_call | solution.py:385
  1.0 0.5 %collective-permute-start = (f32[16,512]{1,0:T(8,128)S(1)}, f32[16,512]{1,0:T(8,128)S(1)}, u32[]{:S(2)}, u32[]{:S(2)}) collective-permute-start(f32[16,512]{1,0:T(8,128)S(1)} %get-tuple-element.15), channel_id=1, source_target_pairs={{0,1},{1,0},{2,3},{3,2},{4,5},{5,4},{6,7},{7,6},{8,9},{9,8},{10,11... | collective-permute-start | bytes 98312 | tf_op jit(solution)/shard_map/ppermute | solution.py:362
  1.5 2.6 %collective-permute-start.1 = (f32[16,512]{1,0:T(8,128)S(1)}, f32[16,512]{1,0:T(8,128)S(1)}, u32[]{:S(2)}, u32[]{:S(2)}) collective-permute-start(f32[16,512]{1,0:T(8,128)S(1)} %get-tuple-element.16), channel_id=1, source_target_pairs={{0,3},{1,2},{2,1},{3,0},{4,7},{5,6},{6,5},{7,4},{8,11},{9,10},{10,... | collective-permute-start | bytes 98312 | tf_op jit(solution)/shard_map/ppermute | solution.py:362
  4.1 0.0 copy-done
  4.1 0.0 copy-done.2
  4.2 0.0 copy-done.3
  4.2 0.0 copy-done.1
  4.2 0.2 own_carry.1
  4.4 1.6 %collective-permute-start.2 = (f32[64,512]{1,0:T(8,128)S(1)}, f32[64,512]{1,0:T(8,128)S(1)}, u32[]{:S(2)}, u32[]{:S(2)}) collective-permute-start(f32[64,512]{1,0:T(8,128)S(1)} %get-tuple-element.17.main.refs_0_.rest_0_), channel_id=1, source_target_pairs={{0,4},{1,9},{2,6},{3,11},{4,0},{5,13},{6,2},{7,15},{8,12},{9,1},{1... | collective-permute-start | bytes 393224 | tf_op jit(solution)/shard_map/ppermute | solution.py:382
  5.9 0.0 collective-permute-done.inside
  5.9 0.0 collective-permute-done.1.across
  5.9 0.1 edge_carry.1
  6.1 1.6 %collective-permute-start.4 = (f32[8,512]{1,0:T(8,128)S(1)}, f32[8,512]{1,0:T(8,128)S(1)}, u32[]{:S(2)}, u32[]{:S(2)}) collective-permute-start(f32[8,512]{1,0:T(8,128)S(1)} %get-tuple-element.20.first.refs_3_.rest_3_), channel_id=1, source_target_pairs={{0,4},{1,9},{2,6},{3,11},{4,0},{5,13},{6,2},{7,15},{8,12},{9,1},{1... | collective-permute-start | bytes 49160 | tf_op jit(solution)/shard_map/ppermute | solution.py:382
  7.7 1.7 %collective-permute-done.2.refs_1_.rest_1_ = f32[64,512]{1,0:T(8,128)S(1)} collective-permute-done((f32[64,512]{1,0:T(8,128)S(1)}, f32[64,512]{1,0:T(8,128)S(1)}, u32[]{:S(2)}, u32[]{:S(2)}) %collective-permute-start.2) | collective-permute-done | bytes 131104 | tf_op jit(solution)/shard_map/ppermute | solution.py:382
  9.4 1.6 %collective-permute-start.3 = (f32[64,512]{1,0:T(8,128)S(1)}, f32[64,512]{1,0:T(8,128)S(1)}, u32[]{:S(2)}, u32[]{:S(2)}) collective-permute-start(f32[64,512]{1,0:T(8,128)S(1)} %add.3), channel_id=1, source_target_pairs={{0,8},{1,17},{2,10},{3,19},{4,12},{5,21},{6,14},{7,23},{8,0},{9,25... | collective-permute-start | bytes 393224 | tf_op jit(solution)/shard_map/ppermute | solution.py:382
  11.1 0.0 collective-permute-done.4.second.refs_4_.rest_4_
  11.1 0.5 %collective-permute-start.5 = (f32[8,512]{1,0:T(8,128)S(1)}, f32[8,512]{1,0:T(8,128)S(1)}, u32[]{:S(2)}, u32[]{:S(2)}) collective-permute-start(f32[8,512]{1,0:T(8,128)S(1)} %add_edges.1), channel_id=1, source_target_pairs={{0,8},{1,17},{2,10},{3,19},{4,12},{5,21},{6,14},{7,23},{8,0},{9,25... | collective-permute-start | bytes 49160 | tf_op jit(solution)/shard_map/ppermute | solution.py:382
  11.6 3.8 %collective-permute-done.5.refs_5_.rest_5_ = f32[8,512]{1,0:T(8,128)S(1)} collective-permute-done((f32[8,512]{1,0:T(8,128)S(1)}, f32[8,512]{1,0:T(8,128)S(1)}, u32[]{:S(2)}, u32[]{:S(2)}) %collective-permute-start.5) | collective-permute-done | bytes 16416 | tf_op jit(solution)/shard_map/ppermute | solution.py:382
  15.3 0.0 collective-permute-done.3.refs_2_.rest_2_
  15.3 0.1 join_edges.1
  15.4 2.5 %collective-permute-start.6 = (f32[136,256]{1,0:T(8,128)S(1)}, f32[136,256]{1,0:T(8,128)S(1)}, u32[]{:S(2)}, u32[]{:S(2)}) collective-permute-start(f32[136,256]{1,0:T(8,128)S(1)} %join_edges.1), channel_id=1, source_target_pairs={{0,16},{1,5},{2,18},{3,7},{4,20},{5,1},{6,22},{7,3},{8,24},{9,13},... | collective-permute-start | bytes 417800 | tf_op jit(solution)/shard_map/ppermute | solution.py:382
  17.9 3.5 %collective-permute-done.6.rest_6_ = f32[136,256]{1,0:T(8,128)S(1)} collective-permute-done((f32[136,256]{1,0:T(8,128)S(1)}, f32[136,256]{1,0:T(8,128)S(1)}, u32[]{:S(2)}, u32[]{:S(2)}) %collective-permute-start.6) | collective-permute-done | bytes 139296 | tf_op jit(solution)/shard_map/ppermute | solution.py:382
  21.5 0.9 %enter_and_couple.1 = f32[2,32,512]{2,1,0:T(8,128)} custom-call(f32[2,32,512]{2,1,0:T(8,128)S(1)} %copy-done, f32[2,32,512]{2,1,0:T(8,128)S(1)} %get-tuple-element.13.own_y, f32[2,32,512]{2,1,0:T(8,128)S(1)} %get-tuple-element.14.own_z, f32[2,8,512]{2,1,0:T(8,128)S(1)} %get-tuple-element.18.own_edge, f32[64,512]{1,0:T(8,128)S(1)} %get-tuple-element.17.main.refs_0_.rest_0_, ...), custom_call_target="tpu_custom_call" | custom-call | tf_op jit(solution)/shard_map/enter_and_couple/pallas_call | solution.py:453
  (2 shorter events, 0.0 us)
Async XLA Ops:
  0.0 4.1 %copy-start = (f32[2,32,512]{2,1,0:T(8,128)S(1)}, f32[2,32,512]{2,1,0:T(8,128)}, u32[]{:S(2)}) copy-start(f32[2,32,512]{2,1,0:T(8,128)} %velocity.7) | copy-start | bytes 393220
  0.0 4.1 %copy-start.2 = (f32[2,32,512]{2,1,0:T(8,128)S(1)}, f32[2,32,512]{2,1,0:T(8,128)}, u32[]{:S(2)}) copy-start(f32[2,32,512]{2,1,0:T(8,128)} %state.5) | copy-start | bytes 393220
  0.0 4.1 %copy-start.3 = (f32[32,512]{1,0:T(8,128)S(1)}, f32[32,512]{1,0:T(8,128)}, u32[]{:S(2)}) copy-start(f32[32,512]{1,0:T(8,128)} %start.3) | copy-start | bytes 196612
  0.0 4.2 %copy-start.1 = (f32[2,32,512]{2,1,0:T(8,128)S(1)}, f32[2,32,512]{2,1,0:T(8,128)}, u32[]{:S(2)}) copy-start(f32[2,32,512]{2,1,0:T(8,128)} %source.3) | copy-start | bytes 393220
  1.0 4.9 %collective-permute-start = (f32[16,512]{1,0:T(8,128)S(1)}, f32[16,512]{1,0:T(8,128)S(1)}, u32[]{:S(2)}, u32[]{:S(2)}) collective-permute-start(f32[16,512]{1,0:T(8,128)S(1)} %get-tuple-element.15), channel_id=1, source_target_pairs={{0,1},{1,0},{2,3},{3,2},{4,5},{5,4},{6,7},{7,6},{8,9},{9,8},{10,11... | collective-permute-start | bytes 98312 | tf_op jit(solution)/shard_map/ppermute | solution.py:362
  1.5 4.4 %collective-permute-start.1 = (f32[16,512]{1,0:T(8,128)S(1)}, f32[16,512]{1,0:T(8,128)S(1)}, u32[]{:S(2)}, u32[]{:S(2)}) collective-permute-start(f32[16,512]{1,0:T(8,128)S(1)} %get-tuple-element.16), channel_id=1, source_target_pairs={{0,3},{1,2},{2,1},{3,0},{4,7},{5,6},{6,5},{7,4},{8,11},{9,10},{10,... | collective-permute-start | bytes 98312 | tf_op jit(solution)/shard_map/ppermute | solution.py:362
  4.4 5.0 %collective-permute-start.2 = (f32[64,512]{1,0:T(8,128)S(1)}, f32[64,512]{1,0:T(8,128)S(1)}, u32[]{:S(2)}, u32[]{:S(2)}) collective-permute-start(f32[64,512]{1,0:T(8,128)S(1)} %get-tuple-element.17.main.refs_0_.rest_0_), channel_id=1, source_target_pairs={{0,4},{1,9},{2,6},{3,11},{4,0},{5,13},{6,2},{7,15},{8,12},{9,1},{1... | collective-permute-start | bytes 393224 | tf_op jit(solution)/shard_map/ppermute | solution.py:382
  6.1 5.0 %collective-permute-start.4 = (f32[8,512]{1,0:T(8,128)S(1)}, f32[8,512]{1,0:T(8,128)S(1)}, u32[]{:S(2)}, u32[]{:S(2)}) collective-permute-start(f32[8,512]{1,0:T(8,128)S(1)} %get-tuple-element.20.first.refs_3_.rest_3_), channel_id=1, source_target_pairs={{0,4},{1,9},{2,6},{3,11},{4,0},{5,13},{6,2},{7,15},{8,12},{9,1},{1... | collective-permute-start | bytes 49160 | tf_op jit(solution)/shard_map/ppermute | solution.py:382
  9.4 5.9 %collective-permute-start.3 = (f32[64,512]{1,0:T(8,128)S(1)}, f32[64,512]{1,0:T(8,128)S(1)}, u32[]{:S(2)}, u32[]{:S(2)}) collective-permute-start(f32[64,512]{1,0:T(8,128)S(1)} %add.3), channel_id=1, source_target_pairs={{0,8},{1,17},{2,10},{3,19},{4,12},{5,21},{6,14},{7,23},{8,0},{9,25... | collective-permute-start | bytes 393224 | tf_op jit(solution)/shard_map/ppermute | solution.py:382
  11.1 4.3 %collective-permute-start.5 = (f32[8,512]{1,0:T(8,128)S(1)}, f32[8,512]{1,0:T(8,128)S(1)}, u32[]{:S(2)}, u32[]{:S(2)}) collective-permute-start(f32[8,512]{1,0:T(8,128)S(1)} %add_edges.1), channel_id=1, source_target_pairs={{0,8},{1,17},{2,10},{3,19},{4,12},{5,21},{6,14},{7,23},{8,0},{9,25... | collective-permute-start | bytes 49160 | tf_op jit(solution)/shard_map/ppermute | solution.py:382
  15.4 6.0 %collective-permute-start.6 = (f32[136,256]{1,0:T(8,128)S(1)}, f32[136,256]{1,0:T(8,128)S(1)}, u32[]{:S(2)}, u32[]{:S(2)}) collective-permute-start(f32[136,256]{1,0:T(8,128)S(1)} %join_edges.1), channel_id=1, source_target_pairs={{0,16},{1,5},{2,18},{3,7},{4,20},{5,1},{6,22},{7,3},{8,24},{9,13},... | collective-permute-start | bytes 417800 | tf_op jit(solution)/shard_map/ppermute | solution.py:382

commit v8 on v7

--- a/solution.py
+++ b/solution.py
@@ -233,18 +233,35 @@
     total[...] = first[...] + second[...]
 
 
-def join_kernel(tm_count, steps, *refs):
-    mains, edges, total = refs[: len(refs) // 2], refs[len(refs) // 2 : -1], refs[-1]
-    rows, half = mains[0].shape[0] // 2, mains[0].shape[1] // 2
-    sub = lax.broadcasted_iota(jnp.int32, edges[0].shape, 0)
+def weighted(sub, weights, of_main, of_edge):
+    rows = of_main.shape[0] // 2
+    values = [of_main[pl.ds(0, rows), :], of_main[pl.ds(rows, rows), :], *unpack_edges(sub, of_edge[...])]
+    same, mixed = weights
+    for k in range(0, len(values), 2):
+        values[k], values[k + 1] = same * values[k], same * values[k + 1] + mixed * values[k]
+    return values
+
+
+def gather_kernel(tm_count, steps, *refs):
+    count = len(refs) // 2 - 1
+    mains, edges, main_out, edge_out = refs[:count], refs[count : 2 * count], refs[-2], refs[-1]
+    rows = main_out.shape[0] // 2
+    sub = lax.broadcasted_iota(jnp.int32, edge_out.shape, 0)
     weights = weights_of(tm_count, steps)
     sums = None
-    for i, (of_main, of_edge) in enumerate(zip(mains, edges)):
-        values = [of_main[pl.ds(0, rows), :], of_main[pl.ds(rows, rows), :], *unpack_edges(sub, of_edge[...])]
-        same, mixed = weights(i - 1 if i else None)
-        for k in range(0, len(values), 2):
-            values[k], values[k + 1] = same * values[k], same * values[k + 1] + mixed * values[k]
+    for i, parts in enumerate(zip(mains, edges)):
+        values = weighted(sub, weights(i - 1 if i else None), *parts)
         sums = values if sums is None else [a + b for a, b in zip(sums, values)]
+    main_out[pl.ds(0, rows), :], main_out[pl.ds(rows, rows), :] = sums[:2]
+    edge_out[...] = pack_edges(sub, *sums[2:])
+
+
+def join_kernel(tm_count, steps, level, main, edge, main_partner, edge_partner, total):
+    rows, half = main.shape[0] // 2, main.shape[1] // 2
+    sub = lax.broadcasted_iota(jnp.int32, edge.shape, 0)
+    gathered = [main[pl.ds(0, rows), :], main[pl.ds(rows, rows), :], *unpack_edges(sub, edge[...])]
+    values = weighted(sub, weights_of(tm_count, steps)(level), main_partner, edge_partner)
+    sums = [a + b for a, b in zip(gathered, values)]
     main_y, main_z, halo_y, halo_z, more_y, more_z = sums
     for i, value in enumerate((with_edges(main_y, more_y), with_edges(main_z, more_z))):
         for side in range(2):
@@ -279,28 +296,53 @@
     return whole(0), whole(2)
 
 
-def final_kernel(tm_count, velocity, own_y, own_z, own_edge, *rest):
-    bits = tm_count.bit_length() - 1
-    mains, edges, last = rest[:bits], rest[bits : 2 * bits], rest[2 * bits]
-    out, done, sems = rest[-3:]
-    steps, time_total, gain, rate = dims_of(own_y.shape[0], tm_count)
-    rows, columns = own_y.shape[1:]
-    rows_pos = lax.axis_index("rows")
-    tm_pos = lax.axis_index("tm")
-    wrap = wrap_weight * rate**time_total
-    turn = wrap / (1.0 - wrap)
-    shear = time_total * gain * wrap / (1.0 - wrap) ** 2
+class Entering:
+    def __init__(self, tm_count, steps):
+        self.bits = tm_count.bit_length() - 1
+        _, self.time_total, self.gain, self.rate = dims_of(steps, tm_count)
+        self.tm_pos, self.rows_pos = lax.axis_index("tm"), lax.axis_index("rows")
+        wrap = wrap_weight * self.rate**self.time_total
+        self.turn = wrap / (1.0 - wrap)
+        self.shear = self.time_total * self.gain * wrap / (1.0 - wrap) ** 2
+        begins = self.tm_pos * steps
+        self.front_rate = power_of(self.rate, begins, self.time_total)
+        self.front_shear = begins.astype(jnp.float32) * self.gain
+
+    def is_upper(self, level):
+        upper = [bit_is_set(self.tm_pos, bit_of(level, self.bits, parity)) for parity in range(2)]
+        if level and level == self.bits - 1:
+            upper[1] = jnp.float32(1.0)
+        return jnp.where(self.rows_pos % 2 == 1, upper[1], upper[0])
+
+    def fields(self, whole_y, whole_z, ahead_y, ahead_z):
+        enter_y = self.front_rate * (ahead_y + self.turn * whole_y)
+        enter_z = self.front_rate * (ahead_z + self.turn * whole_z + self.shear * whole_y)
+        return enter_y, enter_z + self.front_shear * enter_y
+
+    def halo_mask(self, sub):
+        not_first = jnp.where(self.rows_pos > 0, jnp.float32(1.0), jnp.float32(0.0))
+        not_last = jnp.where(self.rows_pos < lax.axis_size("rows") - 1, jnp.float32(1.0), jnp.float32(0.0))
+        return jnp.where(sub < 4, not_last, not_first)
+
+
+def off_diagonal(value, outside, velocity):
+    rows = value.shape[0]
+    row = lax.broadcasted_iota(jnp.int32, value.shape, 0)
+    above = jnp.where(row == 0, outside[tile - 1 :], pltpu.roll(value, 1, 0))
+    below = jnp.where(row == rows - 1, outside[:1], pltpu.roll(value, rows - 1, 0))
+    left, right = sides(value)
+    return -diffusion * (above + below + left + right) + 0.5 * (
+        velocity[0] * (right - left) + velocity[1] * (below - above)
+    )
+
+
+def base_kernel(tm_count, velocity, own_y, own_z, own_edge, *rest):
+    steps, rows, columns = own_y.shape
+    entering = Entering(tm_count, steps)
+    bits, gain, rate = entering.bits, entering.gain, entering.rate
+    mains, edges, base = rest[:bits], rest[bits : 2 * bits], rest[-1]
     sub = lax.broadcasted_iota(jnp.int32, (tile, columns), 0)
-
-    odd = rows_pos % 2 == 1
-
-    def is_upper(level):
-        upper = [bit_is_set(tm_pos, bit_of(level, bits, parity)) for parity in range(2)]
-        if level and level == bits - 1:
-            upper[1] = jnp.float32(1.0)
-        return jnp.where(odd, upper[1], upper[0])
-
-    uppers = [is_upper(level) for level in range(bits)]
+    uppers = [entering.is_upper(level) for level in range(bits - 1)]
 
     def sums(own, *others):
         whole, ahead = own, jnp.zeros_like(own)
@@ -309,34 +351,15 @@
             ahead = ahead + upper * value
         return whole, ahead
 
-    begins = tm_pos * steps
-    front_rate = power_of(rate, begins, time_total)
-    front_shear = begins.astype(jnp.float32) * gain
-
-    def entering(whole_y, whole_z, ahead_y, ahead_z):
-        enter_y = front_rate * (ahead_y + turn * whole_y)
-        enter_z = front_rate * (ahead_z + turn * whole_z + shear * whole_y) + front_shear * enter_y
-        return enter_y, enter_z
-
-    def main_sums(i):
-        here = pl.ds(i * rows, rows)
-        left, right = pl.ds(2 * i * rows, rows), pl.ds((2 * i + 1) * rows, rows)
-        return sums(*[part[here, :] for part in mains], jnp.concatenate([last[left, :], last[right, :]], axis=1))
-
-    (whole_y, ahead_y), (whole_z, ahead_z) = main_sums(0), main_sums(1)
-    enter_y, enter_z = entering(whole_y, whole_z, ahead_y, ahead_z)
+    def fields(parts):
+        (whole_y, ahead_y), (whole_z, ahead_z) = [sums(*field) for field in zip(*parts)]
+        return entering.fields(whole_y, whole_z, ahead_y, ahead_z)
+
+    enter_y, enter_z = fields([(part[pl.ds(0, rows), :], part[pl.ds(rows, rows), :]) for part in mains])
     tiles = [unpack_edges(sub, part[...]) for part in edges]
-    halos = [part[:2] for part in tiles] + [split_halo(last[pl.ds(4 * rows, tile), :])]
-    (whole_y, ahead_y), (whole_z, ahead_z) = [sums(*field) for field in zip(*halos)]
-    halo_y, halo_z = entering(whole_y, whole_z, ahead_y, ahead_z)
-    (whole_y, ahead_y), (whole_z, ahead_z) = [sums(*field) for field in zip(*[part[2:] for part in tiles])]
-    more_y, more_z = entering(whole_y, whole_z, ahead_y, ahead_z)
-    not_first = jnp.where(rows_pos > 0, jnp.float32(1.0), jnp.float32(0.0))
-    not_last = jnp.where(rows_pos < lax.axis_size("rows") - 1, jnp.float32(1.0), jnp.float32(0.0))
-    kept = jnp.where(sub < 4, not_last, not_first)
-    row = lax.broadcasted_iota(jnp.int32, (rows, columns), 0)
-
-    copies = []
+    halo_y, halo_z = fields([part[:2] for part in tiles])
+    more_y, more_z = fields([part[2:] for part in tiles])
+    kept = entering.halo_mask(sub)
     for j in range(steps):
         decay, lag = rate ** (j + 1), (j + 1) * gain
         _, edge_z, edge_more_y, edge_more_z = unpack_edges(sub, own_edge[j])
@@ -345,14 +368,48 @@
             own_z[j] + decay * (enter_z + lag * enter_y), edge_more_z + decay * (more_z + lag * more_y)
         )
         outside = kept * (edge_z + decay * (halo_z + lag * halo_y))
-        above = jnp.where(row == 0, outside[tile - 1 :], pltpu.roll(z, 1, 0))
-        below = jnp.where(row == rows - 1, outside[:1], pltpu.roll(z, rows - 1, 0))
-        left, right = sides(z)
-        coupled = -diffusion * (above + below + left + right) + 0.5 * (
-            velocity[0] * (right - left) + velocity[1] * (below - above)
-        )
-        done[j] = y - coupled
-        copies.append(pltpu.make_async_copy(done.at[j], out.at[j], sems.at[j]))
+        base[j] = y - off_diagonal(z, outside, velocity)
+
+
+def band_of(rows):
+    return 2 * tile if rows % (2 * tile) == 0 else rows
+
+
+def final_kernel(tm_count, velocity, base, last, out, done, sems):
+    steps, rows, columns = base.shape
+    entering = Entering(tm_count, steps)
+    sub = lax.broadcasted_iota(jnp.int32, (tile, columns), 0)
+    upper = entering.is_upper(entering.bits - 1)
+
+    def field(i):
+        left, right = pl.ds(2 * i * rows, rows), pl.ds((2 * i + 1) * rows, rows)
+        return jnp.concatenate([last[left, :], last[right, :]], axis=1)
+
+    def fields(y, z):
+        return entering.fields(y, z, upper * y, upper * z)
+
+    enter_y, enter_z = fields(field(0), field(1))
+    halo_y, halo_z = fields(*split_halo(last[pl.ds(4 * rows, tile), :]))
+    kept = entering.halo_mask(sub)
+
+    def rows_of(value, halo, at, height):
+        outside = kept * halo
+        before = outside[tile - 1 :] if at == 0 else value[at - 1 : at]
+        after = outside[:1] if at + height == rows else value[at + height : at + height + 1]
+        return value[at : at + height], jnp.where(sub < 4, after, before)
+
+    copies, band = [], band_of(rows)
+    for at in range(0, rows, band):
+        here = pl.ds(at, band)
+        around = [velocity[i, here, :] for i in range(2)]
+        y, beside_y = rows_of(enter_y, halo_y, at, band)
+        z, beside_z = rows_of(enter_z, halo_z, at, band)
+        first = y - off_diagonal(z, beside_z, around)
+        second = off_diagonal(y, beside_y, around)
+        for j in range(steps):
+            decay, lag = entering.rate ** (j + 1), (j + 1) * entering.gain
+            done[j, here, :] = base[j, here, :] + decay * (first - lag * second)
+        copies.append(pltpu.make_async_copy(done.at[:, here, :], out.at[:, here, :], sems.at[at // band]))
         copies[-1].start()
     for copy in copies:
         copy.wait()
@@ -440,25 +497,42 @@
         )(*[pltpu.with_memory_space_constraint(part, pltpu.VMEM) for part in (edge, edges[-1])])
         mains.append(exchanged(main, level))
         edges.append(exchanged(edge, level))
+    gathered = pl.pallas_call(
+        functools.partial(gather_kernel, tm_count, steps),
+        out_shape=[pltpu.VMEM((2 * rows, columns), f32), pltpu.VMEM((tile, columns), f32)],
+        in_specs=[in_vmem] * (2 * bits - 2),
+        out_specs=[in_vmem] * 2,
+        compiler_params=params,
+        name="gather_groups",
+    )(*mains[:-1], *edges[:-1])
     joined = pl.pallas_call(
-        functools.partial(join_kernel, tm_count, steps),
+        functools.partial(join_kernel, tm_count, steps, bits - 2),
         out_shape=pltpu.VMEM((4 * rows + tile, columns // 2), f32),
-        in_specs=[in_vmem] * (2 * bits),
+        in_specs=[in_vmem] * 4,
         out_specs=in_vmem,
         compiler_params=params,
         name="join_edges",
-    )(*mains, *edges)
+    )(*gathered, mains[-1], edges[-1])
     last = exchanged(joined, bits - 1)
+
+    base = pl.pallas_call(
+        functools.partial(base_kernel, tm_count),
+        out_shape=pltpu.VMEM((steps, rows, columns), f32),
+        in_specs=[in_vmem] * (4 + 2 * bits),
+        out_specs=in_vmem,
+        compiler_params=params,
+        name="all_but_last",
+    )(velocity, own_y, own_z, own_edge, *mains, *edges)
 
     return pl.pallas_call(
         functools.partial(final_kernel, tm_count),
         out_shape=jax.ShapeDtypeStruct((steps, rows, columns), f32),
-        in_specs=[in_vmem] * (5 + 2 * bits),
+        in_specs=[in_vmem] * 3,
         out_specs=in_hbm,
-        scratch_shapes=[pltpu.VMEM((steps, rows, columns), f32), pltpu.SemaphoreType.DMA((steps,))],
-        compiler_params=params,
-        name="enter_and_couple",
-    )(velocity, own_y, own_z, own_edge, *mains, *edges, last)
+        scratch_shapes=[pltpu.VMEM((steps, rows, columns), f32), pltpu.SemaphoreType.DMA((rows // band_of(rows),))],
+        compiler_params=params,
+        name="add_last",
+    )(velocity, base, last)
 
 
 def solution(mesh):

time: 22.5 us -> 22.4 us (level)
  waiting for transfers between devices: 9.05 us -> 8.75 us
    ppermute x5, waiting for transfers between devices: 9.05 us -> 8.75 us  [exchanged(): return lax.ppermute(value, ('tm', 'rows'), pairs)]
    pallas_call x1 -> x3, Pallas kernels: 0.08 us -> 0.34 us  [the longest x1 0.24 us: on_device(): pl.pallas_call(functools.partial(base_kernel, tm_count), out_shape=pltpu....]
  transfers between devices with their start and end apart: 7 -> 7, of which waited for: 3 -> 3; matrix products, arithmetic and copies ran while one was open for 0% -> 0% of each run, Pallas kernels for 1% -> 3%
where the time goes in v8:
time: 22.4 us; the launch traced here: 22.2 us
  starting transfers between devices  11 us (49%)
  waiting for transfers between devices  8.75 us (39%)
  Pallas kernels  2.45 us (11%)
    ppermute x5, waiting for transfers between devices, exchanged(): return lax.ppermute(value, ('tm', 'rows'), pairs)  8.75 us
    ppermute x5, starting transfers between devices, exchanged(): return lax.ppermute(value, ('tm', 'rows'), pairs)  7.81 us
    ppermute x2, starting transfers between devices, swapped(): lax.ppermute(value, axis, [(i, partner(i)) for i in range(lax.axis_size(a...  3.14 us
    pallas_call x1, Pallas kernels, on_device(): pl.pallas_call(pack_kernel, out_shape=[pack, pack], in_specs=[in_hbm] * 4...  0.98 us
    pallas_call x1, Pallas kernels, on_device(): pl.pallas_call(functools.partial(final_kernel, tm_count), out_shape=jax.S...  0.82 us
  transfers between devices with their start and end apart: 7, of which 3 were waited for; matrix products, arithmetic and copies ran while one was open for 0% of the time, Pallas kernels for 3%

profile of v8, /device:TPU:0, one launch (start us, length us, event | category | flops | bytes accessed | tf_op | source)
XLA Modules:
  0.0 22.2 jit_solution(16405336619509810827)
XLA Ops:
  0.0 0.0 copy-start
  0.0 0.0 copy-start.2
  0.0 0.0 copy-start.1
  0.0 0.0 copy-start.3
  0.0 1.0 %pack_edge_rows.1 = (f32[16,512]{1,0:T(8,128)S(1)}, f32[16,512]{1,0:T(8,128)S(1)}) custom-call(f32[2,32,512]{2,1,0:T(8,128)} %state.5, f32[2,32,512]{2,1,0:T(8,128)} %source.3, f32[32,512]{1,0:T(8,128)} %start.3, f32[2,32,512]{2,1,0:T(8,128)} %velocity.9), custom_call_target="tpu_custom_call" | custom-call | tf_op jit(solution)/shard_map/pack_edge_rows/pallas_call | solution.py:442
  1.0 0.5 %collective-permute-start = (f32[16,512]{1,0:T(8,128)S(1)}, f32[16,512]{1,0:T(8,128)S(1)}, u32[]{:S(2)}, u32[]{:S(2)}) collective-permute-start(f32[16,512]{1,0:T(8,128)S(1)} %get-tuple-element.17), channel_id=1, source_target_pairs={{0,1},{1,0},{2,3},{3,2},{4,5},{5,4},{6,7},{7,6},{8,9},{9,8},{10,11... | collective-permute-start | bytes 98312 | tf_op jit(solution)/shard_map/ppermute | solution.py:419
  1.5 2.6 %collective-permute-start.1 = (f32[16,512]{1,0:T(8,128)S(1)}, f32[16,512]{1,0:T(8,128)S(1)}, u32[]{:S(2)}, u32[]{:S(2)}) collective-permute-start(f32[16,512]{1,0:T(8,128)S(1)} %get-tuple-element.18), channel_id=1, source_target_pairs={{0,3},{1,2},{2,1},{3,0},{4,7},{5,6},{6,5},{7,4},{8,11},{9,10},{10,... | collective-permute-start | bytes 98312 | tf_op jit(solution)/shard_map/ppermute | solution.py:419
  4.1 0.0 copy-done
  4.1 0.0 copy-done.2
  4.2 0.0 copy-done.1
  4.2 0.0 copy-done.3
  4.2 0.2 own_carry.1
  4.4 1.6 %collective-permute-start.2 = (f32[64,512]{1,0:T(8,128)S(1)}, f32[64,512]{1,0:T(8,128)S(1)}, u32[]{:S(2)}, u32[]{:S(2)}) collective-permute-start(f32[64,512]{1,0:T(8,128)S(1)} %get-tuple-element.19.main.rest_0_.refs_0_), channel_id=1, source_target_pairs={{0,4},{1,9},{2,6},{3,11},{4,0},{5,13},{6,2},{7,15},{8,12},{9,1},{1... | collective-permute-start | bytes 393224 | tf_op jit(solution)/shard_map/ppermute | solution.py:439
  5.9 0.0 collective-permute-done.inside
  5.9 0.0 collective-permute-done.1.across
  5.9 0.1 edge_carry.1
  6.1 1.6 %collective-permute-start.4 = (f32[8,512]{1,0:T(8,128)S(1)}, f32[8,512]{1,0:T(8,128)S(1)}, u32[]{:S(2)}, u32[]{:S(2)}) collective-permute-start(f32[8,512]{1,0:T(8,128)S(1)} %get-tuple-element.22.first.rest_3_.refs_2_), channel_id=1, source_target_pairs={{0,4},{1,9},{2,6},{3,11},{4,0},{5,13},{6,2},{7,15},{8,12},{9,1},{1... | collective-permute-start | bytes 49160 | tf_op jit(solution)/shard_map/ppermute | solution.py:439
  7.7 1.7 %collective-permute-done.2.rest_1_.refs_1_ = f32[64,512]{1,0:T(8,128)S(1)} collective-permute-done((f32[64,512]{1,0:T(8,128)S(1)}, f32[64,512]{1,0:T(8,128)S(1)}, u32[]{:S(2)}, u32[]{:S(2)}) %collective-permute-start.2) | collective-permute-done | bytes 131104 | tf_op jit(solution)/shard_map/ppermute | solution.py:439
  9.4 1.6 %collective-permute-start.3 = (f32[64,512]{1,0:T(8,128)S(1)}, f32[64,512]{1,0:T(8,128)S(1)}, u32[]{:S(2)}, u32[]{:S(2)}) collective-permute-start(f32[64,512]{1,0:T(8,128)S(1)} %add.3), channel_id=1, source_target_pairs={{0,8},{1,17},{2,10},{3,19},{4,12},{5,21},{6,14},{7,23},{8,0},{9,25... | collective-permute-start | bytes 393224 | tf_op jit(solution)/shard_map/ppermute | solution.py:439
  11.1 0.0 collective-permute-done.4.second.rest_4_.refs_3_
  11.1 0.5 %collective-permute-start.5 = (f32[8,512]{1,0:T(8,128)S(1)}, f32[8,512]{1,0:T(8,128)S(1)}, u32[]{:S(2)}, u32[]{:S(2)}) collective-permute-start(f32[8,512]{1,0:T(8,128)S(1)} %add_edges.1), channel_id=1, source_target_pairs={{0,8},{1,17},{2,10},{3,19},{4,12},{5,21},{6,14},{7,23},{8,0},{9,25... | collective-permute-start | bytes 49160 | tf_op jit(solution)/shard_map/ppermute | solution.py:439
  11.6 0.1 gather_groups.1
  11.6 3.7 %collective-permute-done.5.rest_5_.edge_partner = f32[8,512]{1,0:T(8,128)S(1)} collective-permute-done((f32[8,512]{1,0:T(8,128)S(1)}, f32[8,512]{1,0:T(8,128)S(1)}, u32[]{:S(2)}, u32[]{:S(2)}) %collective-permute-start.5) | collective-permute-done | bytes 16416 | tf_op jit(solution)/shard_map/ppermute | solution.py:439
  15.3 0.0 collective-permute-done.3.rest_2_.main_partner
  15.4 2.5 %collective-permute-start.6 = (f32[136,256]{1,0:T(8,128)S(1)}, f32[136,256]{1,0:T(8,128)S(1)}, u32[]{:S(2)}, u32[]{:S(2)}) collective-permute-start(f32[136,256]{1,0:T(8,128)S(1)} %join_edges.1), channel_id=1, source_target_pairs={{0,16},{1,5},{2,18},{3,7},{4,20},{5,1},{6,22},{7,3},{8,24},{9,13},... | collective-permute-start | bytes 417800 | tf_op jit(solution)/shard_map/ppermute | solution.py:439
  17.9 0.2 %all_but_last.1.base = f32[2,32,512]{2,1,0:T(8,128)S(1)} custom-call(f32[2,32,512]{2,1,0:T(8,128)S(1)} %copy-done, f32[2,32,512]{2,1,0:T(8,128)S(1)} %get-tuple-element.15.own_y, f32[2,32,512]{2,1,0:T(8,128)S(1)} %get-tuple-element.16.own_z, f32[2,8,512]{2,1,0:T(8,128)S(1)} %get-tuple-element.20.own_edge, ...), custom_call_target="tpu_custom_call" | custom-call | tf_op jit(solution)/shard_map/all_but_last/pallas_call | solution.py:518
  18.1 3.3 %collective-permute-done.6.last = f32[136,256]{1,0:T(8,128)S(1)} collective-permute-done((f32[136,256]{1,0:T(8,128)S(1)}, f32[136,256]{1,0:T(8,128)S(1)}, u32[]{:S(2)}, u32[]{:S(2)}) %collective-permute-start.6) | collective-permute-done | bytes 139296 | tf_op jit(solution)/shard_map/ppermute | solution.py:439
  21.4 0.8 %add_last.1 = f32[2,32,512]{2,1,0:T(8,128)} custom-call(f32[2,32,512]{2,1,0:T(8,128)S(1)} %copy-done, f32[2,32,512]{2,1,0:T(8,128)S(1)} %all_but_last.1.base, f32[136,256]{1,0:T(8,128)S(1)} %collective-permute-done.6.last), custom_call_target="tpu_custom_call" | custom-call | tf_op jit(solution)/shard_map/add_last/pallas_call | solution.py:527
  (3 shorter events, 0.1 us)
Async XLA Ops:
  0.0 4.1 %copy-start = (f32[2,32,512]{2,1,0:T(8,128)S(1)}, f32[2,32,512]{2,1,0:T(8,128)}, u32[]{:S(2)}) copy-start(f32[2,32,512]{2,1,0:T(8,128)} %velocity.9) | copy-start | bytes 393220
  0.0 4.1 %copy-start.2 = (f32[2,32,512]{2,1,0:T(8,128)S(1)}, f32[2,32,512]{2,1,0:T(8,128)}, u32[]{:S(2)}) copy-start(f32[2,32,512]{2,1,0:T(8,128)} %state.5) | copy-start | bytes 393220
  0.0 4.1 %copy-start.1 = (f32[2,32,512]{2,1,0:T(8,128)S(1)}, f32[2,32,512]{2,1,0:T(8,128)}, u32[]{:S(2)}) copy-start(f32[2,32,512]{2,1,0:T(8,128)} %source.3) | copy-start | bytes 393220
  0.0 4.2 %copy-start.3 = (f32[32,512]{1,0:T(8,128)S(1)}, f32[32,512]{1,0:T(8,128)}, u32[]{:S(2)}) copy-start(f32[32,512]{1,0:T(8,128)} %start.3) | copy-start | bytes 196612
  1.0 4.9 %collective-permute-start = (f32[16,512]{1,0:T(8,128)S(1)}, f32[16,512]{1,0:T(8,128)S(1)}, u32[]{:S(2)}, u32[]{:S(2)}) collective-permute-start(f32[16,512]{1,0:T(8,128)S(1)} %get-tuple-element.17), channel_id=1, source_target_pairs={{0,1},{1,0},{2,3},{3,2},{4,5},{5,4},{6,7},{7,6},{8,9},{9,8},{10,11... | collective-permute-start | bytes 98312 | tf_op jit(solution)/shard_map/ppermute | solution.py:419
  1.5 4.4 %collective-permute-start.1 = (f32[16,512]{1,0:T(8,128)S(1)}, f32[16,512]{1,0:T(8,128)S(1)}, u32[]{:S(2)}, u32[]{:S(2)}) collective-permute-start(f32[16,512]{1,0:T(8,128)S(1)} %get-tuple-element.18), channel_id=1, source_target_pairs={{0,3},{1,2},{2,1},{3,0},{4,7},{5,6},{6,5},{7,4},{8,11},{9,10},{10,... | collective-permute-start | bytes 98312 | tf_op jit(solution)/shard_map/ppermute | solution.py:419
  4.4 5.0 %collective-permute-start.2 = (f32[64,512]{1,0:T(8,128)S(1)}, f32[64,512]{1,0:T(8,128)S(1)}, u32[]{:S(2)}, u32[]{:S(2)}) collective-permute-start(f32[64,512]{1,0:T(8,128)S(1)} %get-tuple-element.19.main.rest_0_.refs_0_), channel_id=1, source_target_pairs={{0,4},{1,9},{2,6},{3,11},{4,0},{5,13},{6,2},{7,15},{8,12},{9,1},{1... | collective-permute-start | bytes 393224 | tf_op jit(solution)/shard_map/ppermute | solution.py:439
  6.1 5.0 %collective-permute-start.4 = (f32[8,512]{1,0:T(8,128)S(1)}, f32[8,512]{1,0:T(8,128)S(1)}, u32[]{:S(2)}, u32[]{:S(2)}) collective-permute-start(f32[8,512]{1,0:T(8,128)S(1)} %get-tuple-element.22.first.rest_3_.refs_2_), channel_id=1, source_target_pairs={{0,4},{1,9},{2,6},{3,11},{4,0},{5,13},{6,2},{7,15},{8,12},{9,1},{1... | collective-permute-start | bytes 49160 | tf_op jit(solution)/shard_map/ppermute | solution.py:439
  9.4 5.9 %collective-permute-start.3 = (f32[64,512]{1,0:T(8,128)S(1)}, f32[64,512]{1,0:T(8,128)S(1)}, u32[]{:S(2)}, u32[]{:S(2)}) collective-permute-start(f32[64,512]{1,0:T(8,128)S(1)} %add.3), channel_id=1, source_target_pairs={{0,8},{1,17},{2,10},{3,19},{4,12},{5,21},{6,14},{7,23},{8,0},{9,25... | collective-permute-start | bytes 393224 | tf_op jit(solution)/shard_map/ppermute | solution.py:439
  11.1 4.3 %collective-permute-start.5 = (f32[8,512]{1,0:T(8,128)S(1)}, f32[8,512]{1,0:T(8,128)S(1)}, u32[]{:S(2)}, u32[]{:S(2)}) collective-permute-start(f32[8,512]{1,0:T(8,128)S(1)} %add_edges.1), channel_id=1, source_target_pairs={{0,8},{1,17},{2,10},{3,19},{4,12},{5,21},{6,14},{7,23},{8,0},{9,25... | collective-permute-start | bytes 49160 | tf_op jit(solution)/shard_map/ppermute | solution.py:439
  15.4 6.0 %collective-permute-start.6 = (f32[136,256]{1,0:T(8,128)S(1)}, f32[136,256]{1,0:T(8,128)S(1)}, u32[]{:S(2)}, u32[]{:S(2)}) collective-permute-start(f32[136,256]{1,0:T(8,128)S(1)} %join_edges.1), channel_id=1, source_target_pairs={{0,16},{1,5},{2,18},{3,7},{4,20},{5,1},{6,22},{7,3},{8,24},{9,13},... | collective-permute-start | bytes 417800 | tf_op jit(solution)/shard_map/ppermute | solution.py:439

commit v9 on v8

--- a/solution.py
+++ b/solution.py
@@ -35,7 +35,7 @@
 
 
 def bit_of(level, bits, parity):
-    return (level + 1) % bits if parity else level
+    return level if parity else bits - 1 - level
 
 
 def slots_of(steps):
@@ -132,7 +132,8 @@
     return carry_y, carry_z
 
 
-def carry_kernel(tm_count, state, source, start, velocity, total, own_y, own_z):
+def carry_kernel(tm_count, state, source, start, velocity, after, total, own_y, own_z):
+    del after
     steps, time_total, gain, rate = dims_of(state.shape[0], tm_count)
     rows, columns = state.shape[1:]
     row = lax.broadcasted_iota(jnp.int32, (rows, columns), 0)
@@ -213,55 +214,84 @@
     return jnp.concatenate([part for part in parts if part.shape[0]], axis=0)
 
 
-def weights_of(tm_count, steps):
+def weights_of(tm_count, steps, level):
     bits = tm_count.bit_length() - 1
     _, time_total, gain, rate = dims_of(steps, tm_count)
     wrap = wrap_weight * rate**time_total
     tm_pos = lax.axis_index("tm")
-    is_odd = bit_is_set(lax.axis_index("rows"), 0)
-
-    def weights(level):
-        is_after = bit_is_set(tm_pos, 0) if level is None else 1.0 - bit_is_set(tm_pos, bit_of(level, bits, 1))
-        is_after = is_odd * is_after
+    is_even = 1.0 - bit_is_set(lax.axis_index("rows"), 0)
+
+    def weights(source):
+        if source:
+            return None
+        if source is None:
+            is_after = bit_is_set(tm_pos, bit_of(level, bits, 0))
+        else:
+            is_after = 1.0 - bit_is_set(tm_pos, bit_of(0, bits, 0))
+        is_after = is_even * is_after
         same = jnp.where(is_after > 0.5, jnp.float32(wrap), jnp.float32(1.0))
         return same, is_after * (wrap * time_total * gain)
 
     return weights
 
 
-def add_kernel(first, second, total):
-    total[...] = first[...] + second[...]
-
-
-def weighted(sub, weights, of_main, of_edge):
-    rows = of_main.shape[0] // 2
-    values = [of_main[pl.ds(0, rows), :], of_main[pl.ds(rows, rows), :], *unpack_edges(sub, of_edge[...])]
+def weigh(weights, values):
+    if weights is None:
+        return list(values)
     same, mixed = weights
-    for k in range(0, len(values), 2):
-        values[k], values[k + 1] = same * values[k], same * values[k + 1] + mixed * values[k]
-    return values
+    result = []
+    for y, z in zip(values[::2], values[1::2]):
+        result += [same * y, same * z + mixed * y]
+    return result
+
+
+def total_of(parts):
+    total = parts[0]
+    for part in parts[1:]:
+        total = [a + b for a, b in zip(total, part)]
+    return total
+
+
+def hand_on_kernel(value, after, out):
+    del after
+    out[...] = value[...]
+
+
+def main_kernel(tm_count, steps, level, *refs):
+    parts, out = refs[:-1], refs[-1]
+    rows = out.shape[0] // 2
+    weights = weights_of(tm_count, steps, level)
+    of_y, of_z = pl.ds(0, rows), pl.ds(rows, rows)
+    out[of_y, :], out[of_z, :] = total_of(
+        [weigh(weights(i - 1 if i else None), [part[of_y, :], part[of_z, :]]) for i, part in enumerate(parts)]
+    )
+
+
+def tile_kernel(tm_count, steps, level, *refs):
+    parts, out = refs[:-1], refs[-1]
+    weights = weights_of(tm_count, steps, level)
+    sub = lax.broadcasted_iota(jnp.int32, out.shape, 0)
+    values = [weigh(weights(i - 1 if i else None), unpack_edges(sub, part[...])) for i, part in enumerate(parts)]
+    out[...] = pack_edges(sub, *total_of(values))
 
 
 def gather_kernel(tm_count, steps, *refs):
     count = len(refs) // 2 - 1
-    mains, edges, main_out, edge_out = refs[:count], refs[count : 2 * count], refs[-2], refs[-1]
-    rows = main_out.shape[0] // 2
-    sub = lax.broadcasted_iota(jnp.int32, edge_out.shape, 0)
-    weights = weights_of(tm_count, steps)
-    sums = None
-    for i, parts in enumerate(zip(mains, edges)):
-        values = weighted(sub, weights(i - 1 if i else None), *parts)
-        sums = values if sums is None else [a + b for a, b in zip(sums, values)]
-    main_out[pl.ds(0, rows), :], main_out[pl.ds(rows, rows), :] = sums[:2]
-    edge_out[...] = pack_edges(sub, *sums[2:])
-
-
-def join_kernel(tm_count, steps, level, main, edge, main_partner, edge_partner, total):
+    level = tm_count.bit_length() - 2
+    main_kernel(tm_count, steps, level, *refs[:count], refs[-2])
+    tile_kernel(tm_count, steps, level, *refs[count : 2 * count], refs[-1])
+
+
+def join_kernel(tm_count, steps, main, edge, main_partner, edge_partner, total):
     rows, half = main.shape[0] // 2, main.shape[1] // 2
     sub = lax.broadcasted_iota(jnp.int32, edge.shape, 0)
-    gathered = [main[pl.ds(0, rows), :], main[pl.ds(rows, rows), :], *unpack_edges(sub, edge[...])]
-    values = weighted(sub, weights_of(tm_count, steps)(level), main_partner, edge_partner)
-    sums = [a + b for a, b in zip(gathered, values)]
+    level = tm_count.bit_length() - 2
+    parts = [
+        [of_main[pl.ds(0, rows), :], of_main[pl.ds(rows, rows), :], *unpack_edges(sub, of_edge[...])]
+        for of_main, of_edge in ((main, edge), (main_partner, edge_partner))
+    ]
+    parts[1] = weigh(weights_of(tm_count, steps, level)(level - 1), parts[1])
+    sums = total_of(parts)
     main_y, main_z, halo_y, halo_z, more_y, more_z = sums
     for i, value in enumerate((with_edges(main_y, more_y), with_edges(main_z, more_z))):
         for side in range(2):
@@ -310,8 +340,8 @@
 
     def is_upper(self, level):
         upper = [bit_is_set(self.tm_pos, bit_of(level, self.bits, parity)) for parity in range(2)]
-        if level and level == self.bits - 1:
-            upper[1] = jnp.float32(1.0)
+        if level:
+            upper[0] = jnp.float32(1.0)
         return jnp.where(self.rows_pos % 2 == 1, upper[1], upper[0])
 
     def fields(self, whole_y, whole_z, ahead_y, ahead_z):
@@ -441,7 +471,7 @@
     pack = pltpu.VMEM((slots_of(steps)[1] * tile, columns), f32)
     inside, across = pl.pallas_call(
         pack_kernel,
-        out_shape=[pack, pack],
+        out_shape=[pack, pltpu.VMEM(((slots_of(steps)[1] + 1) * tile, columns), f32)],
         in_specs=[in_hbm] * 4,
         out_specs=[in_vmem] * 2,
         scratch_shapes=[
@@ -455,7 +485,6 @@
         name="pack_edge_rows",
     )(*[pltpu.with_memory_space_constraint(a, pltpu.HBM) for a in (state, source, start, velocity)])
 
-    inside = swapped(inside, "rows", lambda i: i ^ 1)
     across = swapped(across, "rows", lambda i: (i + (1 if i % 2 else -1)) % rows_count)
 
     main, own_y, own_z = pl.pallas_call(
@@ -465,12 +494,21 @@
             pltpu.VMEM((steps, rows, columns), f32),
             pltpu.VMEM((steps, rows, columns), f32),
         ],
-        in_specs=[in_vmem] * 4,
+        in_specs=[in_vmem] * 4 + [in_hbm],
         out_specs=[in_vmem] * 3,
         compiler_params=params,
         name="own_carry",
-    )(state, source, start, velocity)
+    )(state, source, start, velocity, inside)
     mains = [main, exchanged(main, 0)]
+    inside = pl.pallas_call(
+        hand_on_kernel,
+        out_shape=pack,
+        in_specs=[in_vmem] * 2,
+        out_specs=in_vmem,
+        cost_estimate=late,
+        name="hand_on",
+    )(*[pltpu.with_memory_space_constraint(a, pltpu.VMEM) for a in (inside, main)])
+    inside = swapped(inside, "rows", lambda i: i ^ 1)
     edge, own_edge, main = pl.pallas_call(
         functools.partial(edge_kernel, tm_count),
         out_shape=[
@@ -481,22 +519,29 @@
         in_specs=[in_vmem] * 5,
         out_specs=[in_vmem] * 3,
         compiler_params=params,
-        cost_estimate=late,
         name="edge_carry",
     )(state, velocity, inside, across, main)
     edges = [edge, exchanged(edge, 0)]
     for level in range(1, bits - 1):
-        main = main + mains[-1]
-        edge = pl.pallas_call(
-            add_kernel,
+        main_payload = pl.pallas_call(
+            functools.partial(main_kernel, tm_count, steps, level),
+            out_shape=pltpu.VMEM((2 * rows, columns), f32),
+            in_specs=[in_vmem] * len(mains),
+            out_specs=in_vmem,
+            compiler_params=params,
+            name="main_payload",
+        )(main, *mains[1:])
+        edge_payload = pl.pallas_call(
+            functools.partial(tile_kernel, tm_count, steps, level),
             out_shape=pltpu.VMEM((tile, columns), f32),
-            in_specs=[in_vmem] * 2,
+            in_specs=[in_vmem] * len(edges),
             out_specs=in_vmem,
+            compiler_params=params,
             cost_estimate=late,
-            name="add_edges",
-        )(*[pltpu.with_memory_space_constraint(part, pltpu.VMEM) for part in (edge, edges[-1])])
-        mains.append(exchanged(main, level))
-        edges.append(exchanged(edge, level))
+            name="edge_payload",
+        )(*[pltpu.with_memory_space_constraint(part, pltpu.VMEM) for part in edges])
+        mains.append(exchanged(main_payload, level))
+        edges.append(exchanged(edge_payload, level))
     gathered = pl.pallas_call(
         functools.partial(gather_kernel, tm_count, steps),
         out_shape=[pltpu.VMEM((2 * rows, columns), f32), pltpu.VMEM((tile, columns), f32)],
@@ -506,7 +551,7 @@
         name="gather_groups",
     )(*mains[:-1], *edges[:-1])
     joined = pl.pallas_call(
-        functools.partial(join_kernel, tm_count, steps, bits - 2),
+        functools.partial(join_kernel, tm_count, steps),
         out_shape=pltpu.VMEM((4 * rows + tile, columns // 2), f32),
         in_specs=[in_vmem] * 4,
         out_specs=in_vmem,

time: 22.4 us -> 22.4 us (level)
    ppermute x2, waiting for transfers between devices: 0.01 us -> 1.21 us  [swapped(): lax.ppermute(value, axis, [(i, partner(i)) for i in range(lax.axis_size(a...]
    ppermute x5, waiting for transfers between devices: 8.75 us -> 7.74 us  [exchanged(): return lax.ppermute(value, ('tm', 'rows'), pairs)]
    ppermute x2, starting transfers between devices: 3.14 us -> 2.46 us  [swapped(): lax.ppermute(value, axis, [(i, partner(i)) for i in range(lax.axis_size(a...]
    ppermute x5, starting transfers between devices: 7.81 us -> 8.3 us  [exchanged(): return lax.ppermute(value, ('tm', 'rows'), pairs)]
    pallas_call x3 -> x5, Pallas kernels: 1.03 us -> 1.08 us  [the longest x1 0.98 us: on_device(): pl.pallas_call(pack_kernel, out_shape=[pack, pltpu.VMEM(((slots_of(steps)...]
  transfers between devices with their start and end apart: 7 -> 7, of which waited for: 3 -> 5; matrix products, arithmetic and copies ran while one was open for 0% -> 0% of each run, Pallas kernels for 3% -> 3%
where the time goes in v9:
time: 22.4 us; the launch traced here: 22.3 us
  starting transfers between devices  10.8 us (48%)
  waiting for transfers between devices  8.95 us (40%)
  Pallas kernels  2.51 us (11%)
    ppermute x5, starting transfers between devices, exchanged(): return lax.ppermute(value, ('tm', 'rows'), pairs)  8.3 us
    ppermute x5, waiting for transfers between devices, exchanged(): return lax.ppermute(value, ('tm', 'rows'), pairs)  7.74 us
    ppermute x2, starting transfers between devices, swapped(): lax.ppermute(value, axis, [(i, partner(i)) for i in range(lax.axis_size(a...  2.46 us
    ppermute x2, waiting for transfers between devices, swapped(): lax.ppermute(value, axis, [(i, partner(i)) for i in range(lax.axis_size(a...  1.21 us
    pallas_call x1, Pallas kernels, on_device(): pl.pallas_call(pack_kernel, out_shape=[pack, pltpu.VMEM(((slots_of(steps)...  0.98 us
    pallas_call x1, Pallas kernels, on_device(): pl.pallas_call(functools.partial(final_kernel, tm_count), out_shape=jax.S...  0.82 us
  transfers between devices with their start and end apart: 7, of which 5 were waited for; matrix products, arithmetic and copies ran while one was open for 0% of the time, Pallas kernels for 3%

profile of v9, /device:TPU:0, one launch (start us, length us, event | category | flops | bytes accessed | tf_op | source)
XLA Modules:
  0.0 22.3 jit_solution(16875854514560893027)
XLA Ops:
  0.0 0.0 copy-start
  0.0 0.0 copy-start.1
  0.0 0.0 copy-start.2
  0.0 0.0 copy-start.3
  0.0 1.0 %pack_edge_rows.1 = (f32[16,512]{1,0:T(8,128)S(1)}, f32[24,512]{1,0:T(8,128)S(1)}) custom-call(f32[2,32,512]{2,1,0:T(8,128)} %state.5, f32[2,32,512]{2,1,0:T(8,128)} %source.3, f32[32,512]{1,0:T(8,128)} %start.3, f32[2,32,512]{2,1,0:T(8,128)} %velocity.9), custom_call_target="tpu_custom_call" | custom-call | tf_op jit(solution)/shard_map/pack_edge_rows/pallas_call | solution.py:472
  1.0 2.5 %collective-permute-start.1 = (f32[24,512]{1,0:T(8,128)S(1)}, f32[24,512]{1,0:T(8,128)S(1)}, u32[]{:S(2)}, u32[]{:S(2)}) collective-permute-start(f32[24,512]{1,0:T(8,128)S(1)} %get-tuple-element.19), channel_id=1, source_target_pairs={{0,3},{1,2},{2,1},{3,0},{4,7},{5,6},{6,5},{7,4},{8,11},{9,10},{10,... | collective-permute-start | bytes 147464 | tf_op jit(solution)/shard_map/ppermute | solution.py:449
  3.5 0.0 copy-done
  3.5 0.0 copy-done.1
  3.5 0.0 copy-done.2
  3.5 0.0 copy-done.3
  3.5 0.2 own_carry.1
  3.7 2.7 %collective-permute-start.2 = (f32[64,512]{1,0:T(8,128)S(1)}, f32[64,512]{1,0:T(8,128)S(1)}, u32[]{:S(2)}, u32[]{:S(2)}) collective-permute-start(f32[64,512]{1,0:T(8,128)S(1)} %get-tuple-element.18.after.main.rest_0_.refs_0_), channel_id=1, source_target_pairs={{0,16},{1,5},{2,18},{3,7},{4,20},{5,1},{6,22},{7,3},{8,24},{9,13},... | collective-permute-start | bytes 393224 | tf_op jit(solution)/shard_map/ppermute | solution.py:469
  6.3 0.0 collective-permute-start
  6.3 1.2 %collective-permute-done.inside = f32[16,512]{1,0:T(8,128)S(1)} collective-permute-done((f32[16,512]{1,0:T(8,128)S(1)}, f32[16,512]{1,0:T(8,128)S(1)}, u32[]{:S(2)}, u32[]{:S(2)}) %collective-permute-start) | collective-permute-done | bytes 32800 | tf_op jit(solution)/shard_map/ppermute | solution.py:449
  7.5 0.0 collective-permute-done.1.across
  7.5 0.1 edge_carry.1
  7.7 1.6 %collective-permute-start.4 = (f32[8,512]{1,0:T(8,128)S(1)}, f32[8,512]{1,0:T(8,128)S(1)}, u32[]{:S(2)}, u32[]{:S(2)}) collective-permute-start(f32[8,512]{1,0:T(8,128)S(1)} %get-tuple-element.22.refs_0_.rest_3_.refs_2_), channel_id=1, source_target_pairs={{0,16},{1,5},{2,18},{3,7},{4,20},{5,1},{6,22},{7,3},{8,24},{9,13},... | collective-permute-start | bytes 49160 | tf_op jit(solution)/shard_map/ppermute | solution.py:469
  9.3 1.7 %collective-permute-done.2.refs_1_.rest_1_ = f32[64,512]{1,0:T(8,128)S(1)} collective-permute-done((f32[64,512]{1,0:T(8,128)S(1)}, f32[64,512]{1,0:T(8,128)S(1)}, u32[]{:S(2)}, u32[]{:S(2)}) %collective-permute-start.2) | collective-permute-done | bytes 131104 | tf_op jit(solution)/shard_map/ppermute | solution.py:469
  11.0 0.8 %collective-permute-start.3 = (f32[64,512]{1,0:T(8,128)S(1)}, f32[64,512]{1,0:T(8,128)S(1)}, u32[]{:S(2)}, u32[]{:S(2)}) collective-permute-start(f32[64,512]{1,0:T(8,128)S(1)} %main_payload.1), channel_id=1, source_target_pairs={{0,8},{1,9},{2,10},{3,11},{4,12},{5,13},{6,14},{7,15},{8,0},{9,1},... | collective-permute-start | bytes 393224 | tf_op jit(solution)/shard_map/ppermute | solution.py:469
  11.8 0.7 %collective-permute-done.4.refs_1_.rest_4_.refs_3_ = f32[8,512]{1,0:T(8,128)S(1)} collective-permute-done((f32[8,512]{1,0:T(8,128)S(1)}, f32[8,512]{1,0:T(8,128)S(1)}, u32[]{:S(2)}, u32[]{:S(2)}) %collective-permute-start.4) | collective-permute-done | bytes 16416 | tf_op jit(solution)/shard_map/ppermute | solution.py:469
  12.5 1.7 %collective-permute-start.5 = (f32[8,512]{1,0:T(8,128)S(1)}, f32[8,512]{1,0:T(8,128)S(1)}, u32[]{:S(2)}, u32[]{:S(2)}) collective-permute-start(f32[8,512]{1,0:T(8,128)S(1)} %edge_payload.1), channel_id=1, source_target_pairs={{0,8},{1,9},{2,10},{3,11},{4,12},{5,13},{6,14},{7,15},{8,0},{9,1},... | collective-permute-start | bytes 49160 | tf_op jit(solution)/shard_map/ppermute | solution.py:469
  14.2 0.1 gather_groups.1
  14.3 2.1 %collective-permute-done.5.rest_5_.edge_partner = f32[8,512]{1,0:T(8,128)S(1)} collective-permute-done((f32[8,512]{1,0:T(8,128)S(1)}, f32[8,512]{1,0:T(8,128)S(1)}, u32[]{:S(2)}, u32[]{:S(2)}) %collective-permute-start.5) | collective-permute-done | bytes 16416 | tf_op jit(solution)/shard_map/ppermute | solution.py:469
  16.3 0.0 collective-permute-done.3.rest_2_.main_partner
  16.4 1.6 %collective-permute-start.6 = (f32[136,256]{1,0:T(8,128)S(1)}, f32[136,256]{1,0:T(8,128)S(1)}, u32[]{:S(2)}, u32[]{:S(2)}) collective-permute-start(f32[136,256]{1,0:T(8,128)S(1)} %join_edges.1), channel_id=1, source_target_pairs={{0,4},{1,17},{2,6},{3,19},{4,0},{5,21},{6,2},{7,23},{8,12},{9,25},... | collective-permute-start | bytes 417800 | tf_op jit(solution)/shard_map/ppermute | solution.py:469
  17.9 0.2 %all_but_last.1.base = f32[2,32,512]{2,1,0:T(8,128)S(1)} custom-call(f32[2,32,512]{2,1,0:T(8,128)S(1)} %copy-done, f32[2,32,512]{2,1,0:T(8,128)S(1)} %get-tuple-element.16.own_y, f32[2,32,512]{2,1,0:T(8,128)S(1)} %get-tuple-element.17.own_z, f32[2,8,512]{2,1,0:T(8,128)S(1)} %get-tuple-element.20.own_edge, ...), custom_call_target="tpu_custom_call" | custom-call | tf_op jit(solution)/shard_map/all_but_last/pallas_call | solution.py:563
  18.2 3.3 %collective-permute-done.6.last = f32[136,256]{1,0:T(8,128)S(1)} collective-permute-done((f32[136,256]{1,0:T(8,128)S(1)}, f32[136,256]{1,0:T(8,128)S(1)}, u32[]{:S(2)}, u32[]{:S(2)}) %collective-permute-start.6) | collective-permute-done | bytes 139296 | tf_op jit(solution)/shard_map/ppermute | solution.py:469
  21.5 0.8 %add_last.1 = f32[2,32,512]{2,1,0:T(8,128)} custom-call(f32[2,32,512]{2,1,0:T(8,128)S(1)} %copy-done, f32[2,32,512]{2,1,0:T(8,128)S(1)} %all_but_last.1.base, f32[136,256]{1,0:T(8,128)S(1)} %collective-permute-done.6.last), custom_call_target="tpu_custom_call" | custom-call | tf_op jit(solution)/shard_map/add_last/pallas_call | solution.py:572
  (4 shorter events, 0.1 us)
Async XLA Ops:
  0.0 3.5 %copy-start = (f32[2,32,512]{2,1,0:T(8,128)S(1)}, f32[2,32,512]{2,1,0:T(8,128)}, u32[]{:S(2)}) copy-start(f32[2,32,512]{2,1,0:T(8,128)} %velocity.9) | copy-start | bytes 393220
  0.0 3.5 %copy-start.1 = (f32[2,32,512]{2,1,0:T(8,128)S(1)}, f32[2,32,512]{2,1,0:T(8,128)}, u32[]{:S(2)}) copy-start(f32[2,32,512]{2,1,0:T(8,128)} %state.5) | copy-start | bytes 393220
  0.0 3.5 %copy-start.2 = (f32[2,32,512]{2,1,0:T(8,128)S(1)}, f32[2,32,512]{2,1,0:T(8,128)}, u32[]{:S(2)}) copy-start(f32[2,32,512]{2,1,0:T(8,128)} %source.3) | copy-start | bytes 393220
  0.0 3.5 %copy-start.3 = (f32[32,512]{1,0:T(8,128)S(1)}, f32[32,512]{1,0:T(8,128)}, u32[]{:S(2)}) copy-start(f32[32,512]{1,0:T(8,128)} %start.3) | copy-start | bytes 196612
  1.0 6.5 %collective-permute-start.1 = (f32[24,512]{1,0:T(8,128)S(1)}, f32[24,512]{1,0:T(8,128)S(1)}, u32[]{:S(2)}, u32[]{:S(2)}) collective-permute-start(f32[24,512]{1,0:T(8,128)S(1)} %get-tuple-element.19), channel_id=1, source_target_pairs={{0,3},{1,2},{2,1},{3,0},{4,7},{5,6},{6,5},{7,4},{8,11},{9,10},{10,... | collective-permute-start | bytes 147464 | tf_op jit(solution)/shard_map/ppermute | solution.py:449
  3.7 7.3 %collective-permute-start.2 = (f32[64,512]{1,0:T(8,128)S(1)}, f32[64,512]{1,0:T(8,128)S(1)}, u32[]{:S(2)}, u32[]{:S(2)}) collective-permute-start(f32[64,512]{1,0:T(8,128)S(1)} %get-tuple-element.18.after.main.rest_0_.refs_0_), channel_id=1, source_target_pairs={{0,16},{1,5},{2,18},{3,7},{4,20},{5,1},{6,22},{7,3},{8,24},{9,13},... | collective-permute-start | bytes 393224 | tf_op jit(solution)/shard_map/ppermute | solution.py:469
  6.3 1.2 %collective-permute-start = (f32[16,512]{1,0:T(8,128)S(1)}, f32[16,512]{1,0:T(8,128)S(1)}, u32[]{:S(2)}, u32[]{:S(2)}) collective-permute-start(f32[16,512]{1,0:T(8,128)S(1)} %hand_on.1), channel_id=1, source_target_pairs={{0,1},{1,0},{2,3},{3,2},{4,5},{5,4},{6,7},{7,6},{8,9},{9,8},{10,11... | collective-permute-start | bytes 98312 | tf_op jit(solution)/shard_map/ppermute | solution.py:449
  7.7 4.8 %collective-permute-start.4 = (f32[8,512]{1,0:T(8,128)S(1)}, f32[8,512]{1,0:T(8,128)S(1)}, u32[]{:S(2)}, u32[]{:S(2)}) collective-permute-start(f32[8,512]{1,0:T(8,128)S(1)} %get-tuple-element.22.refs_0_.rest_3_.refs_2_), channel_id=1, source_target_pairs={{0,16},{1,5},{2,18},{3,7},{4,20},{5,1},{6,22},{7,3},{8,24},{9,13},... | collective-permute-start | bytes 49160 | tf_op jit(solution)/shard_map/ppermute | solution.py:469
  11.0 5.3 %collective-permute-start.3 = (f32[64,512]{1,0:T(8,128)S(1)}, f32[64,512]{1,0:T(8,128)S(1)}, u32[]{:S(2)}, u32[]{:S(2)}) collective-permute-start(f32[64,512]{1,0:T(8,128)S(1)} %main_payload.1), channel_id=1, source_target_pairs={{0,8},{1,9},{2,10},{3,11},{4,12},{5,13},{6,14},{7,15},{8,0},{9,1},... | collective-permute-start | bytes 393224 | tf_op jit(solution)/shard_map/ppermute | solution.py:469
  12.5 3.8 %collective-permute-start.5 = (f32[8,512]{1,0:T(8,128)S(1)}, f32[8,512]{1,0:T(8,128)S(1)}, u32[]{:S(2)}, u32[]{:S(2)}) collective-permute-start(f32[8,512]{1,0:T(8,128)S(1)} %edge_payload.1), channel_id=1, source_target_pairs={{0,8},{1,9},{2,10},{3,11},{4,12},{5,13},{6,14},{7,15},{8,0},{9,1},... | collective-permute-start | bytes 49160 | tf_op jit(solution)/shard_map/ppermute | solution.py:469
  16.4 5.1 %collective-permute-start.6 = (f32[136,256]{1,0:T(8,128)S(1)}, f32[136,256]{1,0:T(8,128)S(1)}, u32[]{:S(2)}, u32[]{:S(2)}) collective-permute-start(f32[136,256]{1,0:T(8,128)S(1)} %join_edges.1), channel_id=1, source_target_pairs={{0,4},{1,17},{2,6},{3,19},{4,0},{5,21},{6,2},{7,23},{8,12},{9,25},... | collective-permute-start | bytes 417800 | tf_op jit(solution)/shard_map/ppermute | solution.py:469

commit v10 on v8

--- a/solution.py
+++ b/solution.py
@@ -89,6 +89,7 @@
         here = pl.ds(t * tile, tile)
         inside[here, :] = jnp.where(odd, top, bottom)
         across[here, :] = jnp.where(odd, bottom, top)
+    across[pl.ds(tiles * tile, tile), :] = jnp.zeros((tile, columns), jnp.float32)
 
 
 def sides(value):
@@ -441,7 +442,7 @@
     pack = pltpu.VMEM((slots_of(steps)[1] * tile, columns), f32)
     inside, across = pl.pallas_call(
         pack_kernel,
-        out_shape=[pack, pack],
+        out_shape=[pack, pltpu.VMEM(((slots_of(steps)[1] + 1) * tile, columns), f32)],
         in_specs=[in_hbm] * 4,
         out_specs=[in_vmem] * 2,
         scratch_shapes=[

time: 22.4 us -> 22.3 us (level)
  waiting for transfers between devices: 8.75 us -> 7.6 us
  starting transfers between devices: 11 us -> 12 us
    ppermute x5, waiting for transfers between devices: 8.75 us -> 7.59 us  [exchanged(): return lax.ppermute(value, ('tm', 'rows'), pairs)]
    ppermute x5, starting transfers between devices: 7.81 us -> 8.91 us  [exchanged(): return lax.ppermute(value, ('tm', 'rows'), pairs)]
where the time goes in v10:
time: 22.3 us; the launch traced here: 22.2 us
  starting transfers between devices  12 us (54%)
  waiting for transfers between devices  7.6 us (34%)
  Pallas kernels  2.45 us (11%)
    ppermute x5, starting transfers between devices, exchanged(): return lax.ppermute(value, ('tm', 'rows'), pairs)  8.91 us
    ppermute x5, waiting for transfers between devices, exchanged(): return lax.ppermute(value, ('tm', 'rows'), pairs)  7.59 us
    ppermute x2, starting transfers between devices, swapped(): lax.ppermute(value, axis, [(i, partner(i)) for i in range(lax.axis_size(a...  3.13 us
    pallas_call x1, Pallas kernels, on_device(): pl.pallas_call(pack_kernel, out_shape=[pack, pltpu.VMEM(((slots_of(steps)...  0.98 us
    pallas_call x1, Pallas kernels, on_device(): pl.pallas_call(functools.partial(final_kernel, tm_count), out_shape=jax.S...  0.82 us
  transfers between devices with their start and end apart: 7, of which 3 were waited for; matrix products, arithmetic and copies ran while one was open for 0% of the time, Pallas kernels for 3%

profile of v10, /device:TPU:0, one launch (start us, length us, event | category | flops | bytes accessed | tf_op | source)
XLA Modules:
  0.0 22.2 jit_solution(17890426903355232643)
XLA Ops:
  0.0 0.0 copy-start
  0.0 0.0 copy-start.2
  0.0 0.0 copy-start.1
  0.0 0.0 copy-start.3
  0.0 1.0 %pack_edge_rows.1 = (f32[16,512]{1,0:T(8,128)S(1)}, f32[24,512]{1,0:T(8,128)S(1)}) custom-call(f32[2,32,512]{2,1,0:T(8,128)} %state.5, f32[2,32,512]{2,1,0:T(8,128)} %source.3, f32[32,512]{1,0:T(8,128)} %start.3, f32[2,32,512]{2,1,0:T(8,128)} %velocity.9), custom_call_target="tpu_custom_call" | custom-call | tf_op jit(solution)/shard_map/pack_edge_rows/pallas_call | solution.py:443
  1.0 2.5 %collective-permute-start.1 = (f32[24,512]{1,0:T(8,128)S(1)}, f32[24,512]{1,0:T(8,128)S(1)}, u32[]{:S(2)}, u32[]{:S(2)}) collective-permute-start(f32[24,512]{1,0:T(8,128)S(1)} %get-tuple-element.18), channel_id=1, source_target_pairs={{0,3},{1,2},{2,1},{3,0},{4,7},{5,6},{6,5},{7,4},{8,11},{9,10},{10,... | collective-permute-start | bytes 147464 | tf_op jit(solution)/shard_map/ppermute | solution.py:420
  3.5 0.7 %collective-permute-start = (f32[16,512]{1,0:T(8,128)S(1)}, f32[16,512]{1,0:T(8,128)S(1)}, u32[]{:S(2)}, u32[]{:S(2)}) collective-permute-start(f32[16,512]{1,0:T(8,128)S(1)} %get-tuple-element.17), channel_id=1, source_target_pairs={{0,1},{1,0},{2,3},{3,2},{4,5},{5,4},{6,7},{7,6},{8,9},{9,8},{10,11... | collective-permute-start | bytes 98312 | tf_op jit(solution)/shard_map/ppermute | solution.py:420
  4.1 0.0 copy-done
  4.1 0.0 copy-done.2
  4.1 0.0 copy-done.1
  4.1 0.0 copy-done.3
  4.1 0.2 own_carry.1
  4.3 1.6 %collective-permute-start.2 = (f32[64,512]{1,0:T(8,128)S(1)}, f32[64,512]{1,0:T(8,128)S(1)}, u32[]{:S(2)}, u32[]{:S(2)}) collective-permute-start(f32[64,512]{1,0:T(8,128)S(1)} %get-tuple-element.19.main.rest_0_.refs_0_), channel_id=1, source_target_pairs={{0,4},{1,9},{2,6},{3,11},{4,0},{5,13},{6,2},{7,15},{8,12},{9,1},{1... | collective-permute-start | bytes 393224 | tf_op jit(solution)/shard_map/ppermute | solution.py:440
  5.9 0.0 collective-permute-done.inside
  5.9 0.0 collective-permute-done.1.across
  5.9 0.1 edge_carry.1
  6.1 2.2 %collective-permute-start.4 = (f32[8,512]{1,0:T(8,128)S(1)}, f32[8,512]{1,0:T(8,128)S(1)}, u32[]{:S(2)}, u32[]{:S(2)}) collective-permute-start(f32[8,512]{1,0:T(8,128)S(1)} %get-tuple-element.22.first.rest_3_.refs_2_), channel_id=1, source_target_pairs={{0,4},{1,9},{2,6},{3,11},{4,0},{5,13},{6,2},{7,15},{8,12},{9,1},{1... | collective-permute-start | bytes 49160 | tf_op jit(solution)/shard_map/ppermute | solution.py:440
  8.2 1.1 %collective-permute-done.2.rest_1_.refs_1_ = f32[64,512]{1,0:T(8,128)S(1)} collective-permute-done((f32[64,512]{1,0:T(8,128)S(1)}, f32[64,512]{1,0:T(8,128)S(1)}, u32[]{:S(2)}, u32[]{:S(2)}) %collective-permute-start.2) | collective-permute-done | bytes 131104 | tf_op jit(solution)/shard_map/ppermute | solution.py:440
  9.4 1.6 %collective-permute-start.3 = (f32[64,512]{1,0:T(8,128)S(1)}, f32[64,512]{1,0:T(8,128)S(1)}, u32[]{:S(2)}, u32[]{:S(2)}) collective-permute-start(f32[64,512]{1,0:T(8,128)S(1)} %add.3), channel_id=1, source_target_pairs={{0,8},{1,17},{2,10},{3,19},{4,12},{5,21},{6,14},{7,23},{8,0},{9,25... | collective-permute-start | bytes 393224 | tf_op jit(solution)/shard_map/ppermute | solution.py:440
  11.0 0.0 collective-permute-done.4.second.rest_4_.refs_3_
  11.0 1.0 %collective-permute-start.5 = (f32[8,512]{1,0:T(8,128)S(1)}, f32[8,512]{1,0:T(8,128)S(1)}, u32[]{:S(2)}, u32[]{:S(2)}) collective-permute-start(f32[8,512]{1,0:T(8,128)S(1)} %add_edges.1), channel_id=1, source_target_pairs={{0,8},{1,17},{2,10},{3,19},{4,12},{5,21},{6,14},{7,23},{8,0},{9,25... | collective-permute-start | bytes 49160 | tf_op jit(solution)/shard_map/ppermute | solution.py:440
  12.0 0.1 gather_groups.1
  12.1 3.2 %collective-permute-done.5.rest_5_.edge_partner = f32[8,512]{1,0:T(8,128)S(1)} collective-permute-done((f32[8,512]{1,0:T(8,128)S(1)}, f32[8,512]{1,0:T(8,128)S(1)}, u32[]{:S(2)}, u32[]{:S(2)}) %collective-permute-start.5) | collective-permute-done | bytes 16416 | tf_op jit(solution)/shard_map/ppermute | solution.py:440
  15.3 0.0 collective-permute-done.3.rest_2_.main_partner
  15.3 2.5 %collective-permute-start.6 = (f32[136,256]{1,0:T(8,128)S(1)}, f32[136,256]{1,0:T(8,128)S(1)}, u32[]{:S(2)}, u32[]{:S(2)}) collective-permute-start(f32[136,256]{1,0:T(8,128)S(1)} %join_edges.1), channel_id=1, source_target_pairs={{0,16},{1,5},{2,18},{3,7},{4,20},{5,1},{6,22},{7,3},{8,24},{9,13},... | collective-permute-start | bytes 417800 | tf_op jit(solution)/shard_map/ppermute | solution.py:440
  17.9 0.2 %all_but_last.1.base = f32[2,32,512]{2,1,0:T(8,128)S(1)} custom-call(f32[2,32,512]{2,1,0:T(8,128)S(1)} %copy-done, f32[2,32,512]{2,1,0:T(8,128)S(1)} %get-tuple-element.15.own_y, f32[2,32,512]{2,1,0:T(8,128)S(1)} %get-tuple-element.16.own_z, f32[2,8,512]{2,1,0:T(8,128)S(1)} %get-tuple-element.20.own_edge, ...), custom_call_target="tpu_custom_call" | custom-call | tf_op jit(solution)/shard_map/all_but_last/pallas_call | solution.py:519
  18.1 3.3 %collective-permute-done.6.last = f32[136,256]{1,0:T(8,128)S(1)} collective-permute-done((f32[136,256]{1,0:T(8,128)S(1)}, f32[136,256]{1,0:T(8,128)S(1)}, u32[]{:S(2)}, u32[]{:S(2)}) %collective-permute-start.6) | collective-permute-done | bytes 139296 | tf_op jit(solution)/shard_map/ppermute | solution.py:440
  21.4 0.8 %add_last.1 = f32[2,32,512]{2,1,0:T(8,128)} custom-call(f32[2,32,512]{2,1,0:T(8,128)S(1)} %copy-done, f32[2,32,512]{2,1,0:T(8,128)S(1)} %all_but_last.1.base, f32[136,256]{1,0:T(8,128)S(1)} %collective-permute-done.6.last), custom_call_target="tpu_custom_call" | custom-call | tf_op jit(solution)/shard_map/add_last/pallas_call | solution.py:528
  (3 shorter events, 0.1 us)
Async XLA Ops:
  0.0 4.1 %copy-start = (f32[2,32,512]{2,1,0:T(8,128)S(1)}, f32[2,32,512]{2,1,0:T(8,128)}, u32[]{:S(2)}) copy-start(f32[2,32,512]{2,1,0:T(8,128)} %velocity.9) | copy-start | bytes 393220
  0.0 4.1 %copy-start.2 = (f32[2,32,512]{2,1,0:T(8,128)S(1)}, f32[2,32,512]{2,1,0:T(8,128)}, u32[]{:S(2)}) copy-start(f32[2,32,512]{2,1,0:T(8,128)} %state.5) | copy-start | bytes 393220
  0.0 4.1 %copy-start.1 = (f32[2,32,512]{2,1,0:T(8,128)S(1)}, f32[2,32,512]{2,1,0:T(8,128)}, u32[]{:S(2)}) copy-start(f32[2,32,512]{2,1,0:T(8,128)} %source.3) | copy-start | bytes 393220
  0.0 4.1 %copy-start.3 = (f32[32,512]{1,0:T(8,128)S(1)}, f32[32,512]{1,0:T(8,128)}, u32[]{:S(2)}) copy-start(f32[32,512]{1,0:T(8,128)} %start.3) | copy-start | bytes 196612
  1.0 4.9 %collective-permute-start.1 = (f32[24,512]{1,0:T(8,128)S(1)}, f32[24,512]{1,0:T(8,128)S(1)}, u32[]{:S(2)}, u32[]{:S(2)}) collective-permute-start(f32[24,512]{1,0:T(8,128)S(1)} %get-tuple-element.18), channel_id=1, source_target_pairs={{0,3},{1,2},{2,1},{3,0},{4,7},{5,6},{6,5},{7,4},{8,11},{9,10},{10,... | collective-permute-start | bytes 147464 | tf_op jit(solution)/shard_map/ppermute | solution.py:420
  3.5 2.5 %collective-permute-start = (f32[16,512]{1,0:T(8,128)S(1)}, f32[16,512]{1,0:T(8,128)S(1)}, u32[]{:S(2)}, u32[]{:S(2)}) collective-permute-start(f32[16,512]{1,0:T(8,128)S(1)} %get-tuple-element.17), channel_id=1, source_target_pairs={{0,1},{1,0},{2,3},{3,2},{4,5},{5,4},{6,7},{7,6},{8,9},{9,8},{10,11... | collective-permute-start | bytes 98312 | tf_op jit(solution)/shard_map/ppermute | solution.py:420
  4.3 5.0 %collective-permute-start.2 = (f32[64,512]{1,0:T(8,128)S(1)}, f32[64,512]{1,0:T(8,128)S(1)}, u32[]{:S(2)}, u32[]{:S(2)}) collective-permute-start(f32[64,512]{1,0:T(8,128)S(1)} %get-tuple-element.19.main.rest_0_.refs_0_), channel_id=1, source_target_pairs={{0,4},{1,9},{2,6},{3,11},{4,0},{5,13},{6,2},{7,15},{8,12},{9,1},{1... | collective-permute-start | bytes 393224 | tf_op jit(solution)/shard_map/ppermute | solution.py:440
  6.1 5.0 %collective-permute-start.4 = (f32[8,512]{1,0:T(8,128)S(1)}, f32[8,512]{1,0:T(8,128)S(1)}, u32[]{:S(2)}, u32[]{:S(2)}) collective-permute-start(f32[8,512]{1,0:T(8,128)S(1)} %get-tuple-element.22.first.rest_3_.refs_2_), channel_id=1, source_target_pairs={{0,4},{1,9},{2,6},{3,11},{4,0},{5,13},{6,2},{7,15},{8,12},{9,1},{1... | collective-permute-start | bytes 49160 | tf_op jit(solution)/shard_map/ppermute | solution.py:440
  9.4 5.9 %collective-permute-start.3 = (f32[64,512]{1,0:T(8,128)S(1)}, f32[64,512]{1,0:T(8,128)S(1)}, u32[]{:S(2)}, u32[]{:S(2)}) collective-permute-start(f32[64,512]{1,0:T(8,128)S(1)} %add.3), channel_id=1, source_target_pairs={{0,8},{1,17},{2,10},{3,19},{4,12},{5,21},{6,14},{7,23},{8,0},{9,25... | collective-permute-start | bytes 393224 | tf_op jit(solution)/shard_map/ppermute | solution.py:440
  11.0 4.2 %collective-permute-start.5 = (f32[8,512]{1,0:T(8,128)S(1)}, f32[8,512]{1,0:T(8,128)S(1)}, u32[]{:S(2)}, u32[]{:S(2)}) collective-permute-start(f32[8,512]{1,0:T(8,128)S(1)} %add_edges.1), channel_id=1, source_target_pairs={{0,8},{1,17},{2,10},{3,19},{4,12},{5,21},{6,14},{7,23},{8,0},{9,25... | collective-permute-start | bytes 49160 | tf_op jit(solution)/shard_map/ppermute | solution.py:440
  15.3 6.0 %collective-permute-start.6 = (f32[136,256]{1,0:T(8,128)S(1)}, f32[136,256]{1,0:T(8,128)S(1)}, u32[]{:S(2)}, u32[]{:S(2)}) collective-permute-start(f32[136,256]{1,0:T(8,128)S(1)} %join_edges.1), channel_id=1, source_target_pairs={{0,16},{1,5},{2,18},{3,7},{4,20},{5,1},{6,22},{7,3},{8,24},{9,13},... | collective-permute-start | bytes 417800 | tf_op jit(solution)/shard_map/ppermute | solution.py:440

commit v11 on v10

--- a/solution.py
+++ b/solution.py
@@ -60,15 +60,17 @@
             from_ref = a.at[here, :] if a is start else a.at[:, here, :]
             copies.append(pltpu.make_async_copy(from_ref, b.at[end], sems.at[len(copies)]))
             copies[-1].start()
-    for copy in copies:
-        copy.wait()
     steps, _, columns = state.shape
     place, tiles = slots_of(steps)
+    kinds = ("state", "source", "velocity", "start")
+    pending = {kind: copies[2 * i : 2 * i + 2] for i, kind in enumerate(kinds)}
     odd = lax.axis_index("rows") % 2 == 1
     sub = lax.broadcasted_iota(jnp.int32, (tile, columns), 0)
 
     def item(name, end):
         kind, j = name
+        for copy in pending.pop(kind, []):
+            copy.wait()
         if kind == "start":
             return start_v[end]
         return {"state": state_v, "source": source_v, "velocity": velocity_v}[kind][end, j]
@@ -156,8 +158,7 @@
     total[rows : 2 * rows, :] = carry_z
 
 
-def edge_kernel(tm_count, state, velocity, inside, across, main, total, own_edge, main_out):
-    main_out[...] = main[...]
+def edge_kernel(tm_count, state, velocity, inside, across, total, own_edge):
     steps, time_total, gain, rate = dims_of(state.shape[0], tm_count)
     rows, columns = state.shape[1:]
     place, _ = slots_of(steps)
@@ -373,7 +374,7 @@
 
 
 def band_of(rows):
-    return 2 * tile if rows % (2 * tile) == 0 else rows
+    return tile if rows % tile == 0 else rows
 
 
 def final_kernel(tm_count, velocity, base, last, out, done, sems):
@@ -472,19 +473,18 @@
         name="own_carry",
     )(state, source, start, velocity)
     mains = [main, exchanged(main, 0)]
-    edge, own_edge, main = pl.pallas_call(
+    edge, own_edge = pl.pallas_call(
         functools.partial(edge_kernel, tm_count),
         out_shape=[
             pltpu.VMEM((tile, columns), f32),
             pltpu.VMEM((steps, tile, columns), f32),
-            pltpu.VMEM((2 * rows, columns), f32),
         ],
-        in_specs=[in_vmem] * 5,
-        out_specs=[in_vmem] * 3,
+        in_specs=[in_vmem] * 4,
+        out_specs=[in_vmem] * 2,
         compiler_params=params,
         cost_estimate=late,
         name="edge_carry",
-    )(state, velocity, inside, across, main)
+    )(state, velocity, inside, across)
     edges = [edge, exchanged(edge, 0)]
     for level in range(1, bits - 1):
         main = main + mains[-1]

time: 22.3 us -> 22.3 us (level)
  no operation moved by 1% of the time
where the time goes in v11:
time: 22.3 us; the launch traced here: 22.2 us
  starting transfers between devices  12 us (54%)
  waiting for transfers between devices  7.6 us (34%)
  Pallas kernels  2.45 us (11%)
    ppermute x5, starting transfers between devices, exchanged(): return lax.ppermute(value, ('tm', 'rows'), pairs)  8.91 us
    ppermute x5, waiting for transfers between devices, exchanged(): return lax.ppermute(value, ('tm', 'rows'), pairs)  7.59 us
    ppermute x2, starting transfers between devices, swapped(): lax.ppermute(value, axis, [(i, partner(i)) for i in range(lax.axis_size(a...  3.13 us
    pallas_call x1, Pallas kernels, on_device(): pl.pallas_call(pack_kernel, out_shape=[pack, pltpu.VMEM(((slots_of(steps)...  0.98 us
    pallas_call x1, Pallas kernels, on_device(): pl.pallas_call(functools.partial(final_kernel, tm_count), out_shape=jax.S...  0.82 us
  transfers between devices with their start and end apart: 7, of which 3 were waited for; matrix products, arithmetic and copies ran while one was open for 0% of the time, Pallas kernels for 3%

profile of v11, /device:TPU:0, one launch (start us, length us, event | category | flops | bytes accessed | tf_op | source)
XLA Modules:
  0.0 22.2 jit_solution(7975376210699136363)
XLA Ops:
  0.0 0.0 copy-start
  0.0 0.0 copy-start.2
  0.0 0.0 copy-start.1
  0.0 0.0 copy-start.3
  0.0 1.0 %pack_edge_rows.1 = (f32[16,512]{1,0:T(8,128)S(1)}, f32[24,512]{1,0:T(8,128)S(1)}) custom-call(f32[2,32,512]{2,1,0:T(8,128)} %state.5, f32[2,32,512]{2,1,0:T(8,128)} %source.3, f32[32,512]{1,0:T(8,128)} %start.3, f32[2,32,512]{2,1,0:T(8,128)} %velocity.9), custom_call_target="tpu_custom_call" | custom-call | tf_op jit(solution)/shard_map/pack_edge_rows/pallas_call | solution.py:444
  1.0 2.5 %collective-permute-start.1 = (f32[24,512]{1,0:T(8,128)S(1)}, f32[24,512]{1,0:T(8,128)S(1)}, u32[]{:S(2)}, u32[]{:S(2)}) collective-permute-start(f32[24,512]{1,0:T(8,128)S(1)} %get-tuple-element.17), channel_id=1, source_target_pairs={{0,3},{1,2},{2,1},{3,0},{4,7},{5,6},{6,5},{7,4},{8,11},{9,10},{10,... | collective-permute-start | bytes 147464 | tf_op jit(solution)/shard_map/ppermute | solution.py:421
  3.4 0.7 %collective-permute-start = (f32[16,512]{1,0:T(8,128)S(1)}, f32[16,512]{1,0:T(8,128)S(1)}, u32[]{:S(2)}, u32[]{:S(2)}) collective-permute-start(f32[16,512]{1,0:T(8,128)S(1)} %get-tuple-element.16), channel_id=1, source_target_pairs={{0,1},{1,0},{2,3},{3,2},{4,5},{5,4},{6,7},{7,6},{8,9},{9,8},{10,11... | collective-permute-start | bytes 98312 | tf_op jit(solution)/shard_map/ppermute | solution.py:421
  4.1 0.0 copy-done
  4.1 0.0 copy-done.2
  4.1 0.0 copy-done.1
  4.1 0.0 copy-done.3
  4.1 0.2 own_carry.1
  4.3 1.6 %collective-permute-start.2 = (f32[64,512]{1,0:T(8,128)S(1)}, f32[64,512]{1,0:T(8,128)S(1)}, u32[]{:S(2)}, u32[]{:S(2)}) collective-permute-start(f32[64,512]{1,0:T(8,128)S(1)} %get-tuple-element.19.rest_0_.refs_0_), channel_id=1, source_target_pairs={{0,4},{1,9},{2,6},{3,11},{4,0},{5,13},{6,2},{7,15},{8,12},{9,1},{1... | collective-permute-start | bytes 393224 | tf_op jit(solution)/shard_map/ppermute | solution.py:441
  5.9 0.0 collective-permute-done.inside
  5.9 0.0 collective-permute-done.1.across
  5.9 0.1 edge_carry.1
  6.0 2.2 %collective-permute-start.4 = (f32[8,512]{1,0:T(8,128)S(1)}, f32[8,512]{1,0:T(8,128)S(1)}, u32[]{:S(2)}, u32[]{:S(2)}) collective-permute-start(f32[8,512]{1,0:T(8,128)S(1)} %get-tuple-element.20.first.rest_3_.refs_2_), channel_id=1, source_target_pairs={{0,4},{1,9},{2,6},{3,11},{4,0},{5,13},{6,2},{7,15},{8,12},{9,1},{1... | collective-permute-start | bytes 49160 | tf_op jit(solution)/shard_map/ppermute | solution.py:441
  8.2 1.1 %collective-permute-done.2.rest_1_.refs_1_ = f32[64,512]{1,0:T(8,128)S(1)} collective-permute-done((f32[64,512]{1,0:T(8,128)S(1)}, f32[64,512]{1,0:T(8,128)S(1)}, u32[]{:S(2)}, u32[]{:S(2)}) %collective-permute-start.2) | collective-permute-done | bytes 131104 | tf_op jit(solution)/shard_map/ppermute | solution.py:441
  9.4 1.6 %collective-permute-start.3 = (f32[64,512]{1,0:T(8,128)S(1)}, f32[64,512]{1,0:T(8,128)S(1)}, u32[]{:S(2)}, u32[]{:S(2)}) collective-permute-start(f32[64,512]{1,0:T(8,128)S(1)} %add.3), channel_id=1, source_target_pairs={{0,8},{1,17},{2,10},{3,19},{4,12},{5,21},{6,14},{7,23},{8,0},{9,25... | collective-permute-start | bytes 393224 | tf_op jit(solution)/shard_map/ppermute | solution.py:441
  11.0 0.0 collective-permute-done.4.second.rest_4_.refs_3_
  11.0 1.0 %collective-permute-start.5 = (f32[8,512]{1,0:T(8,128)S(1)}, f32[8,512]{1,0:T(8,128)S(1)}, u32[]{:S(2)}, u32[]{:S(2)}) collective-permute-start(f32[8,512]{1,0:T(8,128)S(1)} %add_edges.1), channel_id=1, source_target_pairs={{0,8},{1,17},{2,10},{3,19},{4,12},{5,21},{6,14},{7,23},{8,0},{9,25... | collective-permute-start | bytes 49160 | tf_op jit(solution)/shard_map/ppermute | solution.py:441
  12.0 0.1 gather_groups.1
  12.1 3.2 %collective-permute-done.5.rest_5_.edge_partner = f32[8,512]{1,0:T(8,128)S(1)} collective-permute-done((f32[8,512]{1,0:T(8,128)S(1)}, f32[8,512]{1,0:T(8,128)S(1)}, u32[]{:S(2)}, u32[]{:S(2)}) %collective-permute-start.5) | collective-permute-done | bytes 16416 | tf_op jit(solution)/shard_map/ppermute | solution.py:441
  15.3 0.0 collective-permute-done.3.rest_2_.main_partner
  15.3 2.5 %collective-permute-start.6 = (f32[136,256]{1,0:T(8,128)S(1)}, f32[136,256]{1,0:T(8,128)S(1)}, u32[]{:S(2)}, u32[]{:S(2)}) collective-permute-start(f32[136,256]{1,0:T(8,128)S(1)} %join_edges.1), channel_id=1, source_target_pairs={{0,16},{1,5},{2,18},{3,7},{4,20},{5,1},{6,22},{7,3},{8,24},{9,13},... | collective-permute-start | bytes 417800 | tf_op jit(solution)/shard_map/ppermute | solution.py:441
  17.9 0.2 %all_but_last.1.base = f32[2,32,512]{2,1,0:T(8,128)S(1)} custom-call(f32[2,32,512]{2,1,0:T(8,128)S(1)} %copy-done, f32[2,32,512]{2,1,0:T(8,128)S(1)} %get-tuple-element.14.own_y, f32[2,32,512]{2,1,0:T(8,128)S(1)} %get-tuple-element.15.own_z, f32[2,8,512]{2,1,0:T(8,128)S(1)} %get-tuple-element.18.own_edge, f32[64,512]{1,0:T(8,128)S(1)} %get-tuple-element.19.rest_0_.refs_0_, ...), custom_call_target="tpu_custom_call" | custom-call | tf_op jit(solution)/shard_map/all_but_last/pallas_call | solution.py:519
  18.1 3.3 %collective-permute-done.6.last = f32[136,256]{1,0:T(8,128)S(1)} collective-permute-done((f32[136,256]{1,0:T(8,128)S(1)}, f32[136,256]{1,0:T(8,128)S(1)}, u32[]{:S(2)}, u32[]{:S(2)}) %collective-permute-start.6) | collective-permute-done | bytes 139296 | tf_op jit(solution)/shard_map/ppermute | solution.py:441
  21.4 0.8 %add_last.1 = f32[2,32,512]{2,1,0:T(8,128)} custom-call(f32[2,32,512]{2,1,0:T(8,128)S(1)} %copy-done, f32[2,32,512]{2,1,0:T(8,128)S(1)} %all_but_last.1.base, f32[136,256]{1,0:T(8,128)S(1)} %collective-permute-done.6.last), custom_call_target="tpu_custom_call" | custom-call | tf_op jit(solution)/shard_map/add_last/pallas_call | solution.py:528
  (3 shorter events, 0.1 us)
Async XLA Ops:
  0.0 4.1 %copy-start = (f32[2,32,512]{2,1,0:T(8,128)S(1)}, f32[2,32,512]{2,1,0:T(8,128)}, u32[]{:S(2)}) copy-start(f32[2,32,512]{2,1,0:T(8,128)} %velocity.9) | copy-start | bytes 393220
  0.0 4.1 %copy-start.2 = (f32[2,32,512]{2,1,0:T(8,128)S(1)}, f32[2,32,512]{2,1,0:T(8,128)}, u32[]{:S(2)}) copy-start(f32[2,32,512]{2,1,0:T(8,128)} %state.5) | copy-start | bytes 393220
  0.0 4.1 %copy-start.1 = (f32[2,32,512]{2,1,0:T(8,128)S(1)}, f32[2,32,512]{2,1,0:T(8,128)}, u32[]{:S(2)}) copy-start(f32[2,32,512]{2,1,0:T(8,128)} %source.3) | copy-start | bytes 393220
  0.0 4.1 %copy-start.3 = (f32[32,512]{1,0:T(8,128)S(1)}, f32[32,512]{1,0:T(8,128)}, u32[]{:S(2)}) copy-start(f32[32,512]{1,0:T(8,128)} %start.3) | copy-start | bytes 196612
  1.0 4.9 %collective-permute-start.1 = (f32[24,512]{1,0:T(8,128)S(1)}, f32[24,512]{1,0:T(8,128)S(1)}, u32[]{:S(2)}, u32[]{:S(2)}) collective-permute-start(f32[24,512]{1,0:T(8,128)S(1)} %get-tuple-element.17), channel_id=1, source_target_pairs={{0,3},{1,2},{2,1},{3,0},{4,7},{5,6},{6,5},{7,4},{8,11},{9,10},{10,... | collective-permute-start | bytes 147464 | tf_op jit(solution)/shard_map/ppermute | solution.py:421
  3.4 2.5 %collective-permute-start = (f32[16,512]{1,0:T(8,128)S(1)}, f32[16,512]{1,0:T(8,128)S(1)}, u32[]{:S(2)}, u32[]{:S(2)}) collective-permute-start(f32[16,512]{1,0:T(8,128)S(1)} %get-tuple-element.16), channel_id=1, source_target_pairs={{0,1},{1,0},{2,3},{3,2},{4,5},{5,4},{6,7},{7,6},{8,9},{9,8},{10,11... | collective-permute-start | bytes 98312 | tf_op jit(solution)/shard_map/ppermute | solution.py:421
  4.3 5.0 %collective-permute-start.2 = (f32[64,512]{1,0:T(8,128)S(1)}, f32[64,512]{1,0:T(8,128)S(1)}, u32[]{:S(2)}, u32[]{:S(2)}) collective-permute-start(f32[64,512]{1,0:T(8,128)S(1)} %get-tuple-element.19.rest_0_.refs_0_), channel_id=1, source_target_pairs={{0,4},{1,9},{2,6},{3,11},{4,0},{5,13},{6,2},{7,15},{8,12},{9,1},{1... | collective-permute-start | bytes 393224 | tf_op jit(solution)/shard_map/ppermute | solution.py:441
  6.0 5.0 %collective-permute-start.4 = (f32[8,512]{1,0:T(8,128)S(1)}, f32[8,512]{1,0:T(8,128)S(1)}, u32[]{:S(2)}, u32[]{:S(2)}) collective-permute-start(f32[8,512]{1,0:T(8,128)S(1)} %get-tuple-element.20.first.rest_3_.refs_2_), channel_id=1, source_target_pairs={{0,4},{1,9},{2,6},{3,11},{4,0},{5,13},{6,2},{7,15},{8,12},{9,1},{1... | collective-permute-start | bytes 49160 | tf_op jit(solution)/shard_map/ppermute | solution.py:441
  9.4 5.9 %collective-permute-start.3 = (f32[64,512]{1,0:T(8,128)S(1)}, f32[64,512]{1,0:T(8,128)S(1)}, u32[]{:S(2)}, u32[]{:S(2)}) collective-permute-start(f32[64,512]{1,0:T(8,128)S(1)} %add.3), channel_id=1, source_target_pairs={{0,8},{1,17},{2,10},{3,19},{4,12},{5,21},{6,14},{7,23},{8,0},{9,25... | collective-permute-start | bytes 393224 | tf_op jit(solution)/shard_map/ppermute | solution.py:441
  11.0 4.2 %collective-permute-start.5 = (f32[8,512]{1,0:T(8,128)S(1)}, f32[8,512]{1,0:T(8,128)S(1)}, u32[]{:S(2)}, u32[]{:S(2)}) collective-permute-start(f32[8,512]{1,0:T(8,128)S(1)} %add_edges.1), channel_id=1, source_target_pairs={{0,8},{1,17},{2,10},{3,19},{4,12},{5,21},{6,14},{7,23},{8,0},{9,25... | collective-permute-start | bytes 49160 | tf_op jit(solution)/shard_map/ppermute | solution.py:441
  15.3 6.0 %collective-permute-start.6 = (f32[136,256]{1,0:T(8,128)S(1)}, f32[136,256]{1,0:T(8,128)S(1)}, u32[]{:S(2)}, u32[]{:S(2)}) collective-permute-start(f32[136,256]{1,0:T(8,128)S(1)} %join_edges.1), channel_id=1, source_target_pairs={{0,16},{1,5},{2,18},{3,7},{4,20},{5,1},{6,22},{7,3},{8,24},{9,13},... | collective-permute-start | bytes 417800 | tf_op jit(solution)/shard_map/ppermute | solution.py:441

commit v12 on v11

--- a/solution.py
+++ b/solution.py
@@ -138,24 +138,28 @@
 def carry_kernel(tm_count, state, source, start, velocity, total, own_y, own_z):
     steps, time_total, gain, rate = dims_of(state.shape[0], tm_count)
     rows, columns = state.shape[1:]
-    row = lax.broadcasted_iota(jnp.int32, (rows, columns), 0)
-    y = z = None
-    for j in range(steps):
-        here = state[j]
-        above = jnp.where(row == 0, 0.0, pltpu.roll(here, 1, 0))
-        below = jnp.where(row == rows - 1, 0.0, pltpu.roll(here, rows - 1, 0))
-        left, right = sides(here)
-        beside_all = above + below + left + right
-        advect = (velocity[0] + here) * (right - left) + (velocity[1] + here) * (below - above)
-        forced = source[j] + diffusion * beside_all - 0.5 * advect
-        y = gain * forced if y is None else rate * y + gain * forced
-        z = gain * (y - here) if z is None else rate * z + gain * (y - here)
-        own_y[j] = y
-        own_z[j] = z
-    jumped = start[...] - wrap_weight * here
-    carry_y, carry_z = carried(tm_count, steps, time_total, gain, rate, y, z, jumped)
-    total[0:rows, :] = carry_y
-    total[rows : 2 * rows, :] = carry_z
+    sub = lax.broadcasted_iota(jnp.int32, (tile, columns), 0)
+    for at in range(0, rows, tile):
+        band = pl.ds(at, tile)
+        y = z = None
+        for j in range(steps):
+            here = state[j, band, :]
+            before = state[j, pl.ds(at - 1, 1), :] if at else 0.0
+            after = state[j, pl.ds(at + tile, 1), :] if at + tile < rows else 0.0
+            above = jnp.where(sub == 0, before, pltpu.roll(here, 1, 0))
+            below = jnp.where(sub == tile - 1, after, pltpu.roll(here, tile - 1, 0))
+            left, right = sides(here)
+            beside_all = above + below + left + right
+            advect = (velocity[0, band, :] + here) * (right - left) + (velocity[1, band, :] + here) * (below - above)
+            forced = source[j, band, :] + diffusion * beside_all - 0.5 * advect
+            y = gain * forced if y is None else rate * y + gain * forced
+            z = gain * (y - here) if z is None else rate * z + gain * (y - here)
+            own_y[j, band, :] = y
+            own_z[j, band, :] = z
+        jumped = start[band, :] - wrap_weight * here
+        carry_y, carry_z = carried(tm_count, steps, time_total, gain, rate, y, z, jumped)
+        total[band, :] = carry_y
+        total[pl.ds(rows + at, tile), :] = carry_z
 
 
 def edge_kernel(tm_count, state, velocity, inside, across, total, own_edge):

time: 22.3 us -> 22.3 us (level)
  no operation moved by 1% of the time
where the time goes in v12:
time: 22.3 us; the launch traced here: 22.2 us
  starting transfers between devices  12.1 us (54%)
  waiting for transfers between devices  7.59 us (34%)
  Pallas kernels  2.44 us (11%)
    ppermute x5, starting transfers between devices, exchanged(): return lax.ppermute(value, ('tm', 'rows'), pairs)  8.93 us
    ppermute x5, waiting for transfers between devices, exchanged(): return lax.ppermute(value, ('tm', 'rows'), pairs)  7.58 us
    ppermute x2, starting transfers between devices, swapped(): lax.ppermute(value, axis, [(i, partner(i)) for i in range(lax.axis_size(a...  3.13 us
    pallas_call x1, Pallas kernels, on_device(): pl.pallas_call(pack_kernel, out_shape=[pack, pltpu.VMEM(((slots_of(steps)...  0.98 us
    pallas_call x1, Pallas kernels, on_device(): pl.pallas_call(functools.partial(final_kernel, tm_count), out_shape=jax.S...  0.82 us
  transfers between devices with their start and end apart: 7, of which 3 were waited for; matrix products, arithmetic and copies ran while one was open for 0% of the time, Pallas kernels for 3%

profile of v12, /device:TPU:0, one launch (start us, length us, event | category | flops | bytes accessed | tf_op | source)
XLA Modules:
  0.0 22.2 jit_solution(15331273385355770625)
XLA Ops:
  0.0 0.0 copy-start
  0.0 0.0 copy-start.2
  0.0 0.0 copy-start.1
  0.0 0.0 copy-start.3
  0.0 1.0 %pack_edge_rows.1 = (f32[16,512]{1,0:T(8,128)S(1)}, f32[24,512]{1,0:T(8,128)S(1)}) custom-call(f32[2,32,512]{2,1,0:T(8,128)} %state.5, f32[2,32,512]{2,1,0:T(8,128)} %source.3, f32[32,512]{1,0:T(8,128)} %start.3, f32[2,32,512]{2,1,0:T(8,128)} %velocity.9), custom_call_target="tpu_custom_call" | custom-call | tf_op jit(solution)/shard_map/pack_edge_rows/pallas_call | solution.py:448
  1.0 2.5 %collective-permute-start.1 = (f32[24,512]{1,0:T(8,128)S(1)}, f32[24,512]{1,0:T(8,128)S(1)}, u32[]{:S(2)}, u32[]{:S(2)}) collective-permute-start(f32[24,512]{1,0:T(8,128)S(1)} %get-tuple-element.17), channel_id=1, source_target_pairs={{0,3},{1,2},{2,1},{3,0},{4,7},{5,6},{6,5},{7,4},{8,11},{9,10},{10,... | collective-permute-start | bytes 147464 | tf_op jit(solution)/shard_map/ppermute | solution.py:425
  3.4 0.7 %collective-permute-start = (f32[16,512]{1,0:T(8,128)S(1)}, f32[16,512]{1,0:T(8,128)S(1)}, u32[]{:S(2)}, u32[]{:S(2)}) collective-permute-start(f32[16,512]{1,0:T(8,128)S(1)} %get-tuple-element.16), channel_id=1, source_target_pairs={{0,1},{1,0},{2,3},{3,2},{4,5},{5,4},{6,7},{7,6},{8,9},{9,8},{10,11... | collective-permute-start | bytes 98312 | tf_op jit(solution)/shard_map/ppermute | solution.py:425
  4.1 0.0 copy-done
  4.1 0.0 copy-done.2
  4.1 0.0 copy-done.1
  4.1 0.0 copy-done.3
  4.1 0.2 own_carry.1
  4.3 1.6 %collective-permute-start.2 = (f32[64,512]{1,0:T(8,128)S(1)}, f32[64,512]{1,0:T(8,128)S(1)}, u32[]{:S(2)}, u32[]{:S(2)}) collective-permute-start(f32[64,512]{1,0:T(8,128)S(1)} %get-tuple-element.19.rest_0_.refs_0_), channel_id=1, source_target_pairs={{0,4},{1,9},{2,6},{3,11},{4,0},{5,13},{6,2},{7,15},{8,12},{9,1},{1... | collective-permute-start | bytes 393224 | tf_op jit(solution)/shard_map/ppermute | solution.py:445
  5.9 0.0 collective-permute-done.inside
  5.9 0.0 collective-permute-done.1.across
  5.9 0.1 edge_carry.1
  6.0 2.2 %collective-permute-start.4 = (f32[8,512]{1,0:T(8,128)S(1)}, f32[8,512]{1,0:T(8,128)S(1)}, u32[]{:S(2)}, u32[]{:S(2)}) collective-permute-start(f32[8,512]{1,0:T(8,128)S(1)} %get-tuple-element.20.first.rest_3_.refs_2_), channel_id=1, source_target_pairs={{0,4},{1,9},{2,6},{3,11},{4,0},{5,13},{6,2},{7,15},{8,12},{9,1},{1... | collective-permute-start | bytes 49160 | tf_op jit(solution)/shard_map/ppermute | solution.py:445
  8.2 1.1 %collective-permute-done.2.rest_1_.refs_1_ = f32[64,512]{1,0:T(8,128)S(1)} collective-permute-done((f32[64,512]{1,0:T(8,128)S(1)}, f32[64,512]{1,0:T(8,128)S(1)}, u32[]{:S(2)}, u32[]{:S(2)}) %collective-permute-start.2) | collective-permute-done | bytes 131104 | tf_op jit(solution)/shard_map/ppermute | solution.py:445
  9.4 1.6 %collective-permute-start.3 = (f32[64,512]{1,0:T(8,128)S(1)}, f32[64,512]{1,0:T(8,128)S(1)}, u32[]{:S(2)}, u32[]{:S(2)}) collective-permute-start(f32[64,512]{1,0:T(8,128)S(1)} %add.3), channel_id=1, source_target_pairs={{0,8},{1,17},{2,10},{3,19},{4,12},{5,21},{6,14},{7,23},{8,0},{9,25... | collective-permute-start | bytes 393224 | tf_op jit(solution)/shard_map/ppermute | solution.py:445
  11.0 0.0 collective-permute-done.4.second.rest_4_.refs_3_
  11.0 1.0 %collective-permute-start.5 = (f32[8,512]{1,0:T(8,128)S(1)}, f32[8,512]{1,0:T(8,128)S(1)}, u32[]{:S(2)}, u32[]{:S(2)}) collective-permute-start(f32[8,512]{1,0:T(8,128)S(1)} %add_edges.1), channel_id=1, source_target_pairs={{0,8},{1,17},{2,10},{3,19},{4,12},{5,21},{6,14},{7,23},{8,0},{9,25... | collective-permute-start | bytes 49160 | tf_op jit(solution)/shard_map/ppermute | solution.py:445
  12.0 0.1 gather_groups.1
  12.1 3.2 %collective-permute-done.5.rest_5_.edge_partner = f32[8,512]{1,0:T(8,128)S(1)} collective-permute-done((f32[8,512]{1,0:T(8,128)S(1)}, f32[8,512]{1,0:T(8,128)S(1)}, u32[]{:S(2)}, u32[]{:S(2)}) %collective-permute-start.5) | collective-permute-done | bytes 16416 | tf_op jit(solution)/shard_map/ppermute | solution.py:445
  15.3 0.0 collective-permute-done.3.rest_2_.main_partner
  15.3 2.5 %collective-permute-start.6 = (f32[136,256]{1,0:T(8,128)S(1)}, f32[136,256]{1,0:T(8,128)S(1)}, u32[]{:S(2)}, u32[]{:S(2)}) collective-permute-start(f32[136,256]{1,0:T(8,128)S(1)} %join_edges.1), channel_id=1, source_target_pairs={{0,16},{1,5},{2,18},{3,7},{4,20},{5,1},{6,22},{7,3},{8,24},{9,13},... | collective-permute-start | bytes 417800 | tf_op jit(solution)/shard_map/ppermute | solution.py:445
  17.9 0.2 %all_but_last.1.base = f32[2,32,512]{2,1,0:T(8,128)S(1)} custom-call(f32[2,32,512]{2,1,0:T(8,128)S(1)} %copy-done, f32[2,32,512]{2,1,0:T(8,128)S(1)} %get-tuple-element.14.own_y, f32[2,32,512]{2,1,0:T(8,128)S(1)} %get-tuple-element.15.own_z, f32[2,8,512]{2,1,0:T(8,128)S(1)} %get-tuple-element.18.own_edge, f32[64,512]{1,0:T(8,128)S(1)} %get-tuple-element.19.rest_0_.refs_0_, ...), custom_call_target="tpu_custom_call" | custom-call | tf_op jit(solution)/shard_map/all_but_last/pallas_call | solution.py:523
  18.1 3.3 %collective-permute-done.6.last = f32[136,256]{1,0:T(8,128)S(1)} collective-permute-done((f32[136,256]{1,0:T(8,128)S(1)}, f32[136,256]{1,0:T(8,128)S(1)}, u32[]{:S(2)}, u32[]{:S(2)}) %collective-permute-start.6) | collective-permute-done | bytes 139296 | tf_op jit(solution)/shard_map/ppermute | solution.py:445
  21.3 0.8 %add_last.1 = f32[2,32,512]{2,1,0:T(8,128)} custom-call(f32[2,32,512]{2,1,0:T(8,128)S(1)} %copy-done, f32[2,32,512]{2,1,0:T(8,128)S(1)} %all_but_last.1.base, f32[136,256]{1,0:T(8,128)S(1)} %collective-permute-done.6.last), custom_call_target="tpu_custom_call" | custom-call | tf_op jit(solution)/shard_map/add_last/pallas_call | solution.py:532
  (3 shorter events, 0.1 us)
Async XLA Ops:
  0.0 4.1 %copy-start = (f32[2,32,512]{2,1,0:T(8,128)S(1)}, f32[2,32,512]{2,1,0:T(8,128)}, u32[]{:S(2)}) copy-start(f32[2,32,512]{2,1,0:T(8,128)} %velocity.9) | copy-start | bytes 393220
  0.0 4.1 %copy-start.2 = (f32[2,32,512]{2,1,0:T(8,128)S(1)}, f32[2,32,512]{2,1,0:T(8,128)}, u32[]{:S(2)}) copy-start(f32[2,32,512]{2,1,0:T(8,128)} %state.5) | copy-start | bytes 393220
  0.0 4.1 %copy-start.1 = (f32[2,32,512]{2,1,0:T(8,128)S(1)}, f32[2,32,512]{2,1,0:T(8,128)}, u32[]{:S(2)}) copy-start(f32[2,32,512]{2,1,0:T(8,128)} %source.3) | copy-start | bytes 393220
  0.0 4.1 %copy-start.3 = (f32[32,512]{1,0:T(8,128)S(1)}, f32[32,512]{1,0:T(8,128)}, u32[]{:S(2)}) copy-start(f32[32,512]{1,0:T(8,128)} %start.3) | copy-start | bytes 196612
  1.0 4.9 %collective-permute-start.1 = (f32[24,512]{1,0:T(8,128)S(1)}, f32[24,512]{1,0:T(8,128)S(1)}, u32[]{:S(2)}, u32[]{:S(2)}) collective-permute-start(f32[24,512]{1,0:T(8,128)S(1)} %get-tuple-element.17), channel_id=1, source_target_pairs={{0,3},{1,2},{2,1},{3,0},{4,7},{5,6},{6,5},{7,4},{8,11},{9,10},{10,... | collective-permute-start | bytes 147464 | tf_op jit(solution)/shard_map/ppermute | solution.py:425
  3.4 2.5 %collective-permute-start = (f32[16,512]{1,0:T(8,128)S(1)}, f32[16,512]{1,0:T(8,128)S(1)}, u32[]{:S(2)}, u32[]{:S(2)}) collective-permute-start(f32[16,512]{1,0:T(8,128)S(1)} %get-tuple-element.16), channel_id=1, source_target_pairs={{0,1},{1,0},{2,3},{3,2},{4,5},{5,4},{6,7},{7,6},{8,9},{9,8},{10,11... | collective-permute-start | bytes 98312 | tf_op jit(solution)/shard_map/ppermute | solution.py:425
  4.3 5.0 %collective-permute-start.2 = (f32[64,512]{1,0:T(8,128)S(1)}, f32[64,512]{1,0:T(8,128)S(1)}, u32[]{:S(2)}, u32[]{:S(2)}) collective-permute-start(f32[64,512]{1,0:T(8,128)S(1)} %get-tuple-element.19.rest_0_.refs_0_), channel_id=1, source_target_pairs={{0,4},{1,9},{2,6},{3,11},{4,0},{5,13},{6,2},{7,15},{8,12},{9,1},{1... | collective-permute-start | bytes 393224 | tf_op jit(solution)/shard_map/ppermute | solution.py:445
  6.0 5.0 %collective-permute-start.4 = (f32[8,512]{1,0:T(8,128)S(1)}, f32[8,512]{1,0:T(8,128)S(1)}, u32[]{:S(2)}, u32[]{:S(2)}) collective-permute-start(f32[8,512]{1,0:T(8,128)S(1)} %get-tuple-element.20.first.rest_3_.refs_2_), channel_id=1, source_target_pairs={{0,4},{1,9},{2,6},{3,11},{4,0},{5,13},{6,2},{7,15},{8,12},{9,1},{1... | collective-permute-start | bytes 49160 | tf_op jit(solution)/shard_map/ppermute | solution.py:445
  9.4 5.9 %collective-permute-start.3 = (f32[64,512]{1,0:T(8,128)S(1)}, f32[64,512]{1,0:T(8,128)S(1)}, u32[]{:S(2)}, u32[]{:S(2)}) collective-permute-start(f32[64,512]{1,0:T(8,128)S(1)} %add.3), channel_id=1, source_target_pairs={{0,8},{1,17},{2,10},{3,19},{4,12},{5,21},{6,14},{7,23},{8,0},{9,25... | collective-permute-start | bytes 393224 | tf_op jit(solution)/shard_map/ppermute | solution.py:445
  11.0 4.2 %collective-permute-start.5 = (f32[8,512]{1,0:T(8,128)S(1)}, f32[8,512]{1,0:T(8,128)S(1)}, u32[]{:S(2)}, u32[]{:S(2)}) collective-permute-start(f32[8,512]{1,0:T(8,128)S(1)} %add_edges.1), channel_id=1, source_target_pairs={{0,8},{1,17},{2,10},{3,19},{4,12},{5,21},{6,14},{7,23},{8,0},{9,25... | collective-permute-start | bytes 49160 | tf_op jit(solution)/shard_map/ppermute | solution.py:445
  15.3 6.0 %collective-permute-start.6 = (f32[136,256]{1,0:T(8,128)S(1)}, f32[136,256]{1,0:T(8,128)S(1)}, u32[]{:S(2)}, u32[]{:S(2)}) collective-permute-start(f32[136,256]{1,0:T(8,128)S(1)} %join_edges.1), channel_id=1, source_target_pairs={{0,16},{1,5},{2,18},{3,7},{4,20},{5,1},{6,22},{7,3},{8,24},{9,13},... | collective-permute-start | bytes 417800 | tf_op jit(solution)/shard_map/ppermute | solution.py:445

commit v13 on v12

--- a/solution.py
+++ b/solution.py
@@ -378,7 +378,7 @@
 
 
 def band_of(rows):
-    return tile if rows % tile == 0 else rows
+    return 2 * tile if rows % (2 * tile) == 0 else rows
 
 
 def final_kernel(tm_count, velocity, base, last, out, done, sems):

time: 22.3 us -> 22.3 us (level)
  no operation moved by 1% of the time
where the time goes in v13:
time: 22.3 us; the launch traced here: 22.2 us
  starting transfers between devices  12.1 us (54%)
  waiting for transfers between devices  7.59 us (34%)
  Pallas kernels  2.43 us (11%)
    ppermute x5, starting transfers between devices, exchanged(): return lax.ppermute(value, ('tm', 'rows'), pairs)  8.93 us
    ppermute x5, waiting for transfers between devices, exchanged(): return lax.ppermute(value, ('tm', 'rows'), pairs)  7.58 us
    ppermute x2, starting transfers between devices, swapped(): lax.ppermute(value, axis, [(i, partner(i)) for i in range(lax.axis_size(a...  3.13 us
    pallas_call x1, Pallas kernels, on_device(): pl.pallas_call(pack_kernel, out_shape=[pack, pltpu.VMEM(((slots_of(steps)...  0.98 us
    pallas_call x1, Pallas kernels, on_device(): pl.pallas_call(functools.partial(final_kernel, tm_count), out_shape=jax.S...  0.82 us
  transfers between devices with their start and end apart: 7, of which 3 were waited for; matrix products, arithmetic and copies ran while one was open for 0% of the time, Pallas kernels for 3%

profile of v13, /device:TPU:0, one launch (start us, length us, event | category | flops | bytes accessed | tf_op | source)
XLA Modules:
  0.0 22.2 jit_solution(5742868466349143551)
XLA Ops:
  0.0 0.0 copy-start
  0.0 0.0 copy-start.2
  0.0 0.0 copy-start.1
  0.0 0.0 copy-start.3
  0.0 1.0 %pack_edge_rows.1 = (f32[16,512]{1,0:T(8,128)S(1)}, f32[24,512]{1,0:T(8,128)S(1)}) custom-call(f32[2,32,512]{2,1,0:T(8,128)} %state.5, f32[2,32,512]{2,1,0:T(8,128)} %source.3, f32[32,512]{1,0:T(8,128)} %start.3, f32[2,32,512]{2,1,0:T(8,128)} %velocity.9), custom_call_target="tpu_custom_call" | custom-call | tf_op jit(solution)/shard_map/pack_edge_rows/pallas_call | solution.py:448
  1.0 2.5 %collective-permute-start.1 = (f32[24,512]{1,0:T(8,128)S(1)}, f32[24,512]{1,0:T(8,128)S(1)}, u32[]{:S(2)}, u32[]{:S(2)}) collective-permute-start(f32[24,512]{1,0:T(8,128)S(1)} %get-tuple-element.17), channel_id=1, source_target_pairs={{0,3},{1,2},{2,1},{3,0},{4,7},{5,6},{6,5},{7,4},{8,11},{9,10},{10,... | collective-permute-start | bytes 147464 | tf_op jit(solution)/shard_map/ppermute | solution.py:425
  3.4 0.7 %collective-permute-start = (f32[16,512]{1,0:T(8,128)S(1)}, f32[16,512]{1,0:T(8,128)S(1)}, u32[]{:S(2)}, u32[]{:S(2)}) collective-permute-start(f32[16,512]{1,0:T(8,128)S(1)} %get-tuple-element.16), channel_id=1, source_target_pairs={{0,1},{1,0},{2,3},{3,2},{4,5},{5,4},{6,7},{7,6},{8,9},{9,8},{10,11... | collective-permute-start | bytes 98312 | tf_op jit(solution)/shard_map/ppermute | solution.py:425
  4.1 0.0 copy-done
  4.1 0.0 copy-done.2
  4.1 0.0 copy-done.1
  4.1 0.0 copy-done.3
  4.1 0.2 own_carry.1
  4.3 1.6 %collective-permute-start.2 = (f32[64,512]{1,0:T(8,128)S(1)}, f32[64,512]{1,0:T(8,128)S(1)}, u32[]{:S(2)}, u32[]{:S(2)}) collective-permute-start(f32[64,512]{1,0:T(8,128)S(1)} %get-tuple-element.19.rest_0_.refs_0_), channel_id=1, source_target_pairs={{0,4},{1,9},{2,6},{3,11},{4,0},{5,13},{6,2},{7,15},{8,12},{9,1},{1... | collective-permute-start | bytes 393224 | tf_op jit(solution)/shard_map/ppermute | solution.py:445
  5.9 0.0 collective-permute-done.inside
  5.9 0.0 collective-permute-done.1.across
  5.9 0.1 edge_carry.1
  6.0 2.2 %collective-permute-start.4 = (f32[8,512]{1,0:T(8,128)S(1)}, f32[8,512]{1,0:T(8,128)S(1)}, u32[]{:S(2)}, u32[]{:S(2)}) collective-permute-start(f32[8,512]{1,0:T(8,128)S(1)} %get-tuple-element.20.first.rest_3_.refs_2_), channel_id=1, source_target_pairs={{0,4},{1,9},{2,6},{3,11},{4,0},{5,13},{6,2},{7,15},{8,12},{9,1},{1... | collective-permute-start | bytes 49160 | tf_op jit(solution)/shard_map/ppermute | solution.py:445
  8.2 1.1 %collective-permute-done.2.rest_1_.refs_1_ = f32[64,512]{1,0:T(8,128)S(1)} collective-permute-done((f32[64,512]{1,0:T(8,128)S(1)}, f32[64,512]{1,0:T(8,128)S(1)}, u32[]{:S(2)}, u32[]{:S(2)}) %collective-permute-start.2) | collective-permute-done | bytes 131104 | tf_op jit(solution)/shard_map/ppermute | solution.py:445
  9.4 1.6 %collective-permute-start.3 = (f32[64,512]{1,0:T(8,128)S(1)}, f32[64,512]{1,0:T(8,128)S(1)}, u32[]{:S(2)}, u32[]{:S(2)}) collective-permute-start(f32[64,512]{1,0:T(8,128)S(1)} %add.3), channel_id=1, source_target_pairs={{0,8},{1,17},{2,10},{3,19},{4,12},{5,21},{6,14},{7,23},{8,0},{9,25... | collective-permute-start | bytes 393224 | tf_op jit(solution)/shard_map/ppermute | solution.py:445
  11.0 0.0 collective-permute-done.4.second.rest_4_.refs_3_
  11.0 1.0 %collective-permute-start.5 = (f32[8,512]{1,0:T(8,128)S(1)}, f32[8,512]{1,0:T(8,128)S(1)}, u32[]{:S(2)}, u32[]{:S(2)}) collective-permute-start(f32[8,512]{1,0:T(8,128)S(1)} %add_edges.1), channel_id=1, source_target_pairs={{0,8},{1,17},{2,10},{3,19},{4,12},{5,21},{6,14},{7,23},{8,0},{9,25... | collective-permute-start | bytes 49160 | tf_op jit(solution)/shard_map/ppermute | solution.py:445
  12.0 0.1 gather_groups.1
  12.1 3.2 %collective-permute-done.5.rest_5_.edge_partner = f32[8,512]{1,0:T(8,128)S(1)} collective-permute-done((f32[8,512]{1,0:T(8,128)S(1)}, f32[8,512]{1,0:T(8,128)S(1)}, u32[]{:S(2)}, u32[]{:S(2)}) %collective-permute-start.5) | collective-permute-done | bytes 16416 | tf_op jit(solution)/shard_map/ppermute | solution.py:445
  15.3 0.0 collective-permute-done.3.rest_2_.main_partner
  15.3 2.5 %collective-permute-start.6 = (f32[136,256]{1,0:T(8,128)S(1)}, f32[136,256]{1,0:T(8,128)S(1)}, u32[]{:S(2)}, u32[]{:S(2)}) collective-permute-start(f32[136,256]{1,0:T(8,128)S(1)} %join_edges.1), channel_id=1, source_target_pairs={{0,16},{1,5},{2,18},{3,7},{4,20},{5,1},{6,22},{7,3},{8,24},{9,13},... | collective-permute-start | bytes 417800 | tf_op jit(solution)/shard_map/ppermute | solution.py:445
  17.9 0.2 %all_but_last.1.base = f32[2,32,512]{2,1,0:T(8,128)S(1)} custom-call(f32[2,32,512]{2,1,0:T(8,128)S(1)} %copy-done, f32[2,32,512]{2,1,0:T(8,128)S(1)} %get-tuple-element.14.own_y, f32[2,32,512]{2,1,0:T(8,128)S(1)} %get-tuple-element.15.own_z, f32[2,8,512]{2,1,0:T(8,128)S(1)} %get-tuple-element.18.own_edge, f32[64,512]{1,0:T(8,128)S(1)} %get-tuple-element.19.rest_0_.refs_0_, ...), custom_call_target="tpu_custom_call" | custom-call | tf_op jit(solution)/shard_map/all_but_last/pallas_call | solution.py:523
  18.1 3.3 %collective-permute-done.6.last = f32[136,256]{1,0:T(8,128)S(1)} collective-permute-done((f32[136,256]{1,0:T(8,128)S(1)}, f32[136,256]{1,0:T(8,128)S(1)}, u32[]{:S(2)}, u32[]{:S(2)}) %collective-permute-start.6) | collective-permute-done | bytes 139296 | tf_op jit(solution)/shard_map/ppermute | solution.py:445
  21.3 0.8 %add_last.1 = f32[2,32,512]{2,1,0:T(8,128)} custom-call(f32[2,32,512]{2,1,0:T(8,128)S(1)} %copy-done, f32[2,32,512]{2,1,0:T(8,128)S(1)} %all_but_last.1.base, f32[136,256]{1,0:T(8,128)S(1)} %collective-permute-done.6.last), custom_call_target="tpu_custom_call" | custom-call | tf_op jit(solution)/shard_map/add_last/pallas_call | solution.py:532
  (3 shorter events, 0.1 us)
Async XLA Ops:
  0.0 4.1 %copy-start = (f32[2,32,512]{2,1,0:T(8,128)S(1)}, f32[2,32,512]{2,1,0:T(8,128)}, u32[]{:S(2)}) copy-start(f32[2,32,512]{2,1,0:T(8,128)} %velocity.9) | copy-start | bytes 393220
  0.0 4.1 %copy-start.2 = (f32[2,32,512]{2,1,0:T(8,128)S(1)}, f32[2,32,512]{2,1,0:T(8,128)}, u32[]{:S(2)}) copy-start(f32[2,32,512]{2,1,0:T(8,128)} %state.5) | copy-start | bytes 393220
  0.0 4.1 %copy-start.1 = (f32[2,32,512]{2,1,0:T(8,128)S(1)}, f32[2,32,512]{2,1,0:T(8,128)}, u32[]{:S(2)}) copy-start(f32[2,32,512]{2,1,0:T(8,128)} %source.3) | copy-start | bytes 393220
  0.0 4.1 %copy-start.3 = (f32[32,512]{1,0:T(8,128)S(1)}, f32[32,512]{1,0:T(8,128)}, u32[]{:S(2)}) copy-start(f32[32,512]{1,0:T(8,128)} %start.3) | copy-start | bytes 196612
  1.0 4.9 %collective-permute-start.1 = (f32[24,512]{1,0:T(8,128)S(1)}, f32[24,512]{1,0:T(8,128)S(1)}, u32[]{:S(2)}, u32[]{:S(2)}) collective-permute-start(f32[24,512]{1,0:T(8,128)S(1)} %get-tuple-element.17), channel_id=1, source_target_pairs={{0,3},{1,2},{2,1},{3,0},{4,7},{5,6},{6,5},{7,4},{8,11},{9,10},{10,... | collective-permute-start | bytes 147464 | tf_op jit(solution)/shard_map/ppermute | solution.py:425
  3.4 2.5 %collective-permute-start = (f32[16,512]{1,0:T(8,128)S(1)}, f32[16,512]{1,0:T(8,128)S(1)}, u32[]{:S(2)}, u32[]{:S(2)}) collective-permute-start(f32[16,512]{1,0:T(8,128)S(1)} %get-tuple-element.16), channel_id=1, source_target_pairs={{0,1},{1,0},{2,3},{3,2},{4,5},{5,4},{6,7},{7,6},{8,9},{9,8},{10,11... | collective-permute-start | bytes 98312 | tf_op jit(solution)/shard_map/ppermute | solution.py:425
  4.3 5.0 %collective-permute-start.2 = (f32[64,512]{1,0:T(8,128)S(1)}, f32[64,512]{1,0:T(8,128)S(1)}, u32[]{:S(2)}, u32[]{:S(2)}) collective-permute-start(f32[64,512]{1,0:T(8,128)S(1)} %get-tuple-element.19.rest_0_.refs_0_), channel_id=1, source_target_pairs={{0,4},{1,9},{2,6},{3,11},{4,0},{5,13},{6,2},{7,15},{8,12},{9,1},{1... | collective-permute-start | bytes 393224 | tf_op jit(solution)/shard_map/ppermute | solution.py:445
  6.0 5.0 %collective-permute-start.4 = (f32[8,512]{1,0:T(8,128)S(1)}, f32[8,512]{1,0:T(8,128)S(1)}, u32[]{:S(2)}, u32[]{:S(2)}) collective-permute-start(f32[8,512]{1,0:T(8,128)S(1)} %get-tuple-element.20.first.rest_3_.refs_2_), channel_id=1, source_target_pairs={{0,4},{1,9},{2,6},{3,11},{4,0},{5,13},{6,2},{7,15},{8,12},{9,1},{1... | collective-permute-start | bytes 49160 | tf_op jit(solution)/shard_map/ppermute | solution.py:445
  9.4 5.9 %collective-permute-start.3 = (f32[64,512]{1,0:T(8,128)S(1)}, f32[64,512]{1,0:T(8,128)S(1)}, u32[]{:S(2)}, u32[]{:S(2)}) collective-permute-start(f32[64,512]{1,0:T(8,128)S(1)} %add.3), channel_id=1, source_target_pairs={{0,8},{1,17},{2,10},{3,19},{4,12},{5,21},{6,14},{7,23},{8,0},{9,25... | collective-permute-start | bytes 393224 | tf_op jit(solution)/shard_map/ppermute | solution.py:445
  11.0 4.2 %collective-permute-start.5 = (f32[8,512]{1,0:T(8,128)S(1)}, f32[8,512]{1,0:T(8,128)S(1)}, u32[]{:S(2)}, u32[]{:S(2)}) collective-permute-start(f32[8,512]{1,0:T(8,128)S(1)} %add_edges.1), channel_id=1, source_target_pairs={{0,8},{1,17},{2,10},{3,19},{4,12},{5,21},{6,14},{7,23},{8,0},{9,25... | collective-permute-start | bytes 49160 | tf_op jit(solution)/shard_map/ppermute | solution.py:445
  15.3 6.0 %collective-permute-start.6 = (f32[136,256]{1,0:T(8,128)S(1)}, f32[136,256]{1,0:T(8,128)S(1)}, u32[]{:S(2)}, u32[]{:S(2)}) collective-permute-start(f32[136,256]{1,0:T(8,128)S(1)} %join_edges.1), channel_id=1, source_target_pairs={{0,16},{1,5},{2,18},{3,7},{4,20},{5,1},{6,22},{7,3},{8,24},{9,13},... | collective-permute-start | bytes 417800 | tf_op jit(solution)/shard_map/ppermute | solution.py:445
